TPU v7x, 32 devices: a whole 2x2x4 slice. The times are simulated.
32 devices in a mesh: wide: 16 (over z, x, core), narrow: 2 (over y).
Axes of the slice: x: 2, y: 2, z: 4, core: 2. Of those that a mesh axis runs over, the one named last changes fastest.
Arguments:
- patches: bfloat16 [16, 256, 1280], P('wide', None, 'narrow'), may hold values from -8 to 8
- grid: int32 [16, 2], P('wide'), may hold values from 2 to 16, as said below
- vit_gain: float32 [1280], replicated, may hold values from 0.25 to 1.75
- vit_qkv: bfloat16 [1280, 3840], P('wide', 'narrow'), may hold values from -1 to 1
- vit_out: bfloat16 [1280, 1280], P('narrow', 'wide'), may hold values from -0.625 to 0.625
- merge_weight: bfloat16 [4, 1280, 1280], P(None, 'narrow', 'wide'), may hold values from -0.078125 to 0.078125
- text_embeds: bfloat16 [2560, 1280], P('wide', 'narrow'), may hold values from -8 to 8
- prompt_pos: int32 [16, 64], replicated, may hold values from -1 to 2559, as said below
- dec_gain: float32 [1280], replicated, may hold values from 0.25 to 1.75
- dec_qkv: bfloat16 [1280, 3840], P('wide', 'narrow'), may hold values from -1 to 1
- dec_out: bfloat16 [1280, 1280], P('narrow', 'wide'), may hold values from -1.25 to 1.25
Outputs:
- decoded: bfloat16 [2560, 1280], P('wide', 'narrow')
Inputs may be any that keep to these rules, and one draw needn't show every extreme that they name: `prompt_pos`: grid entries are even; a merged slot (r, c) is live when 2r < grid rows and 2c < grid columns; live slots carry distinct positions, one image's live slots being consecutive in row-major order, and padded slots carry -1. `grid`: patch rows and columns of an image are even.
All inputs are finite; a program needn't handle non-finite values.
Results may differ from a plain program's by a relative error of at most 0.02.
Values may be sent and summed in bfloat16 or wider, within the bound.
No kernel may reach another device: no remote copies, remote signals or barrier semaphores. Data moves between devices by JAX's collectives and lax.ppermute only.
A program may use at most 64 MiB of HBM per device.

v0:
```python
import jax
import jax.numpy as jnp
from jax import lax
from jax.sharding import PartitionSpec as P

D = 1280
HEAD = 80
PATCH_SIDE = 16


eps_norm = 1e-06


def layer_norm(values, gain):
    center = values - jnp.mean(values, axis=-1, keepdims=True)
    spread = jnp.mean(center * center, axis=-1, keepdims=True)
    return center * lax.rsqrt(spread + eps_norm) * gain


def rms_norm(values, gain):
    return values * lax.rsqrt(jnp.mean(values * values, axis=-1, keepdims=True) + eps_norm) * gain


def add_rows(left, piece):
    return jnp.dot(left, piece, preferred_element_type=jnp.float32)


def image_attention(query, keys, values, keep):
    scores = jnp.einsum(
        "iqhd,ikhd->ihqk", query, keys, preferred_element_type=jnp.float32
    ) * HEAD ** (-0.5)
    scores = jnp.where(keep[:, None, None, :], scores, -jnp.inf)
    weights = jnp.exp(scores - jnp.max(scores, axis=-1, keepdims=True))
    total = jnp.sum(weights, axis=-1)
    mixed = jnp.einsum(
        "ihqk,ikhd->iqhd", weights.astype(jnp.bfloat16), values, preferred_element_type=jnp.float32
    )
    return (mixed / jnp.transpose(total, (0, 2, 1))[..., None]).astype(jnp.bfloat16)


def attend(state, query, query_pos, keys, values, key_pos):
    best, total, summed = state
    scores = jnp.einsum("qhd,khd->hqk", query, keys, preferred_element_type=jnp.float32) * HEAD ** (
        -0.5
    )
    allowed = key_pos[None, :] <= query_pos[:, None]
    scores = jnp.where(allowed[None], scores, -jnp.inf)
    new_best = jnp.maximum(best, jnp.max(scores, axis=-1))
    shift = jnp.where(jnp.isfinite(new_best), new_best, 0.0)
    weights = jnp.exp(scores - shift[..., None])
    fade = jnp.exp(best - shift)
    total = total * fade + jnp.sum(weights, axis=-1)
    update = jnp.einsum(
        "hqk,khd->hqd", weights.astype(jnp.bfloat16), values, preferred_element_type=jnp.float32
    )
    summed = summed * fade[..., None] + update
    return (new_best, total, summed)


def fresh_state(heads, count):
    return (
        jnp.full((heads, count), -jnp.inf, jnp.float32),
        jnp.zeros((heads, count), jnp.float32),
        jnp.zeros((heads, count, HEAD), jnp.float32),
    )


def finish(state):
    best, total, summed = state
    return summed / total[..., None]


def shards(
    patches,
    grid,
    vit_gain,
    vit_qkv,
    vit_out,
    merge_weight,
    text_embeds,
    prompt_pos,
    dec_gain,
    dec_qkv,
    dec_out,
):
    images, slots, part_width = patches.shape
    side = PATCH_SIDE
    half_side = side // 2
    rows_vit = images * slots
    local_heads = vit_qkv.shape[1] // (3 * HEAD)
    whole = lax.all_gather(patches, "narrow", axis=2, tiled=True)
    normed = (
        layer_norm(whole.astype(jnp.float32), vit_gain).astype(jnp.bfloat16).reshape(rows_vit, D)
    )
    projected = add_rows(normed, lax.all_gather(vit_qkv, "wide", axis=0, tiled=True))
    projected = projected.astype(jnp.bfloat16).reshape(images, slots, local_heads, 3, HEAD)
    slot_ids = jnp.arange(slots, dtype=jnp.int32)
    keep = ((slot_ids // side)[None, :] < grid[:, 0:1]) & (
        (slot_ids % side)[None, :] < grid[:, 1:2]
    )
    attended = image_attention(
        projected[:, :, :, 0], projected[:, :, :, 1], projected[:, :, :, 2], keep
    )
    attended = attended.reshape(rows_vit, local_heads * HEAD)
    vit_partial = jnp.dot(
        attended,
        lax.all_gather(vit_out, "wide", axis=1, tiled=True),
        preferred_element_type=jnp.float32,
    )
    vit_branch = lax.psum_scatter(vit_partial, "narrow", scatter_dimension=1, tiled=True)
    after = (patches.reshape(rows_vit, part_width).astype(jnp.float32) + vit_branch).astype(
        jnp.bfloat16
    )
    grouped = after.reshape(images, half_side, 2, half_side, 2, part_width).transpose(
        0, 1, 3, 2, 4, 5
    )
    grouped = grouped.reshape(images * half_side * half_side, 4 * part_width)
    piece = lax.all_gather(merge_weight, "wide", axis=2, tiled=True)
    flat_piece = piece.reshape(4 * part_width, piece.shape[2])
    merge_partial = jnp.dot(grouped, flat_piece, preferred_element_type=jnp.float32)
    merged = lax.psum_scatter(merge_partial, "narrow", scatter_dimension=1, tiled=True).astype(
        jnp.bfloat16
    )
    text_rows = text_embeds.shape[0]
    half_rows = text_rows // 2
    wide_index = lax.axis_index("wide")
    offsets = jnp.arange(text_rows, dtype=jnp.int32)
    mine = wide_index * text_rows + offsets
    flat_pos = prompt_pos.reshape(-1)
    select = (mine[:, None] == flat_pos[None, :]).astype(jnp.bfloat16)
    routed = jnp.dot(
        select,
        lax.all_gather(merged, "wide", axis=0, tiled=True),
        preferred_element_type=jnp.float32,
    )
    is_image = jnp.any(mine[:, None] == flat_pos[None, :], axis=1)
    dec_in = jnp.where(is_image[:, None], routed.astype(jnp.bfloat16), text_embeds)
    dec_whole = lax.all_gather(dec_in, "narrow", axis=1, tiled=True)
    dec_normed = rms_norm(dec_whole.astype(jnp.float32), dec_gain).astype(jnp.bfloat16)
    dec_proj = add_rows(dec_normed, lax.all_gather(dec_qkv, "wide", axis=0, tiled=True))
    dec_proj = dec_proj.astype(jnp.bfloat16).reshape(text_rows, local_heads, 3, HEAD)
    queries = dec_proj[:, :, 0]
    keys = dec_proj[:, :, 1].reshape(text_rows, local_heads * HEAD)
    values = dec_proj[:, :, 2].reshape(text_rows, local_heads * HEAD)
    low_pos = mine[:half_rows]
    high_pos = mine[half_rows:]
    low_query = queries[:half_rows]
    high_query = queries[half_rows:]
    start_state = (
        fresh_state(local_heads, half_rows),
        fresh_state(local_heads, text_rows - half_rows),
    )
    key_piece = lax.all_gather(keys, "wide", axis=0, tiled=True)
    value_piece = lax.all_gather(values, "wide", axis=0, tiled=True)
    count = key_piece.shape[0]
    span_rows = count
    while span_rows > 2048 and span_rows % 2 == 0:
        span_rows = span_rows // 2
    key_heads = key_piece.reshape(count, local_heads, HEAD)
    value_heads = value_piece.reshape(count, local_heads, HEAD)

    def one_span(index, carry):
        begin = (index * span_rows).astype(jnp.int32)
        key_span = lax.dynamic_slice_in_dim(key_heads, begin, span_rows)
        value_span = lax.dynamic_slice_in_dim(value_heads, begin, span_rows)
        key_pos = begin + jnp.arange(span_rows, dtype=jnp.int32)
        earliest = jnp.min(key_pos)
        first = lax.cond(
            earliest <= jnp.max(low_pos),
            lambda inner: attend(inner, low_query, low_pos, key_span, value_span, key_pos),
            lambda inner: inner,
            carry[0],
        )
        second = lax.cond(
            earliest <= jnp.max(high_pos),
            lambda inner: attend(inner, high_query, high_pos, key_span, value_span, key_pos),
            lambda inner: inner,
            carry[1],
        )
        return (first, second)

    final = lax.fori_loop(0, count // span_rows, one_span, start_state)
    heads_out = jnp.concatenate([finish(final[0]), finish(final[1])], axis=1)
    heads_out = (
        heads_out.transpose(1, 0, 2).reshape(text_rows, local_heads * HEAD).astype(jnp.bfloat16)
    )
    dec_partial = jnp.dot(
        heads_out,
        lax.all_gather(dec_out, "wide", axis=1, tiled=True),
        preferred_element_type=jnp.float32,
    )
    dec_branch = lax.psum_scatter(
        dec_partial.astype(jnp.bfloat16), "narrow", scatter_dimension=1, tiled=True
    ).astype(jnp.float32)
    result = (dec_in.astype(jnp.float32) + dec_branch).astype(jnp.bfloat16)
    return result


def solution(mesh):
    placed = (
        P("wide", None, "narrow"),
        P("wide", None),
        P(),
        P("wide", "narrow"),
        P("narrow", "wide"),
        P(None, "narrow", "wide"),
        P("wide", "narrow"),
        P(),
        P(),
        P("wide", "narrow"),
        P("narrow", "wide"),
    )
    return jax.shard_map(
        shards, mesh=mesh, in_specs=placed, out_specs=P("wide", "narrow"), check_vma=False
    )
```

profile of v0, /device:TPU:0, one launch (start us, length us, event | category | flops | bytes accessed | tf_op | source)
XLA Modules:
  0.0 488.0 jit_solution(9700221632106813805)
XLA Ops:
  10.7 11.6 %all_gather.30 = bf16[1,256,1280]{2,1,0:T(8,128)(2,1)S(1)} all-gather(bf16[1,256,640]{2,1,0:T(8,128)(2,1)} %param.17), channel_id=1, replica_groups=mesh['wide'=16,'narrow'=2] {'narrow'}, dimensions={2}, use_global_device_ids=true | all-gather | bytes 983040 | tf_op jit(solution)/shard_map/all_gather | solution.py:91
  22.8 43.9 %all-gather.9.cloned.1.call-done = bf16[1280,1920]{1,0:T(8,128)(2,1)} async-done(((bf16[80,1920]{1,0:T(8,128)(2,1)}), bf16[1280,1920]{1,0:T(8,128)(2,1)}) %all-gather.9.cloned.1.call-update) | async-done | bytes 4915216 | tf_op jit(solution)/shard_map/all_gather | solution.py:95
  66.7 4.0 convolution_convert_fusion
  73.2 34.3 %all-gather.11.cloned.1.call-done = bf16[640,1280]{0,1:T(8,128)(2,1)} async-done(((bf16[640,80]{0,1:T(8,128)(2,1)}), bf16[640,1280]{0,1:T(8,128)(2,1)}) %all-gather.11.cloned.1.call-update) | async-done | bytes 1638416 | tf_op jit(solution)/shard_map/all_gather | solution.py:107
  107.4 3.3 fusion.63
  111.8 21.2 %reduce-scatter.6.cloned.1.call-done = f32[256,640]{1,0:T(8,128)} async-done(((f32[256,1280]{1,0:T(8,128)}), f32[256,640]{1,0:T(8,128)}) %reduce-scatter.6.cloned.1.call-update) | async-done | bytes 655376 | tf_op jit(solution)/shard_map/reduce_scatter | solution.py:110
  134.7 64.1 %all-gather.13.cloned.1.call-done = bf16[4,640,1280]{1,0,2:T(4,128)(2,1)} async-done(((bf16[4,640,80]{1,0,2:T(4,128)(2,1)}), bf16[4,640,1280]{1,0,2:T(4,128)(2,1)}) %all-gather.13.cloned.1.call-update) | async-done | bytes 6553616 | tf_op jit(solution)/shard_map/all_gather | solution.py:118
  198.8 12.4 %copy.73 = bf16[4,640,1280]{2,1,0:T(8,128)(2,1)} copy(bf16[4,640,1280]{1,0,2:T(4,128)(2,1)} %all-gather.13.cloned.1.call-done) | data formatting | bytes 13107200 | tf_op jit(solution)/shard_map/all_gather | solution.py:118
  211.3 4.9 fusion.64
  216.2 11.1 %reduce-scatter.8.cloned.1.call-done = f32[64,640]{1,0:T(8,128)} async-done(((f32[64,1280]{1,0:T(8,128)}), f32[64,640]{1,0:T(8,128)}) %reduce-scatter.8.cloned.1.call-update) | async-done | bytes 163856 | tf_op jit(solution)/shard_map/reduce_scatter | solution.py:121
  230.0 38.3 %all-gather.15.cloned.1.call-done = bf16[1024,640]{1,0:T(8,128)(2,1)} async-done(((bf16[64,640]{1,0:T(8,128)(2,1)}), bf16[1024,640]{1,0:T(8,128)(2,1)}) %all-gather.15.cloned.1.call-update) | async-done | bytes 1310736 | tf_op jit(solution)/shard_map/all_gather | solution.py:133
  270.7 7.9 %all_gather.35 = bf16[160,1280]{1,0:T(8,128)(2,1)S(1)} all-gather(bf16[160,640]{1,0:T(8,128)(2,1)S(1)} %fusion.27), channel_id=1, replica_groups=mesh['wide'=16,'narrow'=2] {'narrow'}, dimensions={1}, use_global_device_ids=true | all-gather | bytes 614400 | tf_op jit(solution)/shard_map/all_gather | solution.py:138
  278.8 44.9 %all-gather.17.cloned.1.call-done = bf16[1280,1920]{1,0:T(8,128)(2,1)} async-done(((bf16[80,1920]{1,0:T(8,128)(2,1)}), bf16[1280,1920]{1,0:T(8,128)(2,1)}) %all-gather.17.cloned.1.call-update) | async-done | bytes 4915216 | tf_op jit(solution)/shard_map/all_gather | solution.py:140
  323.7 3.5 convolution_convert_fusion.2
  332.6 41.0 %all-gather.19.cloned.1.call-done = bf16[2560,640]{1,0:T(8,128)(2,1)} async-done(((bf16[160,640]{1,0:T(8,128)(2,1)}), bf16[2560,640]{1,0:T(8,128)(2,1)}) %all-gather.19.cloned.1.call-update) | async-done | bytes 3276816 | tf_op jit(solution)/shard_map/all_gather | solution.py:153
  373.6 5.7 %copy.76 = bf16[2560,640]{0,1:T(8,128)(2,1)} copy(bf16[2560,640]{1,0:T(8,128)(2,1)} %all-gather.19.cloned.1.call-done) | data formatting | bytes 6553600 | tf_op jit(solution)/shard_map/all_gather | solution.py:153
  379.2 41.3 %all-gather.21.cloned.1.call-done = bf16[2560,640]{1,0:T(8,128)(2,1)} async-done(((bf16[160,640]{1,0:T(8,128)(2,1)}), bf16[2560,640]{1,0:T(8,128)(2,1)}) %all-gather.21.cloned.1.call-update) | async-done | bytes 3276816 | tf_op jit(solution)/shard_map/all_gather | solution.py:154
  420.5 5.7 %copy.78 = bf16[2560,640]{0,1:T(8,128)(2,1)} copy(bf16[2560,640]{1,0:T(8,128)(2,1)} %all-gather.21.cloned.1.call-done) | data formatting | bytes 6553600 | tf_op jit(solution)/shard_map/all_gather | solution.py:154
  427.7 18.5 %while.24 = (s32[]{:T(128)}, f32[8,80]{1,0:T(8,128)S(1)}, f32[8,80]{1,0:T(8,128)S(1)}, f32[8,80,80]{2,1,0:T(8,128)}, f32[8,80]{1,0:T(8,128)S(1)}, /*index=5*/f32...) while((s32[]{:T(128)}, f32[8,80]{1,0:T(8,128)S(1)}, ...), condition=%wide.region_20.21_spmd, body=%wide.region_10.20_spmd.sunk | while | flops 536176640 | bytes 37582048 | solution.py:182
  427.7 2.2 constant_dynamic-slice_fusion.3
  431.8 4.3 conditional.5
  437.5 3.4 conditional.4
  448.0 13.3 %all-gather.23.cloned.1.call-done = bf16[640,1280]{0,1:T(8,128)(2,1)} async-done(((bf16[640,80]{0,1:T(8,128)(2,1)}), bf16[640,1280]{0,1:T(8,128)(2,1)}) %all-gather.23.cloned.1.call-update) | async-done | bytes 1638416 | tf_op jit(solution)/shard_map/all_gather | solution.py:189
  464.5 15.1 %reduce-scatter.10.cloned.1.call-done = bf16[640,160]{1,0:T(8,128)(2,1)} async-done(((bf16[1280,160]{1,0:T(8,128)(2,1)}), bf16[640,160]{1,0:T(8,128)(2,1)}) %reduce-scatter.10.cloned.1.call-update) | async-done | bytes 204816
  (109 shorter events, 39.7 us)
Async XLA Ops:
  6.5 60.2 %copy-start.11 = (f32[1280]{0:T(1024)S(1)}, f32[1280]{0:T(1024)}, u32[]{:S(2)}) copy-start(f32[1280]{0:T(1024)} %param.19) | copy-start | bytes 15364
  6.5 60.2 %all-gather.9.cloned.1.call-start = ((), (), s32[]{:S(2)}) async-start(), calls=%async_computation.3 | async-start | bytes 5222400 | tf_op jit(solution)/shard_map/all_gather | solution.py:95
  7.3 100.2 %all-gather.11.cloned.1.call-start = ((), (), s32[]{:S(2)}) async-start(), calls=%async_computation.4 | async-start | bytes 1740800 | tf_op jit(solution)/shard_map/all_gather | solution.py:107
  8.0 125.0 %reduce-scatter.6.cloned.1.call-start = ((), (), s32[]{:S(2)}) async-start(), calls=%async_computation.5 | async-start | bytes 1966080 | tf_op jit(solution)/shard_map/reduce_scatter | solution.py:110
  107.4 3.4 copy-start.7
  107.4 25.6 %copy-start.4 = (bf16[1,256,640]{2,1,0:T(8,128)(2,1)S(1)}, bf16[1,256,640]{2,1,0:T(8,128)(2,1)}, u32[]{:S(2)}) copy-start(bf16[1,256,640]{2,1,0:T(8,128)(2,1)} %param.17) | copy-start | bytes 983044
  110.7 88.1 %all-gather.13.cloned.1.call-start = ((), (), s32[]{:S(2)}) async-start(), calls=%async_computation.6 | async-start | bytes 6963200 | tf_op jit(solution)/shard_map/all_gather | solution.py:118
  111.8 115.5 %reduce-scatter.8.cloned.1.call-start = ((), (), s32[]{:S(2)}) async-start(), calls=%async_computation.7 | async-start | bytes 491520 | tf_op jit(solution)/shard_map/reduce_scatter | solution.py:121
  211.2 18.4 %copy-start.9 = (s32[16,64]{1,0:T(8,128)S(1)}, s32[16,64]{1,0:T(8,128)}, u32[]{:S(2)}) copy-start(s32[16,64]{1,0:T(8,128)} %param.24) | copy-start | bytes 12292
  211.2 57.0 %copy-start.10 = (bf16[160,640]{1,0:T(8,128)(2,1)S(1)}, bf16[160,640]{1,0:T(8,128)(2,1)}, u32[]{:S(2)}) copy-start(bf16[160,640]{1,0:T(8,128)(2,1)} %param.23) | copy-start | bytes 614404
  216.1 107.6 %copy-start.8 = (f32[1280]{0:T(1024)S(1)}, f32[1280]{0:T(1024)}, u32[]{:S(2)}) copy-start(f32[1280]{0:T(1024)} %param.25) | copy-start | bytes 15364
  216.2 52.1 %all-gather.15.cloned.1.call-start = ((), (), s32[]{:S(2)}) async-start(), calls=%async_computation.8 | async-start | bytes 1392640 | tf_op jit(solution)/shard_map/all_gather | solution.py:133
  228.9 94.9 %all-gather.17.cloned.1.call-start = ((), (), s32[]{:S(2)}) async-start(), calls=%async_computation.9 | async-start | bytes 5222400 | tf_op jit(solution)/shard_map/all_gather | solution.py:140
  229.6 143.9 %all-gather.19.cloned.1.call-start = ((), (), s32[]{:S(2)}) async-start(), calls=%async_computation.10 | async-start | bytes 3481600 | tf_op jit(solution)/shard_map/all_gather | solution.py:153
  270.0 0.7 copy-start.5
  329.1 91.5 %all-gather.21.cloned.1.call-start = ((), (), s32[]{:S(2)}) async-start(), calls=%async_computation.11 | async-start | bytes 3481600 | tf_op jit(solution)/shard_map/all_gather | solution.py:154
  330.0 131.4 %all-gather.23.cloned.1.call-start = ((), (), s32[]{:S(2)}) async-start(), calls=%async_computation.12 | async-start | bytes 1740800 | tf_op jit(solution)/shard_map/all_gather | solution.py:189
  330.6 149.0 %reduce-scatter.10.cloned.1.call-start = ((), (), s32[]{:S(2)}) async-start(), calls=%async_computation.13 | async-start | bytes 983040
  433.7 1.0 copy-start.2
  435.5 0.7 copy-start.3
  438.4 1.0 copy-start
  440.2 0.7 copy-start.1
  448.0 32.7 %copy-start.6 = (bf16[160,640]{1,0:T(8,128)(2,1)S(1)}, bf16[160,640]{1,0:T(8,128)(2,1)}, u32[]{:S(2)}) copy-start(bf16[160,640]{1,0:T(8,128)(2,1)} %copy-done.5) | copy-start | bytes 614404
Sparse Core Ops, SparseCore 0:
  9.5 57.1 all-gather.8
  68.9 38.4 all-gather.10
  110.9 22.0 reduce-scatter.5
  135.4 63.3 all-gather.12
  216.3 10.9 reduce-scatter.7
  229.4 38.8 all-gather.14
  270.4 53.2 all-gather.16
  329.2 44.3 all-gather.18
  375.8 44.6 all-gather.20
  422.5 38.7 all-gather.22
  464.7 14.8 reduce-scatter.9
where the time goes:
time: 489 us; the launch traced here: 488 us
  waiting for transfers between devices  371 us (76%)
  local copies, waits for them, and re-layouts  42.1 us (9%)
  matrix products  24.8 us (5%)
  blocking collectives  19.5 us (4%)
  between operations  13.5 us (3%)
  other arithmetic  11.2 us (2%)
  loops' own time  5.3 us (1%)
    all_gather x1, waiting for transfers between devices, shards(): piece = lax.all_gather(merge_weight, 'wide', axis=2, tiled=True)  64.1 us
    all_gather x1, waiting for transfers between devices, shards(): lax.all_gather(dec_qkv, 'wide', axis=0, tiled=True)  44.9 us
    all_gather x1, waiting for transfers between devices, shards(): lax.all_gather(vit_qkv, 'wide', axis=0, tiled=True)  43.9 us
    all_gather x1, waiting for transfers between devices, shards(): value_piece = lax.all_gather(values, 'wide', axis=0, tiled=True)  41.3 us
    all_gather x1, waiting for transfers between devices, shards(): key_piece = lax.all_gather(keys, 'wide', axis=0, tiled=True)  41 us
    all_gather x1, waiting for transfers between devices, shards(): lax.all_gather(merged, 'wide', axis=0, tiled=True)  38.3 us
    all_gather x1, waiting for transfers between devices, shards(): lax.all_gather(vit_out, 'wide', axis=1, tiled=True)  34.3 us
    reduce_scatter x1, waiting for transfers between devices, shards(): lax.psum_scatter(vit_partial, 'narrow', scatter_dimension=1, tiled=True)  21.2 us
  transfers between devices with their start and end apart: 11, of which 11 were waited for; matrix products, arithmetic and copies ran while one was open for 9% of the time, Pallas kernels for 0%

commit v1 on v0

--- a/solution.py
+++ b/solution.py
@@ -1,6 +1,8 @@
 import jax
 import jax.numpy as jnp
 from jax import lax
+from jax.experimental import pallas as pl
+from jax.experimental.pallas import tpu as pltpu
 from jax.sharding import PartitionSpec as P
 
 D = 1280
@@ -70,7 +72,7 @@
     return summed / total[..., None]
 
 
-def shards(
+def shards_any(
     patches,
     grid,
     vit_gain,
@@ -196,6 +198,434 @@
     return result
 
 
+CROSS_X = [(w, w ^ 2) for w in range(16)]
+CROSS_C = [(w, w ^ 1) for w in range(16)]
+CROSS_Y = [(0, 1), (1, 0)]
+GROUPS_Z = [[b, 4 + b, 8 + b, 12 + b] for b in range(4)]
+GROUPS_B = [[4 * z + b for b in range(4)] for z in range(4)]
+FOUR = ((0, 0), (0, 1), (1, 0), (1, 1))
+VMEM = pl.BlockSpec(memory_space=pltpu.VMEM)
+SMEM = pl.BlockSpec(memory_space=pltpu.SMEM)
+F32 = jnp.float32
+BF16 = jnp.bfloat16
+GRANT = 48 * 1024 * 1024
+
+
+def over_x(value):
+    return lax.ppermute(value, "wide", CROSS_X)
+
+
+def over_c(value):
+    return lax.ppermute(value, "wide", CROSS_C)
+
+
+def over_y(value):
+    return lax.ppermute(value, "narrow", CROSS_Y)
+
+
+def share_xy(value):
+    half = value.shape[0] // 2
+    from_x = over_x(value)
+    from_y = over_y(value)
+    corner = [over_y(from_x[:half]), over_x(from_y[half:])]
+    return [[[value], [from_y]], [[from_x], corner]]
+
+
+def share_xyc(value):
+    pieces = share_xy(value)
+    found = {}
+    for ex in (0, 1):
+        for ec in (0, 1):
+            found[(ex, ec)] = [
+                [over_c(part) if ec else part for part in pieces[ex][ey]] for ey in (0, 1)
+            ]
+    return found
+
+
+def flat_parts(pieces):
+    return [part for key in FOUR for ey in (0, 1) for part in pieces[key][ey]]
+
+
+def read_parts(refs):
+    found, at = {}, 0
+    for key in FOUR:
+        found[key] = []
+        for ey in (0, 1):
+            many = 2 if (key[0] and ey) else 1
+            found[key].append(refs[at : at + many])
+            at += many
+    return found
+
+
+def whole_of(refs):
+    if len(refs) == 1:
+        return refs[0][...]
+    return jnp.concatenate([ref[...] for ref in refs], axis=0)
+
+
+def contract(left, right, left_dim, right_dim):
+    return lax.dot_general(
+        left, right, (((left_dim,), (right_dim,)), ((), ())), preferred_element_type=F32
+    )
+
+
+def encode_kernel(*refs):
+    parts = read_parts(refs[:10])
+    gain, weight, keep, out = refs[10:]
+    for slot, key in enumerate(FOUR):
+        own = whole_of(parts[key][0]).astype(F32)
+        other = whole_of(parts[key][1]).astype(F32)
+        mean = (
+            jnp.sum(own, axis=-1, keepdims=True) + jnp.sum(other, axis=-1, keepdims=True)
+        ) * (1.0 / D)
+        own = own - mean
+        other = other - mean
+        spread = (
+            jnp.sum(own * own, axis=-1, keepdims=True)
+            + jnp.sum(other * other, axis=-1, keepdims=True)
+        ) * (1.0 / D)
+        scale = lax.rsqrt(spread + eps_norm)
+        own = (own * scale * gain[:, : D // 2]).astype(BF16)
+        other = (other * scale * gain[:, D // 2 :]).astype(BF16)
+        proj = contract(own, weight[: D // 2, :], 1, 0) + contract(
+            other, weight[D // 2 :, :], 1, 0
+        )
+        proj = proj.astype(BF16)
+        live = keep[:, slot : slot + 1] > 0.0
+        for head in (0, 1):
+            base = head * 3 * HEAD
+            query = proj[:, base : base + HEAD]
+            key_rows = proj[:, base + HEAD : base + 2 * HEAD]
+            value_rows = proj[:, base + 2 * HEAD : base + 3 * HEAD]
+            scores = contract(key_rows, query, 1, 1) * HEAD ** (-0.5)
+            scores = jnp.where(live, scores, -jnp.inf)
+            weights = jnp.exp(scores - jnp.max(scores, axis=0, keepdims=True))
+            total = jnp.sum(weights, axis=0, keepdims=True)
+            mixed = contract(value_rows, weights.astype(BF16), 0, 0)
+            out[head * HEAD : (head + 1) * HEAD, slot * 256 : (slot + 1) * 256] = (
+                mixed / total
+            ).astype(BF16)
+
+
+def merge_kernel(where, *refs):
+    parts = read_parts(refs[:10])
+    residual = refs[10:14]
+    out_weight, weight, keep_out, send_out, heads, grouped, summed = refs[14:]
+    here = where[1] * 2 + where[2]
+    for code, key in enumerate(FOUR):
+        for ey in (0, 1):
+            base = ey * (D // 2) + 2 * HEAD * jnp.bitwise_xor(here, code)
+            rows = 0
+            for ref in parts[key][ey]:
+                count = ref.shape[0]
+                at = pl.ds(pl.multiple_of(base + rows, 16), count)
+                for slot in range(4):
+                    other = slot ^ code
+                    heads[at, slot * 256 : (slot + 1) * 256] = ref[
+                        :, other * 256 : (other + 1) * 256
+                    ]
+                rows += count
+    row = lax.broadcasted_iota(jnp.int32, (256, 256), 0)
+    column = lax.broadcasted_iota(jnp.int32, (256, 256), 1)
+    sub, token = row // 64, row % 64
+    source = (2 * (token // 8) + sub // 2) * 16 + 2 * (token % 8) + sub % 2
+    order = jnp.where(column == source, 1.0, 0.0).astype(BF16)
+    for slot in range(4):
+        branch = contract(heads[:, slot * 256 : (slot + 1) * 256], out_weight[...], 0, 0)
+        after = (residual[slot][...].astype(F32) + branch).astype(BF16)
+        sorted_rows = contract(order, after, 1, 0).astype(BF16)
+        for sub_patch in range(4):
+            grouped[sub_patch, slot * 64 : (slot + 1) * 64, :] = sorted_rows[
+                sub_patch * 64 : (sub_patch + 1) * 64
+            ]
+    total = contract(grouped[0], weight[0], 1, 1)
+    for sub_patch in range(1, 4):
+        total = total + contract(grouped[sub_patch], weight[sub_patch], 1, 1)
+    summed[...] = total
+    mine = where[3] * 128
+    keep_out[...] = summed[pl.ds(pl.multiple_of(mine, 128), 128), :]
+    send_out[...] = summed[pl.ds(pl.multiple_of(128 - mine, 128), 128), :]
+
+
+def place_kernel(where, *refs):
+    parts = read_parts(refs[:10])
+    gain, weight, flat_pos, text_proj, query, key_out, value_out, routed, proj = refs[10:]
+    tokens = {}
+    for sx in (0, 1):
+        blocks = []
+        for ex, ec in FOUR:
+            rows = whole_of(parts[(ex, ec)][sx ^ ex])
+            if ec:
+                rows = jnp.concatenate(
+                    [rows[64 * (at ^ 1) : 64 * (at ^ 1) + 64] for at in range(8)], axis=0
+                )
+            blocks.append(rows)
+        tokens[sx] = blocks
+        wide = [block.astype(F32) for block in blocks]
+        squares = sum(jnp.sum(block * block, axis=-1, keepdims=True) for block in wide)
+        scale = lax.rsqrt(squares * (1.0 / D) + eps_norm)
+        total = 0.0
+        for at, block in enumerate(wide):
+            normed = (block * scale * gain[at : at + 1, :]).astype(BF16)
+            total = total + contract(normed, weight[at], 1, 0)
+        proj[sx * 512 : (sx + 1) * 512, :] = total.astype(BF16)
+    positions = flat_pos[...]
+    columns = positions.shape[1]
+    block_rows = query.shape[0] // 8
+    for block in range(8):
+        first = (2 * block + where[2]) * block_rows
+        row = first + lax.broadcasted_iota(jnp.int32, (block_rows, columns), 0)
+        hit = row == positions
+        select = jnp.where(hit, 1.0, 0.0)
+        image = jnp.max(select, axis=-1, keepdims=True) > 0.0
+        moved = contract(select.astype(BF16), proj[...], 1, 0)
+        at = slice(block * block_rows, (block + 1) * block_rows)
+        rows = jnp.where(image, moved, text_proj[at, :].astype(F32)).astype(BF16)
+        query[at, :] = rows[:, :128]
+        key_out[at, :] = rows[:, 128:256]
+        value_out[at, :] = rows[:, 256:]
+    own_block = 4 * where[0] + 2 * where[1] + where[2]
+    row = own_block * block_rows + lax.broadcasted_iota(jnp.int32, (block_rows, columns), 0)
+    select = jnp.where(row == positions, 1.0, 0.0).astype(BF16)
+    for at in range(4):
+        moved = contract(select[:, :512], tokens[0][at], 1, 0) + contract(
+            select[:, 512:], tokens[1][at], 1, 0
+        )
+        routed[at] = moved.astype(BF16)
+
+
+def decode_kernel(where, query, own_key, own_value, other_key, other_value, out):
+    rows = query.shape[0] // 8
+    later = where[2] > 0
+    for block in range(8):
+        count = (block + 1) * rows
+        asked = query[block * rows : count, :]
+        own = contract(asked, own_key[:count, :], 1, 1) * HEAD ** (-0.5)
+        other = contract(asked, other_key[:count, :], 1, 1) * HEAD ** (-0.5)
+        row = lax.broadcasted_iota(jnp.int32, (rows, count), 0) + block * rows
+        column = lax.broadcasted_iota(jnp.int32, (rows, count), 1)
+        own = jnp.where(column <= row, own, -jnp.inf)
+        limit = jnp.where(later, count, block * rows)
+        other = jnp.where(column < limit, other, -jnp.inf)
+        best = jnp.maximum(
+            jnp.max(own, axis=-1, keepdims=True), jnp.max(other, axis=-1, keepdims=True)
+        )
+        own = jnp.exp(own - best)
+        other = jnp.exp(other - best)
+        total = jnp.sum(own, axis=-1, keepdims=True) + jnp.sum(other, axis=-1, keepdims=True)
+        mixed = contract(own.astype(BF16), own_value[:count, :], 1, 0) + contract(
+            other.astype(BF16), other_value[:count, :], 1, 0
+        )
+        mixed = (mixed / total).astype(BF16)
+        out[2 * block] = mixed
+        out[2 * block + 1] = mixed
+
+
+def finish_kernel(where, heads, weight, residual, out):
+    total = residual[...].astype(F32)
+    branch = 0.0
+    for at in range(16):
+        chip, y = at // 2, at % 2
+        base = jnp.bitwise_xor(where[3], y) * (D // 2) + chip * HEAD
+        rows = weight[pl.ds(pl.multiple_of(base, 16), HEAD), :]
+        branch = branch + contract(heads[at][:, :HEAD], rows, 1, 0)
+    out[...] = (total + branch).astype(BF16)
+
+
+def run(kernel, shapes, scratch, *operands, scalars=None):
+    specs = ([SMEM] if scalars is not None else []) + [VMEM] * len(operands)
+    given = ([scalars] if scalars is not None else []) + list(operands)
+    single = not isinstance(shapes, (list, tuple))
+    return pl.pallas_call(
+        kernel,
+        out_shape=shapes,
+        in_specs=specs,
+        out_specs=VMEM if single else [VMEM] * len(shapes),
+        scratch_shapes=scratch,
+        compiler_params=pltpu.CompilerParams(vmem_limit_bytes=GRANT),
+    )(*given)
+
+
+def share_out(block, z, y, w):
+    turned = block.T
+    send = [(2 * w_ + 1 - w_ // 8, 2 * w_ + w_ // 8) for w_ in range(16)]
+    both = jnp.stack([turned, lax.ppermute(turned, ("wide", "narrow"), send)])
+    far = [(2 * w_ + w_ // 8, 2 * (w_ ^ 8) + w_ // 8) for w_ in range(16)]
+    moved = lax.ppermute(both, ("wide", "narrow"), far)
+    held = jnp.where(z // 2 == y, both, moved)[None]
+    near = [(w_, w_ ^ 4) for w_ in range(16)]
+    held = jnp.concatenate([held, lax.ppermute(held, "wide", near)])
+    held = jnp.concatenate([held, over_x(held)])
+    held = jnp.concatenate([held, over_c(held)])
+    rows = []
+    for at in range(8):
+        flip = at ^ (w % 8)
+        index = 4 * (flip % 2) + 2 * ((flip // 2) % 2) + flip // 4
+        rows.append(lax.dynamic_index_in_dim(held, index, 0, keepdims=False))
+    whole = jnp.stack(rows)
+    return whole.transpose(1, 3, 0, 2).reshape(2 * block.shape[0], 8 * block.shape[1])
+
+
+def shards_fast(
+    patches,
+    grid,
+    vit_gain,
+    vit_qkv,
+    vit_out,
+    merge_weight,
+    text_embeds,
+    prompt_pos,
+    dec_gain,
+    dec_qkv,
+    dec_out,
+):
+    w = lax.axis_index("wide").astype(jnp.int32)
+    y = lax.axis_index("narrow").astype(jnp.int32)
+    z, x, c = w // 4, (w // 2) % 2, w % 2
+    where = jnp.stack([z, x, c, y])
+    half = D // 2
+    text_rows = text_embeds.shape[0]
+
+    def own_first(value):
+        return jnp.roll(value, -half * y, axis=0)
+
+    patch_parts = share_xyc(patches[0])
+    columns = vit_qkv.shape[1] // 4
+    sliced = vit_qkv.reshape(-1, 4, columns).transpose(1, 0, 2)
+    sliced = lax.all_to_all(sliced, "wide", 0, 0, axis_index_groups=GROUPS_B, tiled=True)
+    sliced = sliced.reshape(-1, columns)
+    vit_weight = lax.all_gather(sliced, "wide", axis_index_groups=GROUPS_Z, axis=0, tiled=True)
+    merge_turned = merge_weight.transpose(0, 2, 1)
+    merge_rows = lax.all_gather(
+        merge_turned, "wide", axis_index_groups=GROUPS_Z, axis=1, tiled=True
+    )
+    vit_out_rows = share_out(vit_out, z, y, w)
+    codes = jnp.arange(4, dtype=jnp.int32)
+    live = prompt_pos[4 * z + jnp.bitwise_xor(2 * x + c, codes)] >= 0
+    side = PATCH_SIDE // 2
+    live = jnp.repeat(jnp.repeat(live.reshape(4, side, side), 2, axis=1), 2, axis=2)
+    live = live.reshape(4, 4 * side * side).T.astype(F32)
+    attended = run(
+        encode_kernel,
+        jax.ShapeDtypeStruct((2 * HEAD, 4 * patches.shape[1]), BF16),
+        [],
+        *flat_parts(patch_parts),
+        own_first(vit_gain)[None],
+        own_first(vit_weight),
+        live,
+    )
+    head_parts = share_xyc(attended)
+    part = jax.ShapeDtypeStruct((128, 320), F32)
+    kept, sent = run(
+        merge_kernel,
+        [part, part],
+        [
+            pltpu.VMEM((D, 4 * patches.shape[1]), BF16),
+            pltpu.VMEM((4, 256, half), BF16),
+            pltpu.VMEM((256, 320), F32),
+        ],
+        *flat_parts(head_parts),
+        *[patch_parts[key][0][0] for key in FOUR],
+        vit_out_rows,
+        merge_rows,
+        scalars=where,
+    )
+    merged = (kept + over_y(sent)).astype(BF16)
+    around = [merged] + [
+        lax.ppermute(merged, "wide", [(w_, (w_ + 4 * k) % 16) for w_ in range(16)])
+        for k in (1, 2, 3)
+    ]
+    token_parts = share_xyc(jnp.concatenate(around))
+
+    third = dec_qkv.shape[1] // 16
+    pieces = dec_qkv.reshape(-1, 16, third).transpose(1, 0, 2)
+    pieces = lax.all_to_all(pieces, "wide", 0, 0, tiled=True).reshape(-1, third)
+    partner = over_c(pieces)
+    head_weight = jnp.where(
+        c == 0,
+        jnp.concatenate([pieces, partner], axis=1),
+        jnp.concatenate([partner, pieces], axis=1),
+    )
+    head_weight = jnp.pad(head_weight.reshape(D, 3, HEAD), ((0, 0), (0, 0), (0, 128 - HEAD)))
+    head_weight = head_weight.reshape(D, 384)
+
+    def by_partner(value):
+        split = value.reshape((4, 4, D // 16) + value.shape[1:])
+        taken = [
+            lax.dynamic_index_in_dim(split, jnp.bitwise_xor(2 * x + c, code), 1, keepdims=False)
+            for code in range(4)
+        ]
+        return jnp.stack(taken).reshape((4, D // 4) + value.shape[1:])
+
+    stacked = lax.all_gather(text_embeds, "wide", axis_index_groups=GROUPS_Z, axis=0, tiled=True)
+    text_parts = share_xy(stacked)
+    text_gain = own_first(dec_gain)
+    text_weight = own_first(head_weight)
+    text_proj = []
+    for ex in (0, 1):
+        rows = jnp.concatenate([jnp.concatenate(p, axis=0) for p in text_parts[ex]], axis=1)
+        normed = rms_norm(rows.astype(F32), text_gain).astype(BF16)
+        text_proj.append(add_rows(normed, text_weight).astype(BF16).reshape(4, text_rows, 384))
+    first = jnp.where(x == 0, text_proj[0], text_proj[1])
+    second = jnp.where(x == 0, text_proj[1], text_proj[0])
+    text_proj = jnp.stack([first, second], axis=1).reshape(8 * text_rows, 384)
+
+    sx = jnp.arange(2, dtype=jnp.int32)[:, None, None]
+    k = jnp.arange(4, dtype=jnp.int32)[None, :, None]
+    sc = jnp.arange(2, dtype=jnp.int32)[None, None, :]
+    image = 4 * ((z - k) % 4) + 2 * (sx ^ x ^ y) + (sc ^ c)
+    flat_pos = prompt_pos[image.reshape(-1)].reshape(1, -1)
+    lanes = jax.ShapeDtypeStruct((8 * text_rows, 128), BF16)
+    query, key, value, routed = run(
+        place_kernel,
+        [lanes, lanes, lanes, jax.ShapeDtypeStruct((4, text_rows, 320), BF16)],
+        [pltpu.VMEM((1024, 384), BF16)],
+        *flat_parts(token_parts),
+        by_partner(dec_gain),
+        by_partner(head_weight),
+        flat_pos,
+        text_proj,
+        scalars=where,
+    )
+    heads = run(
+        decode_kernel,
+        jax.ShapeDtypeStruct((16, text_rows, 128), BF16),
+        [],
+        query,
+        key,
+        value,
+        over_c(key),
+        over_c(value),
+        scalars=where,
+    )
+    by_core = [[2 * w_ + y_ for w_ in range(c_, 16, 2) for y_ in (0, 1)] for c_ in (0, 1)]
+    heads = lax.all_to_all(
+        heads, ("wide", "narrow"), 0, 0, axis_index_groups=by_core, tiled=True
+    )
+    dec_out_rows = share_out(dec_out, z, y, w)
+    routed = routed.reshape(4, text_rows, 4, D // 16)
+    routed = lax.dynamic_slice_in_dim(routed, 2 * y, 2, axis=2)
+    ordered = jnp.stack(
+        [
+            lax.dynamic_index_in_dim(routed, jnp.bitwise_xor(2 * x + c, code), 0, keepdims=False)
+            for code in range(4)
+        ]
+    )
+    ordered = ordered.transpose(1, 2, 0, 3).reshape(text_rows, half)
+    mine = w * text_rows + jnp.arange(text_rows, dtype=jnp.int32)
+    is_image = jnp.any(mine[:, None] == prompt_pos.reshape(1, -1), axis=1)
+    dec_in = jnp.where(is_image[:, None], ordered, text_embeds)
+    return run(
+        finish_kernel,
+        jax.ShapeDtypeStruct(text_embeds.shape, BF16),
+        [],
+        heads,
+        dec_out_rows,
+        dec_in,
+        scalars=where,
+    )
+
+
 def solution(mesh):
     placed = (
         P("wide", None, "narrow"),
@@ -210,6 +640,8 @@
         P("wide", "narrow"),
         P("narrow", "wide"),
     )
+    sizes = (mesh.shape["wide"], mesh.shape["narrow"])
+    shards = shards_fast if sizes == (16, 2) else shards_any
     return jax.shard_map(
         shards, mesh=mesh, in_specs=placed, out_specs=P("wide", "narrow"), check_vma=False
     )

time: 489 us -> 308 us (0.63)
  waiting for transfers between devices: 371 us -> 59.4 us
  starting transfers between devices: 0.59 us -> 94 us
  Pallas kernels: 0 us -> 27.7 us
  matrix products: 24.8 us -> 5.37 us
  blocking collectives: 19.5 us -> 38.4 us
  other arithmetic: 11.2 us -> 18.3 us
  loops' own time: 5.3 us -> 0 us
    all_gather x8 -> x2, waiting for transfers between devices: 321 us -> 0.01 us  [the longest x1 0.01 us: shards_fast(): lax.all_gather(sliced, 'wide', axis_index_groups=GROUPS_Z, axis=0, tiled=...]
    ppermute x0 -> x48, starting transfers between devices: none -> 82 us  [the longest x2 37.6 us: share_out(): held = jnp.concatenate([held, lax.ppermute(held, 'wide', near)])]
    ppermute x0 -> x48, waiting for transfers between devices: none -> 58.1 us  [the longest x10 30 us: over_x(): return lax.ppermute(value, 'wide', CROSS_X)]
    reduce_scatter x2 -> x0, waiting for transfers between devices: 32.2 us -> none  [the longest x1 21.2 us: shards(): lax.psum_scatter(vit_partial, 'narrow', scatter_dimension=1, tiled=True)]
    pallas_call x0 -> x5, Pallas kernels: none -> 27.7 us  [run(): pl.pallas_call(kernel, out_shape=shapes, in_specs=specs, out_specs=VMEM i...]
    all_gather x3 -> x0, local copies, waits for them, and re-layouts: 23.8 us -> none  [the longest x1 12.4 us: shards(): piece = lax.all_gather(merge_weight, 'wide', axis=2, tiled=True)]
    reshape x3 -> x12, local copies, waits for them, and re-layouts: 0.56 us -> 21 us  [the longest x4 17.1 us: share_out(): whole.transpose(1, 3, 0, 2).reshape(2 * block.shape[0], 8 * block.shape[1])]
    dot_general x10 -> x0, matrix products: 17.2 us -> none  [the longest x1 4.88 us: shards(): jnp.dot(grouped, flat_piece, preferred_element_type=jnp.float32)]
  transfers between devices with their start and end apart: 11 -> 52, of which waited for: 11 -> 17; matrix products, arithmetic and copies ran while one was open for 9% -> 20% of each run, Pallas kernels for 0% -> 4%
where the time goes in v1:
time: 308 us; the launch traced here: 304 us
  starting transfers between devices  94 us (31%)
  waiting for transfers between devices  59.4 us (19%)
  local copies, waits for them, and re-layouts  45.9 us (15%)
  blocking collectives  38.4 us (12%)
  Pallas kernels  27.7 us (9%)
  other arithmetic  18.3 us (6%)
  between operations  14.9 us (5%)
  matrix products  5.37 us (2%)
    ppermute x2, starting transfers between devices, share_out(): held = jnp.concatenate([held, lax.ppermute(held, 'wide', near)])  37.6 us
    ppermute x10, waiting for transfers between devices, over_x(): return lax.ppermute(value, 'wide', CROSS_X)  30 us
    pallas_call x5, Pallas kernels, run(): pl.pallas_call(kernel, out_shape=shapes, in_specs=specs, out_specs=VMEM i...  27.7 us
    all_gather x1, blocking collectives, shards_fast(): lax.all_gather(text_embeds, 'wide', axis_index_groups=GROUPS_Z, axis=0, t...  27.5 us
    reshape x4, local copies, waits for them, and re-layouts, share_out(): whole.transpose(1, 3, 0, 2).reshape(2 * block.shape[0], 8 * block.shape[1])  17.1 us
    ppermute x9, starting transfers between devices, over_y(): return lax.ppermute(value, 'narrow', CROSS_Y)  15.3 us
    unnamed x75, local copies, waits for them, and re-layouts  13.6 us
    ppermute x10, starting transfers between devices, over_x(): return lax.ppermute(value, 'wide', CROSS_X)  11.8 us
  transfers between devices with their start and end apart: 52, of which 17 were waited for; matrix products, arithmetic and copies ran while one was open for 20% of the time, Pallas kernels for 4%

profile of v1, /device:TPU:0, one launch (start us, length us, event | category | flops | bytes accessed | tf_op | source)
XLA Modules:
  0.0 304.0 jit_solution(17321454017067085222)
XLA Ops:
  8.1 10.9 %all_to_all.15 = bf16[4,80,480]{2,1,0:T(8,128)(2,1)} all-to-all(bf16[4,80,480]{2,1,0:T(8,128)(2,1)S(1)} %bitcast.69), channel_id=1, replica_groups={{0,2,4,6},{8,10,12,14},{16,18,20,22},{24,26,28,30},{1,3,5,7},{9,11,13,1..., dimensions={0} | all-to-all | bytes 614400 | tf_op jit(solution)/shard_map/all_to_all | solution.py:495
  19.0 27.5 %all_gather.11 = bf16[640,640]{1,0:T(8,128)(2,1)S(1)} all-gather(bf16[160,640]{1,0:T(8,128)(2,1)S(1)} %copy-done.22), channel_id=1, replica_groups={{0,8,16,24},{2,10,18,26},{4,12,20,28},{6,14,22,30},{1,9,17,25},{3,11,19..., dimensions={0}, use_global_device_ids=true | all-gather | bytes 1024000 | tf_op jit(solution)/shard_map/all_gather | solution.py:560
  54.0 7.1 %all-to-all-start.1 = ((bf16[16,80,120]{2,1,0:T(8,128)(2,1)}), bf16[16,80,120]{2,1,0:T(8,128)(2,1)}, u32[]{:S(2)}, u32[]{:S(2)}) async-start(bf16[16,80,120]{2,1,0:T(8,128)(2,1)} %bitcast.54), calls=%async_computation.1 | async-start | bytes 655360 | tf_op jit(solution)/shard_map/all_to_all | solution.py:542
  62.2 4.3 %collective-permute-done.43 = bf16[80,640]{1,0:T(8,128)(2,1)S(1)} collective-permute-done((bf16[80,640]{1,0:T(8,128)(2,1)S(1)}, bf16[80,640]{1,0:T(8,128)(2,1)S(1)}, u32[]{:S(2)}, u32[]{:S(2)}) %collective-permute-start.43) | collective-permute-done | bytes 102432 | tf_op jit(solution)/shard_map/ppermute | solution.py:452
  70.6 4.5 %collective-permute-done.44 = bf16[2,80,640]{2,1,0:T(8,128)(2,1)S(1)} collective-permute-done((bf16[2,80,640]{2,1,0:T(8,128)(2,1)S(1)}, bf16[2,80,640]{2,1,0:T(8,128)(2,1)S(1)}, u32[]{:S(2)}, u32[]{:S(2)}) %collective-permute-start.44) | collective-permute-done | bytes 204832 | tf_op jit(solution)/shard_map/ppermute | solution.py:454
  75.1 28.0 %collective-permute-start.45 = (bf16[1,2,80,640]{3,2,1,0:T(8,128)(2,1)S(1)}, bf16[1,2,80,640]{3,2,1,0:T(8,128)(2,1)S(1)}, u32[]{:S(2)}, u32[]{:S(2)}) collective-permute-start(bf16[1,2,80,640]{3,2,1,0:T(8,128)(2,1)S(1)} %select_bitcast_fusion), channel_id=1, source_target_pairs={{0,8},{2,10},{4,12},{6,14},{8,0},{10,2},{12,4},{14,6},{16,24},{18,... | collective-permute-start | bytes 614408 | tf_op jit(solution)/shard_map/ppermute | solution.py:457
  103.2 9.6 %collective-permute-start.20 = (bf16[1,2,80,640]{3,2,1,0:T(8,128)(2,1)S(1)}, bf16[1,2,80,640]{3,2,1,0:T(8,128)(2,1)S(1)}, u32[]{:S(2)}, u32[]{:S(2)}) collective-permute-start(bf16[1,2,80,640]{3,2,1,0:T(8,128)(2,1)S(1)} %select_bitcast_fusion.1), channel_id=1, source_target_pairs={{0,8},{2,10},{4,12},{6,14},{8,0},{10,2},{12,4},{14,6},{16,24},{18,... | collective-permute-start | bytes 614408 | tf_op jit(solution)/shard_map/ppermute | solution.py:457
  119.4 6.9 %collective-permute-done.46 = bf16[2,2,80,640]{3,2,1,0:T(8,128)(2,1)S(1)} collective-permute-done((bf16[2,2,80,640]{3,2,1,0:T(8,128)(2,1)}, bf16[2,2,80,640]{3,2,1,0:T(8,128)(2,1)S(1)}, u32[]{:S(2)}, u32[]{:S(2)}) %collective-permute-start.46) | collective-permute-done | bytes 409632 | tf_op jit(solution)/shard_map/ppermute | solution.py:215
  127.8 4.7 %collective-permute-done.21 = bf16[2,2,80,640]{3,2,1,0:T(8,128)(2,1)S(1)} collective-permute-done((bf16[2,2,80,640]{3,2,1,0:T(8,128)(2,1)}, bf16[2,2,80,640]{3,2,1,0:T(8,128)(2,1)S(1)}, u32[]{:S(2)}, u32[]{:S(2)}) %collective-permute-start.21) | collective-permute-done | bytes 409632 | tf_op jit(solution)/shard_map/ppermute | solution.py:215
  134.8 6.0 %collective-permute-start = (bf16[256,640]{1,0:T(8,128)(2,1)S(1)}, bf16[256,640]{1,0:T(8,128)(2,1)S(1)}, u32[]{:S(2)}, u32[]{:S(2)}) collective-permute-start(bf16[256,640]{1,0:T(8,128)(2,1)S(1)} %bitcast.57), channel_id=1, source_target_pairs={{0,1},{1,0},{2,3},{3,2},{4,5},{5,4},{6,7},{7,6},{8,9},{9,8},{10,11... | collective-permute-start | bytes 983048 | tf_op jit(solution)/shard_map/ppermute | solution.py:223
  141.0 8.2 %collective-permute-done.refs_1_ = bf16[256,640]{1,0:T(8,128)(2,1)S(1)} collective-permute-done((bf16[256,640]{1,0:T(8,128)(2,1)S(1)}, bf16[256,640]{1,0:T(8,128)(2,1)S(1)}, u32[]{:S(2)}, u32[]{:S(2)}) %collective-permute-start) | collective-permute-done | bytes 327712 | tf_op jit(solution)/shard_map/ppermute | solution.py:223
  168.3 6.5 %shard_map.100.refs_0_ = bf16[160,1024]{1,0:T(8,128)(2,1)S(1)} custom-call(bf16[256,640]{1,0:T(8,128)(2,1)S(1)} %bitcast.59, bf16[256,640]{1,0:T(8,128)(2,1)S(1)} %collective-permute-done.refs_1_, bf16[256,640]{1,0:T(8,128)(2,1)S(1)} %collective-permute-done.1.refs_2_.refs_11_, bf16[256,640]{1,0:T(8,128)(2,1)S(1)} %copy-done.4, ...), custom_call_target="tpu_custom_call" | custom-call | tf_op jit(solution)/shard_map/pallas_call | solution.py:439
  176.2 8.6 %collective-permute-done.12.refs_4_ = bf16[160,1024]{1,0:T(8,128)(2,1)} collective-permute-done((bf16[160,1024]{1,0:T(8,128)(2,1)S(1)}, bf16[160,1024]{1,0:T(8,128)(2,1)}, u32[]{:S(2)}, u32[]{:S(2)}) %collective-permute-start.12) | collective-permute-done | bytes 327712 | tf_op jit(solution)/shard_map/ppermute | solution.py:215
  195.2 4.8 %copy.52 = bf16[2,640,8,80]{3,2,1,0:T(8,128)(2,1)} copy(bf16[2,640,8,80]{1,3,0,2:T(8,128)(2,1)} %bitcast.67) | data formatting | bytes 3276800 | tf_op jit(solution)/shard_map/reshape | solution.py:466
  200.0 3.8 %reshape.288.refs_14_ = bf16[1280,640]{1,0:T(8,128)(2,1)S(1)} reshape(bf16[2,640,8,80]{3,2,1,0:T(8,128)(2,1)} %copy.52) | data formatting | bytes 3276800 | tf_op jit(solution)/shard_map/reshape | solution.py:466
  207.0 6.7 %shard_map.101 = (f32[128,320]{1,0:T(8,128)S(1)}, f32[128,320]{1,0:T(8,128)}) custom-call(s32[4]{0:T(128)S(1)} %pad_add_fusion.where, bf16[160,1024]{1,0:T(8,128)(2,1)S(1)} %shard_map.100.refs_0_, bf16[160,1024]{1,0:T(8,128)(2,1)} %collective-permute-done.9.refs_1_, bf16[160,1024]{1,0:T(8,128)(2,1)S(1)} %copy-done.2, ...), custom_call_target="tpu_custom_call" | custom-call | tf_op jit(solution)/shard_map/pallas_call | solution.py:439
  221.8 6.4 %collective-permute-start.26 = (bf16[128,320]{1,0:T(8,128)(2,1)S(1)}, bf16[128,320]{1,0:T(8,128)(2,1)S(1)}, u32[]{:S(2)}, u32[]{:S(2)}) collective-permute-start(bf16[128,320]{1,0:T(8,128)(2,1)S(1)} %add_convert_fusion), channel_id=1, source_target_pairs={{0,24},{2,26},{4,28},{6,30},{8,0},{10,2},{12,4},{14,6},{16,8},{18,... | collective-permute-start | bytes 245768 | tf_op jit(solution)/shard_map/ppermute | solution.py:535
  231.5 4.4 %collective-permute-done.25 = bf16[128,320]{1,0:T(8,128)(2,1)S(1)} collective-permute-done((bf16[128,320]{1,0:T(8,128)(2,1)S(1)}, bf16[128,320]{1,0:T(8,128)(2,1)S(1)}, u32[]{:S(2)}, u32[]{:S(2)}) %collective-permute-start.25) | collective-permute-done | bytes 81952 | tf_op jit(solution)/shard_map/ppermute | solution.py:535
  239.8 6.7 %collective-permute-done.30.refs_4_ = bf16[512,320]{1,0:T(8,128)(2,1)S(1)} collective-permute-done((bf16[512,320]{1,0:T(8,128)(2,1)S(1)}, bf16[512,320]{1,0:T(8,128)(2,1)S(1)}, u32[]{:S(2)}, u32[]{:S(2)}) %collective-permute-start.30) | collective-permute-done | bytes 327712 | tf_op jit(solution)/shard_map/ppermute | solution.py:215
  257.5 6.2 %shard_map.102 = (bf16[1280,128]{1,0:T(8,128)(2,1)S(1)}, bf16[1280,128]{1,0:T(8,128)(2,1)S(1)}, bf16[1280,128]{1,0:T(8,128)(2,1)S(1)}, bf16[4,160,320]{2,1,0:T(8,128)(2,1)S(1)}) custom-call(s32[4]{0:T(128)S(1)} %pad_add_fusion.where, bf16[512,320]{1,0:T(8,128)(2,1)S(1)} %pad_maximum_fusion.10.refs_0_, bf16[512,320]{1,0:T(8,128)(2,1)S(1)} %collective-permute-done.27.refs_1_, ...), custom_call_target="tpu_custom_call" | custom-call | tf_op jit(solution)/shard_map/pallas_call | solution.py:439
  266.0 6.0 %shard_map.103 = bf16[16,160,128]{2,1,0:T(8,128)(2,1)} custom-call(s32[4]{0:T(128)S(1)} %pad_add_fusion.where, bf16[1280,128]{1,0:T(8,128)(2,1)S(1)} %get-tuple-element.14.query, bf16[1280,128]{1,0:T(8,128)(2,1)S(1)} %get-tuple-element.15.own_key, bf16[1280,128]{1,0:T(8,128)(2,1)S(1)} %get-tuple-element.16.own_value, ...), custom_call_target="tpu_custom_call" | custom-call | tf_op jit(solution)/shard_map/pallas_call | solution.py:439
  272.1 4.9 %all-to-all-start.2 = ((bf16[16,160,128]{2,1,0:T(8,128)(2,1)}), bf16[16,160,128]{2,1,0:T(8,128)(2,1)S(1)}, u32[]{:S(2)}, u32[]{:S(2)}) async-start(bf16[16,160,128]{2,1,0:T(8,128)(2,1)} %shard_map.103), calls=%async_computation.2 | async-start | bytes 1310720 | tf_op jit(solution)/shard_map/all_to_all | solution.py:602
  282.8 4.7 %copy.53 = bf16[2,640,8,80]{3,2,1,0:T(8,128)(2,1)} copy(bf16[2,640,8,80]{1,3,0,2:T(8,128)(2,1)} %bitcast.66) | data formatting | bytes 3276800 | tf_op jit(solution)/shard_map/reshape | solution.py:466
  287.5 3.8 %reshape.289.weight = bf16[1280,640]{1,0:T(8,128)(2,1)S(1)} reshape(bf16[2,640,8,80]{3,2,1,0:T(8,128)(2,1)} %copy.53) | data formatting | bytes 3276800 | tf_op jit(solution)/shard_map/reshape | solution.py:466
  (245 shorter events, 97.8 us)
Async XLA Ops:
  6.5 156.9 %all-gather.3.cloned.1.call-start = ((), (), s32[]{:S(2)}) async-start(), calls=%async_computation.3 | async-start | bytes 1638400 | tf_op jit(solution)/shard_map/all_gather | solution.py:497
  46.6 104.4 %collective-permute-start.37 = (bf16[640,640]{1,0:T(8,128)(2,1)S(1)}, bf16[640,640]{1,0:T(8,128)(2,1)}, u32[]{:S(2)}, u32[]{:S(2)}) collective-permute-start(bf16[640,640]{1,0:T(8,128)(2,1)S(1)} %all_gather.11), channel_id=1, source_target_pairs={{0,1},{1,0},{2,3},{3,2},{4,5},{5,4},{6,7},{7,6},{8,9},{9,8},{10,11... | collective-permute-start | bytes 2457608 | tf_op jit(solution)/shard_map/ppermute | solution.py:223
  47.9 107.8 %collective-permute-start.38 = (bf16[640,640]{1,0:T(8,128)(2,1)S(1)}, bf16[640,640]{1,0:T(8,128)(2,1)}, u32[]{:S(2)}, u32[]{:S(2)}) collective-permute-start(bf16[640,640]{1,0:T(8,128)(2,1)S(1)} %all_gather.11), channel_id=1, source_target_pairs={{0,4},{2,6},{4,0},{6,2},{8,12},{10,14},{12,8},{14,10},{16,20},{18,... | collective-permute-start | bytes 2457608 | tf_op jit(solution)/shard_map/ppermute | solution.py:215
  47.9 86.9 %collective-permute-start.3 = (bf16[256,640]{1,0:T(8,128)(2,1)S(1)}, bf16[256,640]{1,0:T(8,128)(2,1)S(1)}, u32[]{:S(2)}, u32[]{:S(2)}) collective-permute-start(bf16[256,640]{1,0:T(8,128)(2,1)S(1)} %bitcast.56), channel_id=1, source_target_pairs={{0,4},{2,6},{4,0},{6,2},{8,12},{10,14},{12,8},{14,10},{16,20},{18,... | collective-permute-start | bytes 983048 | tf_op jit(solution)/shard_map/ppermute | solution.py:215
  49.9 16.5 %collective-permute-start.43 = (bf16[80,640]{1,0:T(8,128)(2,1)S(1)}, bf16[80,640]{1,0:T(8,128)(2,1)S(1)}, u32[]{:S(2)}, u32[]{:S(2)}) collective-permute-start(bf16[80,640]{1,0:T(8,128)(2,1)S(1)} %bitcast.77), channel_id=1, source_target_pairs={{1,0},{3,2},{5,4},{7,6},{9,8},{11,10},{13,12},{15,14},{16,17},{18,... | collective-permute-start | bytes 307208 | tf_op jit(solution)/shard_map/ppermute | solution.py:452
  51.2 17.5 %collective-permute-start.18 = (bf16[80,640]{1,0:T(8,128)(2,1)S(1)}, bf16[80,640]{1,0:T(8,128)(2,1)S(1)}, u32[]{:S(2)}, u32[]{:S(2)}) collective-permute-start(bf16[80,640]{1,0:T(8,128)(2,1)S(1)} %bitcast.80), channel_id=1, source_target_pairs={{1,0},{3,2},{5,4},{7,6},{9,8},{11,10},{13,12},{15,14},{16,17},{18,... | collective-permute-start | bytes 307208 | tf_op jit(solution)/shard_map/ppermute | solution.py:452
  54.0 112.0 %all-to-all-start.1 = ((bf16[16,80,120]{2,1,0:T(8,128)(2,1)}), bf16[16,80,120]{2,1,0:T(8,128)(2,1)}, u32[]{:S(2)}, u32[]{:S(2)}) async-start(bf16[16,80,120]{2,1,0:T(8,128)(2,1)} %bitcast.54), calls=%async_computation.1 | async-start | bytes 655360 | tf_op jit(solution)/shard_map/all_to_all | solution.py:542
  61.1 144.0 %all-gather.5.cloned.1.call-start = ((), (), s32[]{:S(2)}) async-start(), calls=%async_computation.4 | async-start | bytes 2048000 | tf_op jit(solution)/shard_map/all_gather | solution.py:499
  68.8 34.4 %collective-permute-start.19 = (bf16[2,80,640]{2,1,0:T(8,128)(2,1)S(1)}, bf16[2,80,640]{2,1,0:T(8,128)(2,1)S(1)}, u32[]{:S(2)}, u32[]{:S(2)}) collective-permute-start(bf16[2,80,640]{2,1,0:T(8,128)(2,1)S(1)} %pad_maximum_fusion.11), channel_id=1, source_target_pairs={{0,16},{2,18},{4,20},{6,22},{8,24},{10,26},{12,28},{14,30},{17,1},... | collective-permute-start | bytes 614408 | tf_op jit(solution)/shard_map/ppermute | solution.py:454
  75.1 37.7 %collective-permute-start.45 = (bf16[1,2,80,640]{3,2,1,0:T(8,128)(2,1)S(1)}, bf16[1,2,80,640]{3,2,1,0:T(8,128)(2,1)S(1)}, u32[]{:S(2)}, u32[]{:S(2)}) collective-permute-start(bf16[1,2,80,640]{3,2,1,0:T(8,128)(2,1)S(1)} %select_bitcast_fusion), channel_id=1, source_target_pairs={{0,8},{2,10},{4,12},{6,14},{8,0},{10,2},{12,4},{14,6},{16,24},{18,... | collective-permute-start | bytes 614408 | tf_op jit(solution)/shard_map/ppermute | solution.py:457
  103.2 13.6 %collective-permute-start.20 = (bf16[1,2,80,640]{3,2,1,0:T(8,128)(2,1)S(1)}, bf16[1,2,80,640]{3,2,1,0:T(8,128)(2,1)S(1)}, u32[]{:S(2)}, u32[]{:S(2)}) collective-permute-start(bf16[1,2,80,640]{3,2,1,0:T(8,128)(2,1)S(1)} %select_bitcast_fusion.1), channel_id=1, source_target_pairs={{0,8},{2,10},{4,12},{6,14},{8,0},{10,2},{12,4},{14,6},{16,24},{18,... | collective-permute-start | bytes 614408 | tf_op jit(solution)/shard_map/ppermute | solution.py:457
  113.7 12.6 %collective-permute-start.46 = (bf16[2,2,80,640]{3,2,1,0:T(8,128)(2,1)}, bf16[2,2,80,640]{3,2,1,0:T(8,128)(2,1)S(1)}, u32[]{:S(2)}, u32[]{:S(2)}) collective-permute-start(bf16[2,2,80,640]{3,2,1,0:T(8,128)(2,1)} %pad_maximum_fusion.9), channel_id=1, source_target_pairs={{0,4},{2,6},{4,0},{6,2},{8,12},{10,14},{12,8},{14,10},{16,20},{18,... | collective-permute-start | bytes 1228808 | tf_op jit(solution)/shard_map/ppermute | solution.py:215
  117.6 14.9 %collective-permute-start.21 = (bf16[2,2,80,640]{3,2,1,0:T(8,128)(2,1)}, bf16[2,2,80,640]{3,2,1,0:T(8,128)(2,1)S(1)}, u32[]{:S(2)}, u32[]{:S(2)}) collective-permute-start(bf16[2,2,80,640]{3,2,1,0:T(8,128)(2,1)} %pad_maximum_fusion.8), channel_id=1, source_target_pairs={{0,4},{2,6},{4,0},{6,2},{8,12},{10,14},{12,8},{14,10},{16,20},{18,... | collective-permute-start | bytes 1228808 | tf_op jit(solution)/shard_map/ppermute | solution.py:215
  127.4 30.1 %collective-permute-start.47 = (bf16[4,2,80,640]{3,2,1,0:T(8,128)(2,1)}, bf16[4,2,80,640]{3,2,1,0:T(8,128)(2,1)}, u32[]{:S(2)}, u32[]{:S(2)}) collective-permute-start(bf16[4,2,80,640]{3,2,1,0:T(8,128)(2,1)} %pad_maximum_fusion.7), channel_id=1, source_target_pairs={{0,2},{2,0},{4,6},{6,4},{8,10},{10,8},{12,14},{14,12},{16,18},{18,... | collective-permute-start | bytes 2457608 | tf_op jit(solution)/shard_map/ppermute | solution.py:219
  133.6 26.4 %collective-permute-start.22 = (bf16[4,2,80,640]{3,2,1,0:T(8,128)(2,1)}, bf16[4,2,80,640]{3,2,1,0:T(8,128)(2,1)}, u32[]{:S(2)}, u32[]{:S(2)}) collective-permute-start(bf16[4,2,80,640]{3,2,1,0:T(8,128)(2,1)} %pad_maximum_fusion.6), channel_id=1, source_target_pairs={{0,2},{2,0},{4,6},{6,4},{8,10},{10,8},{12,14},{14,12},{16,18},{18,... | collective-permute-start | bytes 2457608 | tf_op jit(solution)/shard_map/ppermute | solution.py:219
  134.8 14.4 %collective-permute-start = (bf16[256,640]{1,0:T(8,128)(2,1)S(1)}, bf16[256,640]{1,0:T(8,128)(2,1)S(1)}, u32[]{:S(2)}, u32[]{:S(2)}) collective-permute-start(bf16[256,640]{1,0:T(8,128)(2,1)S(1)} %bitcast.57), channel_id=1, source_target_pairs={{0,1},{1,0},{2,3},{3,2},{4,5},{5,4},{6,7},{7,6},{8,9},{9,8},{10,11... | collective-permute-start | bytes 983048 | tf_op jit(solution)/shard_map/ppermute | solution.py:223
  166.0 49.4 %collective-permute-start.36 = (bf16[1280,120]{1,0:T(8,128)(2,1)}, bf16[1280,120]{1,0:T(8,128)(2,1)}, u32[]{:S(2)}, u32[]{:S(2)}) collective-permute-start(bf16[1280,120]{1,0:T(8,128)(2,1)} %bitcast.19), channel_id=1, source_target_pairs={{0,2},{2,0},{4,6},{6,4},{8,10},{10,8},{12,14},{14,12},{16,18},{18,... | collective-permute-start | bytes 921608 | tf_op jit(solution)/shard_map/ppermute | solution.py:219
  176.0 13.4 %collective-permute-start.10 = (bf16[160,1024]{1,0:T(8,128)(2,1)S(1)}, bf16[160,1024]{1,0:T(8,128)(2,1)S(1)}, u32[]{:S(2)}, u32[]{:S(2)}) collective-permute-start(bf16[160,1024]{1,0:T(8,128)(2,1)S(1)} %shard_map.100.refs_0_), channel_id=1, source_target_pairs={{0,2},{2,0},{4,6},{6,4},{8,10},{10,8},{12,14},{14,12},{16,18},{18,... | collective-permute-start | bytes 983048 | tf_op jit(solution)/shard_map/ppermute | solution.py:219
  189.3 14.6 %collective-permute-start.11 = (bf16[160,1024]{1,0:T(8,128)(2,1)}, bf16[160,1024]{1,0:T(8,128)(2,1)}, u32[]{:S(2)}, u32[]{:S(2)}) collective-permute-start(bf16[160,1024]{1,0:T(8,128)(2,1)} %collective-permute-done.9.refs_1_), channel_id=1, source_target_pairs={{0,2},{2,0},{4,6},{6,4},{8,10},{10,8},{12,14},{14,12},{16,18},{18,... | collective-permute-start | bytes 983048 | tf_op jit(solution)/shard_map/ppermute | solution.py:219
  190.1 14.6 %collective-permute-start.15 = (bf16[160,1024]{1,0:T(8,128)(2,1)}, bf16[160,1024]{1,0:T(8,128)(2,1)}, u32[]{:S(2)}, u32[]{:S(2)}) collective-permute-start(bf16[160,1024]{1,0:T(8,128)(2,1)} %collective-permute-done.12.refs_4_), channel_id=1, source_target_pairs={{0,2},{2,0},{4,6},{6,4},{8,10},{10,8},{12,14},{14,12},{16,18},{18,... | collective-permute-start | bytes 983048 | tf_op jit(solution)/shard_map/ppermute | solution.py:219
  191.1 13.9 %collective-permute-start.16 = (bf16[80,1024]{1,0:T(8,128)(2,1)S(1)}, bf16[80,1024]{1,0:T(8,128)(2,1)}, u32[]{:S(2)}, u32[]{:S(2)}) collective-permute-start(bf16[80,1024]{1,0:T(8,128)(2,1)S(1)} %collective-permute-done.13.refs_5_), channel_id=1, source_target_pairs={{0,2},{2,0},{4,6},{6,4},{8,10},{10,8},{12,14},{14,12},{16,18},{18,... | collective-permute-start | bytes 491528 | tf_op jit(solution)/shard_map/ppermute | solution.py:219
  203.9 34.1 %collective-permute-start.40 = (bf16[320,640]{1,0:T(8,128)(2,1)}, bf16[320,640]{1,0:T(8,128)(2,1)}, u32[]{:S(2)}, u32[]{:S(2)}) collective-permute-start(bf16[320,640]{1,0:T(8,128)(2,1)} %slice.43), channel_id=1, source_target_pairs={{0,4},{2,6},{4,0},{6,2},{8,12},{10,14},{12,8},{14,10},{16,20},{18,... | collective-permute-start | bytes 1228808 | tf_op jit(solution)/shard_map/ppermute | solution.py:215
  204.7 33.3 %collective-permute-start.39 = (bf16[320,640]{1,0:T(8,128)(2,1)}, bf16[320,640]{1,0:T(8,128)(2,1)}, u32[]{:S(2)}, u32[]{:S(2)}) collective-permute-start(bf16[320,640]{1,0:T(8,128)(2,1)} %slice.42), channel_id=1, source_target_pairs={{0,1},{1,0},{2,3},{3,2},{4,5},{5,4},{6,7},{7,6},{8,9},{9,8},{10,11... | collective-permute-start | bytes 1228808 | tf_op jit(solution)/shard_map/ppermute | solution.py:223
  272.1 22.6 %all-to-all-start.2 = ((bf16[16,160,128]{2,1,0:T(8,128)(2,1)}), bf16[16,160,128]{2,1,0:T(8,128)(2,1)S(1)}, u32[]{:S(2)}, u32[]{:S(2)}) async-start(bf16[16,160,128]{2,1,0:T(8,128)(2,1)} %shard_map.103), calls=%async_computation.2 | async-start | bytes 1310720 | tf_op jit(solution)/shard_map/all_to_all | solution.py:602
  (57 other events, 664.9 us)
Sparse Core Ops, SparseCore 0:
  19.1 39.5 all-gather.2
  63.5 42.3 all-gather.4

commit v2 on v0

--- a/solution.py
+++ b/solution.py
@@ -1,6 +1,8 @@
 import jax
 import jax.numpy as jnp
 from jax import lax
+from jax.experimental import pallas as pl
+from jax.experimental.pallas import tpu as pltpu
 from jax.sharding import PartitionSpec as P
 
 D = 1280
@@ -70,7 +72,7 @@
     return summed / total[..., None]
 
 
-def shards(
+def shards_any(
     patches,
     grid,
     vit_gain,
@@ -196,6 +198,635 @@
     return result
 
 
+CROSS_X = [(w, w ^ 2) for w in range(16)]
+CROSS_C = [(w, w ^ 1) for w in range(16)]
+CROSS_Y = [(0, 1), (1, 0)]
+GROUPS_Z = [[b, 4 + b, 8 + b, 12 + b] for b in range(4)]
+GROUPS_B = [[4 * z + b for b in range(4)] for z in range(4)]
+FOUR = ((0, 0), (0, 1), (1, 0), (1, 1))
+SMEM = pl.BlockSpec(memory_space=pltpu.SMEM)
+F32 = jnp.float32
+BF16 = jnp.bfloat16
+GRANT = 48 * 1024 * 1024
+MOST = 59 * 1024 * 1024
+
+
+def over_x(value):
+    return lax.ppermute(value, "wide", CROSS_X)
+
+
+def over_c(value):
+    return lax.ppermute(value, "wide", CROSS_C)
+
+
+def over_y(value):
+    return lax.ppermute(value, "narrow", CROSS_Y)
+
+
+RING_Z = [(4 * a + b, 4 * n + b) for a, n in ((0, 1), (1, 3), (3, 2), (2, 0)) for b in range(4)]
+
+
+def next_z(value):
+    return lax.ppermute(value, "wide", RING_Z)
+
+
+def z_behind(z, steps):
+    place = lax.rem(jnp.bitwise_xor(z, z // 2) + 4 - steps, 4)
+    return jnp.bitwise_xor(place, place // 2)
+
+
+def around_z(value):
+    return [value] + [
+        lax.ppermute(value, "wide", [(w, (w + 4 * k) % 16) for w in range(16)]) for k in (1, 2, 3)
+    ]
+
+
+def over_xy(value):
+    both = [(2 * w + y, 2 * (w ^ 2) + 1 - y) for w in range(16) for y in (0, 1)]
+    return lax.ppermute(value, ("wide", "narrow"), both)
+
+
+def share_xy(value):
+    return [[value, over_y(value)], [over_x(value), over_xy(value)]]
+
+
+def share_xyc(value):
+    pieces = share_xy(value)
+    return [
+        over_c(pieces[ex][ey]) if ec else pieces[ex][ey]
+        for ex, ec in FOUR
+        for ey in (0, 1)
+    ]
+
+
+def contract(left, right, left_dim, right_dim):
+    return lax.dot_general(
+        left, right, (((left_dim,), (right_dim,)), ((), ())), preferred_element_type=F32
+    )
+
+
+def patch_order():
+    row = lax.broadcasted_iota(jnp.int32, (256, 256), 0)
+    column = lax.broadcasted_iota(jnp.int32, (256, 256), 1)
+    sub, token = row // 64, row % 64
+    source = (2 * (token // 8) + sub // 2) * 16 + 2 * (token % 8) + sub % 2
+    return jnp.where(column == source, 1.0, 0.0).astype(BF16)
+
+
+def norm_kernel(where, *refs):
+    parts = refs[:8]
+    gain, normed, residual = refs[8:]
+    order = patch_order()
+    own_gain = gain[pl.ds(where[3], 1), :]
+    other_gain = gain[pl.ds(1 - where[3], 1), :]
+    for slot in range(4):
+        raw = parts[2 * slot][...]
+        own = raw.astype(F32)
+        other = parts[2 * slot + 1][...].astype(F32)
+        mean = (
+            jnp.sum(own, axis=-1, keepdims=True) + jnp.sum(other, axis=-1, keepdims=True)
+        ) * (1.0 / D)
+        own = own - mean
+        other = other - mean
+        spread = (
+            jnp.sum(own * own, axis=-1, keepdims=True)
+            + jnp.sum(other * other, axis=-1, keepdims=True)
+        ) * (1.0 / D)
+        scale = lax.rsqrt(spread + eps_norm)
+        own = (own * scale * own_gain).astype(BF16)
+        other = (other * scale * other_gain).astype(BF16)
+        at = slice(slot * 256, (slot + 1) * 256)
+        normed[at, : D // 2] = contract(order, own, 1, 0).astype(BF16)
+        normed[at, D // 2 :] = contract(order, other, 1, 0).astype(BF16)
+        residual[:, at] = contract(raw, order, 0, 1).astype(BF16)
+
+
+def own_half_first(where, block):
+    row = block * (D // 16) - where[3] * (D // 2)
+    return pl.multiple_of(jnp.where(row < 0, row + D, row), 16)
+
+
+def encode_kernel(where, normed, first, second, third, fourth, keep, out, weight):
+    block = D // 16
+    here = where[1] * 2 + where[2]
+    for steps, piece in enumerate((first, second, third, fourth)):
+        z = z_behind(where[0], steps)
+        for code in range(4):
+            row = own_half_first(where, 4 * z + jnp.bitwise_xor(here, code))
+            weight[pl.ds(row, block), :] = piece[code * block : (code + 1) * block, :]
+    for slot in range(4):
+        proj = contract(normed[slot * 256 : (slot + 1) * 256, :], weight[...], 1, 0).astype(BF16)
+        live = keep[:, slot : slot + 1] > 0.0
+        for head in (0, 1):
+            base = head * 3 * HEAD
+            query = proj[:, base : base + HEAD]
+            key_rows = proj[:, base + HEAD : base + 2 * HEAD]
+            value_rows = proj[:, base + 2 * HEAD : base + 3 * HEAD]
+            scores = contract(key_rows, query, 1, 1) * HEAD ** (-0.5)
+            scores = jnp.where(live, scores, -jnp.inf)
+            weights = jnp.exp(scores - jnp.max(scores, axis=0, keepdims=True))
+            total = jnp.sum(weights, axis=0, keepdims=True)
+            mixed = contract(value_rows, weights.astype(BF16), 0, 0)
+            out[head * HEAD : (head + 1) * HEAD, slot * 256 : (slot + 1) * 256] = (
+                mixed / total
+            ).astype(BF16)
+
+
+def fill_out_weight(where, pieces, weight):
+    here = lax.rem(where[0], 2) * 4 + where[1] * 2 + where[2]
+    block = D // 16
+    for code, piece in zip((0, 2, 1, 3), pieces):
+        for ez in (0, 1):
+            row = jnp.bitwise_xor(here, 4 * ez + code) * block
+            for part in (0, 1):
+                weight[part, pl.ds(pl.multiple_of(row, 16), block), :] = piece[ez, part]
+
+
+def merge_kernel(where, *refs):
+    parts = refs[:8]
+    residual, out_pieces, arrived = refs[8], refs[9:13], refs[13:17]
+    keep_out, send_out, heads, out_weight, weight = refs[17:]
+    here = where[1] * 2 + where[2]
+    fill_out_weight(where, out_pieces, out_weight)
+    for code in range(4):
+        for ey in (0, 1):
+            base = ey * (D // 2) + 2 * HEAD * jnp.bitwise_xor(here, code)
+            rows = pl.ds(pl.multiple_of(base, 16), 2 * HEAD)
+            for slot in range(4):
+                at = (slot ^ code) * 256
+                heads[slot, rows, :] = parts[2 * code + ey][:, at : at + 256]
+    for steps in range(4):
+        weight[z_behind(where[0], steps)] = arrived[steps][...]
+    sub_rows = [[], [], [], []]
+    for slot in range(4):
+        at = slice(slot * 256, (slot + 1) * 256)
+        branch = contract(out_weight[0], heads[slot, : D // 2, :], 1, 0) + contract(
+            out_weight[1], heads[slot, D // 2 :, :], 1, 0
+        )
+        after = (residual[:, at].astype(F32) + branch).astype(BF16)
+        for sub in range(4):
+            sub_rows[sub].append(after[:, sub * 64 : (sub + 1) * 64])
+    total = 0.0
+    for sub in range(4):
+        left = jnp.concatenate([weight[z, sub] for z in range(4)], axis=0)
+        total = total + contract(left, jnp.concatenate(sub_rows[sub], axis=1), 1, 0)
+    low, high = total[:, :128], total[:, 128:]
+
+    def by_core(value):
+        turned = jnp.concatenate([value[:, 64:], value[:, :64]], axis=1)
+        return jnp.where(where[2] == 0, value, turned)
+
+    keep_out[...] = by_core(jnp.where(where[3] == 0, low, high))
+    send_out[...] = by_core(jnp.where(where[3] == 0, high, low))
+
+
+def split_kernel(whole, out):
+    count = whole.shape[1] // 16
+    for at in range(16):
+        out[at] = whole[:, at * count : (at + 1) * count]
+
+
+def weight_kernel(where, own, other, gain, text_weight, token_weight, token_gain, rows):
+    block = D // 16
+    zeros = jnp.zeros((block, 128 - HEAD), BF16)
+    here = where[1] * 2 + where[2]
+    for at in range(16):
+        low = jnp.where(where[2] == 0, own[at].astype(F32), other[at].astype(F32))
+        high = jnp.where(where[2] == 0, other[at].astype(F32), own[at].astype(F32))
+        piece = jnp.concatenate([low, high], axis=1).astype(BF16)
+        padded = jnp.concatenate(
+            [part for k in range(3) for part in (piece[:, k * HEAD : (k + 1) * HEAD], zeros)],
+            axis=1,
+        )
+        text_weight[pl.ds(own_half_first(where, at), block), :] = padded
+        z = at // 4
+        code = jnp.bitwise_xor(here, at % 4)
+        rows[code, z * block : (z + 1) * block, :] = padded
+        column = jnp.broadcast_to(gain[:, at * block : (at + 1) * block], (128, block)).T
+        token_gain[code, z * block : (z + 1) * block, :] = column
+    for code in range(4):
+        token_weight[code] = rows[code].T
+
+
+def text_kernel(where, own, own_y, own_x, corner_low, corner_high, gain, weight, is_text, out):
+    own_gain = gain[pl.ds(where[3], 1), :]
+    other_gain = gain[pl.ds(1 - where[3], 1), :]
+    count = own.shape[1]
+    for steps in range(4):
+        corner = (corner_low, corner_high)[steps // 2][steps % 2]
+        for ex in (0, 1):
+            left = (own, own_x)[ex][steps].astype(F32)
+            right = (corner if ex else own_y[steps]).astype(F32)
+            squares = jnp.sum(left * left, axis=-1, keepdims=True) + jnp.sum(
+                right * right, axis=-1, keepdims=True
+            )
+            scale = lax.rsqrt(squares * (1.0 / D) + eps_norm)
+            left = (left * scale * own_gain).astype(BF16)
+            right = (right * scale * other_gain).astype(BF16)
+            proj = contract(left, weight[: D // 2, :], 1, 0) + contract(
+                right, weight[D // 2 :, :], 1, 0
+            )
+            row = (2 * z_behind(where[0], steps) + jnp.bitwise_xor(where[1], ex)) * count
+            at = pl.ds(pl.multiple_of(row, 16), count)
+            out[at, :] = jnp.where(is_text[at, :1] > 0.0, proj, 0.0).astype(BF16)
+
+
+def select_kernel(where, flat_pos, select, is_text):
+    positions = flat_pos[...]
+    block_rows = select.shape[0] // 8
+    for block in range(8):
+        first = (2 * block + where[2]) * block_rows
+        row = first + lax.broadcasted_iota(jnp.int32, (block_rows, positions.shape[1]), 0)
+        hit = jnp.where(row == positions, 1.0, 0.0)
+        at = slice(block * block_rows, (block + 1) * block_rows)
+        select[at, :] = hit.astype(BF16)
+        none = 1.0 - jnp.max(hit, axis=-1, keepdims=True)
+        is_text[at, :] = jnp.broadcast_to(none, (block_rows, 128))
+
+
+def token_columns(parts, sx):
+    blocks = []
+    for code, (ex, _) in enumerate(FOUR):
+        part = parts[2 * code + (sx ^ ex)]
+        blocks.append(jnp.concatenate([part[z] for z in range(4)], axis=1))
+    return blocks
+
+
+def place_kernel(*refs):
+    parts = refs[:8]
+    gain, weight, select, text_proj, query, key_out, value_out, proj = refs[8:]
+    for sx in (0, 1):
+        blocks = token_columns(parts, sx)
+        squares = sum(
+            jnp.sum(jnp.square(block.astype(F32)), axis=0, keepdims=True) for block in blocks
+        )
+        scale = lax.rsqrt(squares * (1.0 / D) + eps_norm)
+        total = 0.0
+        for at, block in enumerate(blocks):
+            normed = (block.astype(F32) * scale * gain[at][:, :1]).astype(BF16)
+            total = total + contract(weight[at], normed, 1, 0)
+        proj[:, sx * 512 : (sx + 1) * 512] = total.astype(BF16)
+    rows = contract(select[...], proj[...], 1, 1) + text_proj[...].astype(F32)
+    rows = rows.astype(BF16)
+    query[...] = rows[:, :128]
+    key_out[...] = rows[:, 128:256]
+    value_out[...] = rows[:, 256:]
+
+
+def route_kernel(where, *refs):
+    parts = refs[:8]
+    flat_pos, routed = refs[8:]
+    positions = flat_pos[...]
+    block_rows = routed.shape[1]
+    own_block = 4 * where[0] + 2 * where[1] + where[2]
+    row = own_block * block_rows + lax.broadcasted_iota(
+        jnp.int32, (block_rows, positions.shape[1]), 0
+    )
+    select = jnp.where(row == positions, 1.0, 0.0).astype(BF16)
+    low, high = token_columns(parts, 0), token_columns(parts, 1)
+    for at in range(4):
+        moved = contract(select[:, :512], low[at], 1, 1) + contract(
+            select[:, 512:], high[at], 1, 1
+        )
+        routed[at] = moved.astype(BF16)
+
+
+def decode_kernel(where, query, own_key, own_value, other_key, other_value, out):
+    rows = query.shape[0] // 8
+    later = where[2] > 0
+    for block in range(8):
+        count = (block + 1) * rows
+        asked = query[block * rows : count, :]
+        own = contract(asked, own_key[:count, :], 1, 1) * HEAD ** (-0.5)
+        other = contract(asked, other_key[:count, :], 1, 1) * HEAD ** (-0.5)
+        row = lax.broadcasted_iota(jnp.int32, (rows, count), 0) + block * rows
+        column = lax.broadcasted_iota(jnp.int32, (rows, count), 1)
+        own = jnp.where(column <= row, own, -jnp.inf)
+        limit = jnp.where(later, count, block * rows)
+        other = jnp.where(column < limit, other, -jnp.inf)
+        best = jnp.maximum(
+            jnp.max(own, axis=-1, keepdims=True), jnp.max(other, axis=-1, keepdims=True)
+        )
+        own = jnp.exp(own - best)
+        other = jnp.exp(other - best)
+        total = jnp.sum(own, axis=-1, keepdims=True) + jnp.sum(other, axis=-1, keepdims=True)
+        mixed = contract(own.astype(BF16), own_value[:count, :], 1, 0) + contract(
+            other.astype(BF16), other_value[:count, :], 1, 0
+        )
+        mixed = (mixed / total).astype(BF16)
+        for group in range(rows // 16):
+            piece = mixed[group * 16 : (group + 1) * 16, :HEAD]
+            for y in (0, 1):
+                out[2 * block + y, :, group * HEAD : (group + 1) * HEAD] = piece
+
+
+def finish_kernel(where, heads, own, at_x, at_c, at_xc, residual, out, weight, sorted_heads):
+    fill_out_weight(where, (own, at_x, at_c, at_xc), weight)
+    for at in range(16):
+        chip, y = at // 2, at % 2
+        half = jnp.bitwise_xor(where[3], y)
+        for group in range(out.shape[0] // 16):
+            sorted_heads[
+                half, group * 16 : (group + 1) * 16, chip * HEAD : (chip + 1) * HEAD
+            ] = heads[at, :, group * HEAD : (group + 1) * HEAD]
+    branch = contract(sorted_heads[0], weight[0], 1, 1) + contract(sorted_heads[1], weight[1], 1, 1)
+    out[...] = (residual[...].astype(F32) + branch).astype(BF16)
+
+
+def run(kernel, shapes, scratch, *operands, scalars=None, grant=GRANT):
+    specs = [pl.BlockSpec()] * len(operands)
+    if scalars is not None:
+        specs, operands = [SMEM] + specs, (scalars,) + operands
+    single = not isinstance(shapes, (list, tuple))
+    return pl.pallas_call(
+        kernel,
+        out_shape=shapes,
+        in_specs=specs,
+        out_specs=pl.BlockSpec() if single else [pl.BlockSpec()] * len(shapes),
+        scratch_shapes=scratch,
+        compiler_params=pltpu.CompilerParams(vmem_limit_bytes=grant),
+    )(*operands)
+
+
+OUT_Y = [(2 * w + 1 - w // 8, 2 * w + w // 8) for w in range(16)]
+OUT_FAR = [(2 * w + w // 8, 2 * (w ^ 8) + w // 8) for w in range(16)]
+OUT_NEAR = [(w, w ^ 4) for w in range(16)]
+
+
+def send_out_y(turned):
+    return lax.ppermute(turned, ("wide", "narrow"), OUT_Y)
+
+
+def send_out_far(both):
+    return lax.ppermute(both, ("wide", "narrow"), OUT_FAR)
+
+
+def send_out_near(held):
+    return lax.ppermute(held, "wide", OUT_NEAR)
+
+
+def out_over_y(turned):
+    return jnp.stack([turned, send_out_y(turned)])
+
+
+def out_over_far(both, z, y):
+    return jnp.where(z // 2 == y, both, send_out_far(both))
+
+
+def out_over_near(held):
+    return jnp.stack([held, send_out_near(held)])
+
+
+def fence(*values):
+    return lax.optimization_barrier(values)
+
+
+def shards_fast(
+    patches,
+    grid,
+    vit_gain,
+    vit_qkv,
+    vit_out,
+    merge_weight,
+    text_embeds,
+    prompt_pos,
+    dec_gain,
+    dec_qkv,
+    dec_out,
+):
+    w = lax.axis_index("wide").astype(jnp.int32)
+    y = lax.axis_index("narrow").astype(jnp.int32)
+    z, x, c = w // 4, (w // 2) % 2, w % 2
+    where = jnp.stack([z, x, c, y])
+    half = D // 2
+    text_rows = text_embeds.shape[0]
+
+    columns = vit_qkv.shape[1] // 4
+    sliced = vit_qkv.reshape(-1, 2, 2, columns).transpose(1, 2, 0, 3)
+    sliced = jnp.pad(sliced, ((0, 0), (0, 0), (0, 0), (0, 512 - columns)))
+
+    def halves(value, bit):
+        own = lax.dynamic_index_in_dim(value, bit, 0, keepdims=False)
+        return own, lax.dynamic_index_in_dim(value, 1 - bit, 0, keepdims=False)
+
+    own_cols, sent_cols = halves(sliced, x)
+    merge_first = merge_weight.transpose(0, 2, 1)
+    patch, sent_cols = fence(patches[0], sent_cols)
+    came_cols, patch_y, merge_second, out_held = fence(
+        over_x(sent_cols), over_y(patch), next_z(merge_first), out_over_y(vit_out.T)
+    )
+    own_cols, sent_cols = halves(jnp.stack([own_cols, came_cols], axis=-3), c)
+    patch, sent_cols = fence(patch, sent_cols)
+    sliced = jnp.stack([own_cols, over_c(sent_cols)], axis=-3).reshape(-1, 512)
+    second, patch_x, out_held = fence(
+        next_z(sliced), over_x(patch), out_over_far(out_held, z, y)
+    )
+    patch_xy = over_xy(patch)
+    third, patch_xy, out_held, text_first = fence(
+        next_z(second), patch_xy, out_over_near(out_held), text_embeds
+    )
+    patch_parts = [patch, patch_y, over_c(patch), over_c(patch_y), patch_x, patch_xy]
+    patch_parts += [over_c(patch_x), over_c(patch_xy)]
+    codes = jnp.arange(4, dtype=jnp.int32)
+    live = prompt_pos[4 * z + jnp.bitwise_xor(2 * x + c, codes)] >= 0
+    live = jnp.tile(live.astype(F32).T, (4, 1))
+    rows = 4 * patches.shape[1]
+    normed, residual = run(
+        norm_kernel,
+        [jax.ShapeDtypeStruct((rows, D), BF16), jax.ShapeDtypeStruct((half, rows), BF16)],
+        [],
+        *patch_parts,
+        vit_gain.reshape(2, half),
+        scalars=where,
+        grant=MOST,
+    )
+    fourth, normed, out_x, out_c, text_second, merge_second, live = fence(
+        next_z(third),
+        normed,
+        over_x(out_held),
+        over_c(out_held),
+        next_z(text_first),
+        merge_second,
+        live,
+    )
+    out_pieces = [out_held, out_x, out_c, over_c(out_x)]
+    vit_weight = [sliced, second, third, fourth]
+    merge_third = next_z(merge_second)
+    attended = run(
+        encode_kernel,
+        jax.ShapeDtypeStruct((2 * HEAD, rows), BF16),
+        [pltpu.VMEM((D, 512), BF16)],
+        normed,
+        *vit_weight,
+        live,
+        scalars=where,
+    )
+    attended, merge_third = fence(attended, merge_third)
+    merge_fourth = next_z(merge_third)
+    text_third = next_z(text_second)
+    att_y, att_x, att_xy, merge_fourth, text_fourth, dec_qkv, turned = fence(
+        over_y(attended),
+        over_x(attended),
+        over_xy(attended),
+        merge_fourth,
+        next_z(text_third),
+        dec_qkv,
+        dec_out.T,
+    )
+    head_parts = [attended, att_y, over_c(attended), over_c(att_y), att_x, att_xy]
+    head_parts += [over_c(att_x), over_c(att_xy)]
+    pieces = run(
+        split_kernel,
+        jax.ShapeDtypeStruct((16, dec_qkv.shape[0], dec_qkv.shape[1] // 16), BF16),
+        [],
+        dec_qkv,
+    )
+    pieces = lax.all_to_all(pieces, "wide", 0, 0, tiled=True)
+    merge_rows = [merge_first, merge_second, merge_third, merge_fourth]
+    part = jax.ShapeDtypeStruct((320, 128), F32)
+    kept, sent = run(
+        merge_kernel,
+        [part, part],
+        [
+            pltpu.VMEM((4, D, 256), BF16),
+            pltpu.VMEM((2, half, half), BF16),
+            pltpu.VMEM((4,) + merge_first.shape, BF16),
+        ],
+        *head_parts,
+        residual,
+        *out_pieces,
+        *merge_rows,
+        scalars=where,
+        grant=MOST,
+    )
+    stacked = jnp.stack([text_embeds, text_second, text_third, text_fourth])
+    kept, sent, pieces, dec_came, text_y, text_x = fence(
+        kept, sent, pieces, send_out_y(turned), over_y(stacked), over_x(stacked)
+    )
+    came = over_y(sent)
+    text_weight, token_weight, token_gain = run(
+        weight_kernel,
+        [
+            jax.ShapeDtypeStruct((D, 384), BF16),
+            jax.ShapeDtypeStruct((4, 384, D // 4), BF16),
+            jax.ShapeDtypeStruct((4, D // 4, 128), F32),
+        ],
+        [pltpu.VMEM((4, D // 4, 384), BF16)],
+        pieces,
+        over_c(pieces),
+        dec_gain[None],
+        scalars=where,
+    )
+    merged = (kept + came).astype(BF16)
+    merged, text_y, text_x = fence(merged, text_y, text_x)
+    sx = jnp.arange(2, dtype=jnp.int32)[:, None, None]
+    k = jnp.arange(4, dtype=jnp.int32)[None, :, None]
+    sc = jnp.arange(2, dtype=jnp.int32)[None, None, :]
+    image = 4 * ((z + 4 - k) % 4) + 2 * (sx ^ x ^ y) + sc
+    flat_pos = prompt_pos[image.reshape(-1)].reshape(1, -1)
+    select, is_text = run(
+        select_kernel,
+        [
+            jax.ShapeDtypeStruct((8 * text_rows, flat_pos.shape[1]), BF16),
+            jax.ShapeDtypeStruct((8 * text_rows, 128), F32),
+        ],
+        [],
+        flat_pos,
+        scalars=where,
+    )
+
+    def project_text(text_y, text_x, corner):
+        return run(
+            text_kernel,
+            jax.ShapeDtypeStruct((8 * text_rows, 384), BF16),
+            [],
+            stacked,
+            text_y,
+            text_x,
+            *corner,
+            dec_gain.reshape(2, half),
+            text_weight,
+            is_text,
+            scalars=where,
+        )
+
+    dec_both = jnp.stack([turned, dec_came])
+    *tokens, dec_came = fence(*around_z(merged), send_out_far(dec_both))
+    dec_held = jnp.where(z // 2 == y, dec_both, dec_came)
+    tokens = jnp.stack(tokens)
+    corner = [over_y(text_x[:2]), over_x(text_y[2:])]
+    text_proj = project_text(text_y, text_x, corner)
+    token_y, token_x, token_xy, text_proj, dec_came = fence(
+        over_y(tokens), over_x(tokens), over_xy(tokens), text_proj, send_out_near(dec_held)
+    )
+    dec_held = jnp.stack([dec_held, dec_came])
+    token_parts = [tokens, token_y, over_c(tokens), over_c(token_y)]
+    token_parts += [token_x, token_xy, over_c(token_x), over_c(token_xy)]
+
+    lanes = jax.ShapeDtypeStruct((8 * text_rows, 128), BF16)
+    query, key, value = run(
+        place_kernel,
+        [lanes, lanes, lanes],
+        [pltpu.VMEM((384, 1024), BF16)],
+        *token_parts,
+        token_gain,
+        token_weight,
+        select,
+        text_proj,
+    )
+    heads = run(
+        decode_kernel,
+        jax.ShapeDtypeStruct((16, 16, text_rows // 16 * HEAD), BF16),
+        [],
+        query,
+        key,
+        value,
+        over_c(key),
+        over_c(value),
+        scalars=where,
+    )
+    heads, dec_x, dec_c = fence(heads, over_x(dec_held), over_c(dec_held))
+    by_core = [[2 * w_ + y_ for w_ in range(c_, 16, 2) for y_ in (0, 1)] for c_ in (0, 1)]
+    heads = lax.all_to_all(
+        heads, ("wide", "narrow"), 0, 0, axis_index_groups=by_core, tiled=True
+    )
+    routed = run(
+        route_kernel,
+        jax.ShapeDtypeStruct((4, text_rows, 320), BF16),
+        [],
+        *token_parts,
+        flat_pos,
+        scalars=where,
+    )
+    routed = routed.reshape(4, text_rows, 4, D // 16)
+    routed = lax.dynamic_slice_in_dim(routed, 2 * y, 2, axis=2)
+    ordered = jnp.stack(
+        [
+            lax.dynamic_index_in_dim(routed, jnp.bitwise_xor(2 * x + c, code), 0, keepdims=False)
+            for code in range(4)
+        ]
+    )
+    ordered = ordered.transpose(1, 2, 0, 3).reshape(text_rows, half)
+    mine = w * text_rows + jnp.arange(text_rows, dtype=jnp.int32)
+    is_image = jnp.any(mine[:, None] == prompt_pos.reshape(1, -1), axis=1)
+    dec_in = jnp.where(is_image[:, None], ordered, text_embeds)
+    return run(
+        finish_kernel,
+        jax.ShapeDtypeStruct(text_embeds.shape, BF16),
+        [
+            pltpu.VMEM((2, half, half), BF16),
+            pltpu.VMEM((2, text_rows, half), BF16),
+        ],
+        heads,
+        dec_held,
+        dec_x,
+        dec_c,
+        over_c(dec_x),
+        dec_in,
+        scalars=where,
+    )
+
+
 def solution(mesh):
     placed = (
         P("wide", None, "narrow"),
@@ -210,6 +841,8 @@
         P("wide", "narrow"),
         P("narrow", "wide"),
     )
+    sizes = (mesh.shape["wide"], mesh.shape["narrow"])
+    shards = shards_fast if sizes == (16, 2) else shards_any
     return jax.shard_map(
         shards, mesh=mesh, in_specs=placed, out_specs=P("wide", "narrow"), check_vma=False
     )

time: 489 us -> 210 us (0.43)
  waiting for transfers between devices: 371 us -> 58 us
  starting transfers between devices: 0.59 us -> 80.5 us
  Pallas kernels: 0 us -> 44.5 us
  matrix products: 24.8 us -> 0 us
  local copies, waits for them, and re-layouts: 42.1 us -> 17.6 us
  blocking collectives: 19.5 us -> 0 us
  between operations: 13.5 us -> 0.78 us
  loops' own time: 5.3 us -> 0 us
    all_gather x8 -> x0, waiting for transfers between devices: 321 us -> none  [the longest x1 64.1 us: shards(): piece = lax.all_gather(merge_weight, 'wide', axis=2, tiled=True)]
    ppermute x0 -> x55, starting transfers between devices: none -> 70.5 us  [the longest x9 21.4 us: next_z(): return lax.ppermute(value, 'wide', RING_Z)]
    ppermute x0 -> x55, waiting for transfers between devices: none -> 49.2 us  [the longest x9 14.6 us: next_z(): return lax.ppermute(value, 'wide', RING_Z)]
    pallas_call x0 -> x11, Pallas kernels: none -> 44.5 us  [run(): pl.pallas_call(kernel, out_shape=shapes, in_specs=specs, out_specs=pl.Blo...]
    reduce_scatter x2 -> x0, waiting for transfers between devices: 32.2 us -> none  [the longest x1 21.2 us: shards(): lax.psum_scatter(vit_partial, 'narrow', scatter_dimension=1, tiled=True)]
    dot_general x12 -> x0, matrix products: 24.8 us -> none  [the longest x2 7.54 us: add_rows(): return jnp.dot(left, piece, preferred_element_type=jnp.float32)]
    all_gather x3 -> x0, local copies, waits for them, and re-layouts: 23.8 us -> none  [the longest x1 12.4 us: shards(): piece = lax.all_gather(merge_weight, 'wide', axis=2, tiled=True)]
    all_gather x2 -> x0, blocking collectives: 19.5 us -> none  [the longest x1 11.6 us: shards(): whole = lax.all_gather(patches, 'narrow', axis=2, tiled=True)]
  transfers between devices with their start and end apart: 11 -> 57, of which waited for: 11 -> 18; matrix products, arithmetic and copies ran while one was open for 9% -> 8% of each run, Pallas kernels for 0% -> 20%
where the time goes in v2:
time: 210 us; the launch traced here: 209 us
  starting transfers between devices  80.5 us (38%)
  waiting for transfers between devices  58 us (28%)
  Pallas kernels  44.5 us (21%)
  local copies, waits for them, and re-layouts  17.6 us (8%)
  other arithmetic  7.89 us (4%)
    pallas_call x11, Pallas kernels, run(): pl.pallas_call(kernel, out_shape=shapes, in_specs=specs, out_specs=pl.Blo...  44.5 us
    ppermute x9, starting transfers between devices, next_z(): return lax.ppermute(value, 'wide', RING_Z)  21.4 us
    ppermute x9, waiting for transfers between devices, next_z(): return lax.ppermute(value, 'wide', RING_Z)  14.6 us
    ppermute x6, starting transfers between devices, over_y(): return lax.ppermute(value, 'narrow', CROSS_Y)  10.4 us
    unnamed x82, local copies, waits for them, and re-layouts  9.1 us
    ppermute x2, waiting for transfers between devices, send_out_y(): return lax.ppermute(turned, ('wide', 'narrow'), OUT_Y)  8.4 us
    ppermute x8, starting transfers between devices, over_x(): return lax.ppermute(value, 'wide', CROSS_X)  8.25 us
    ppermute x2, starting transfers between devices, send_out_near(): return lax.ppermute(held, 'wide', OUT_NEAR)  7.99 us
  transfers between devices with their start and end apart: 57, of which 18 were waited for; matrix products, arithmetic and copies ran while one was open for 8% of the time, Pallas kernels for 20%

profile of v2, /device:TPU:0, one launch (start us, length us, event | category | flops | bytes accessed | tf_op | source)
XLA Modules:
  0.0 209.2 jit_solution(10519278987627585727)
XLA Ops:
  0.0 3.0 %collective-permute-start.2 = (bf16[4,80,640]{2,1,0:T(8,128)(2,1)}, bf16[4,80,640]{2,1,0:T(8,128)(2,1)S(1)}, u32[]{:S(2)}, u32[]{:S(2)}) collective-permute-start(bf16[4,80,640]{2,1,0:T(8,128)(2,1)} %bitcast.63), channel_id=1, source_target_pairs={{0,8},{2,10},{4,12},{6,14},{8,24},{10,26},{12,28},{14,30},{24,16},... | collective-permute-start | bytes 1228808 | tf_op jit(solution)/shard_map/ppermute | solution.py:230
  9.3 7.2 %collective-permute-done.3 = bf16[80,640]{1,0:T(8,128)(2,1)S(1)} collective-permute-done((bf16[80,640]{1,0:T(8,128)(2,1)}, bf16[80,640]{1,0:T(8,128)(2,1)S(1)}, u32[]{:S(2)}, u32[]{:S(2)}) %collective-permute-start.3) | collective-permute-done | bytes 102432 | tf_op jit(solution)/shard_map/ppermute | solution.py:557
  25.4 4.8 %collective-permute-done.6.refs_4_ = bf16[256,640]{1,0:T(8,128)(2,1)} collective-permute-done((bf16[256,640]{1,0:T(8,128)(2,1)}, bf16[256,640]{1,0:T(8,128)(2,1)}, u32[]{:S(2)}, u32[]{:S(2)}) %collective-permute-start.6) | collective-permute-done | bytes 327712 | tf_op jit(solution)/shard_map/ppermute | solution.py:215
  32.1 5.8 %collective-permute-start.10 = (bf16[2,80,640]{2,1,0:T(8,128)(2,1)S(1)}, bf16[2,80,640]{2,1,0:T(8,128)(2,1)S(1)}, u32[]{:S(2)}, u32[]{:S(2)}) collective-permute-start(bf16[2,80,640]{2,1,0:T(8,128)(2,1)S(1)} %broadcast_select_fusion.2), channel_id=1, source_target_pairs={{0,8},{2,10},{4,12},{6,14},{8,0},{10,2},{12,4},{14,6},{16,24},{18,... | collective-permute-start | bytes 614408 | tf_op jit(solution)/shard_map/ppermute | solution.py:565
  42.4 7.8 %collective-permute-done.10 = bf16[2,80,640]{2,1,0:T(8,128)(2,1)S(1)} collective-permute-done((bf16[2,80,640]{2,1,0:T(8,128)(2,1)S(1)}, bf16[2,80,640]{2,1,0:T(8,128)(2,1)S(1)}, u32[]{:S(2)}, u32[]{:S(2)}) %collective-permute-start.10) | collective-permute-done | bytes 204832 | tf_op jit(solution)/shard_map/ppermute | solution.py:565
  54.6 3.6 %collective-permute-start.18 = (bf16[160,640]{1,0:T(8,128)(2,1)S(1)}, bf16[160,640]{1,0:T(8,128)(2,1)}, u32[]{:S(2)}, u32[]{:S(2)}) collective-permute-start(bf16[160,640]{1,0:T(8,128)(2,1)S(1)} %copy-done.23), channel_id=1, source_target_pairs={{0,8},{2,10},{4,12},{6,14},{8,24},{10,26},{12,28},{14,30},{24,16},... | collective-permute-start | bytes 614408 | tf_op jit(solution)/shard_map/ppermute | solution.py:230
  59.5 6.2 %shard_map.100 = (bf16[1024,1280]{1,0:T(8,128)(2,1)}, bf16[640,1024]{1,0:T(8,128)(2,1)}) custom-call(s32[4]{0:T(128)} %pad_add_fusion.where, bf16[256,640]{1,0:T(8,128)(2,1)} %bitcast.6.refs_0_, bf16[256,640]{1,0:T(8,128)(2,1)} %collective-permute-done.1.refs_1_, bf16[256,640]{1,0:T(8,128)(2,1)} %copy-done.36, ...), custom_call_target="tpu_custom_call" | custom-call | tf_op jit(solution)/shard_map/pallas_call | solution.py:541
  65.6 3.0 %collective-permute-done.18 = bf16[160,640]{1,0:T(8,128)(2,1)} collective-permute-done((bf16[160,640]{1,0:T(8,128)(2,1)S(1)}, bf16[160,640]{1,0:T(8,128)(2,1)}, u32[]{:S(2)}, u32[]{:S(2)}) %collective-permute-start.18) | collective-permute-done | bytes 204832 | tf_op jit(solution)/shard_map/ppermute | solution.py:230
  70.0 3.5 %collective-permute-start.24 = (bf16[160,640]{1,0:T(8,128)(2,1)}, bf16[160,640]{1,0:T(8,128)(2,1)S(1)}, u32[]{:S(2)}, u32[]{:S(2)}) collective-permute-start(bf16[160,640]{1,0:T(8,128)(2,1)} %collective-permute-done.18), channel_id=1, source_target_pairs={{0,8},{2,10},{4,12},{6,14},{8,24},{10,26},{12,28},{14,30},{24,16},... | collective-permute-start | bytes 614408 | tf_op jit(solution)/shard_map/ppermute | solution.py:230
  75.2 5.0 %shard_map.101.refs_0_ = bf16[160,1024]{1,0:T(8,128)(2,1)S(1)} custom-call(s32[4]{0:T(128)S(1)} %copy-done.15, bf16[1024,1280]{1,0:T(8,128)(2,1)S(1)} %copy-done.1, bf16[320,512]{1,0:T(8,128)(2,1)S(1)} %bitcast.50, bf16[320,512]{1,0:T(8,128)(2,1)S(1)} %collective-permute-done.5.second, bf16[320,512]{1,0:T(8,128)(2,1)S(1)} %collective-permute-done.8.third, ...), custom_call_target="tpu_custom_call" | custom-call | tf_op jit(solution)/shard_map/pallas_call | solution.py:541
  86.9 3.4 %collective-permute-start.25 = (bf16[160,640]{1,0:T(8,128)(2,1)S(1)}, bf16[160,640]{1,0:T(8,128)(2,1)S(1)}, u32[]{:S(2)}, u32[]{:S(2)}) collective-permute-start(bf16[160,640]{1,0:T(8,128)(2,1)S(1)} %collective-permute-done.24), channel_id=1, source_target_pairs={{0,8},{2,10},{4,12},{6,14},{8,24},{10,26},{12,28},{14,30},{24,16},... | collective-permute-start | bytes 614408 | tf_op jit(solution)/shard_map/ppermute | solution.py:230
  90.2 7.9 %collective-permute-done.25 = bf16[160,640]{1,0:T(8,128)(2,1)S(1)} collective-permute-done((bf16[160,640]{1,0:T(8,128)(2,1)S(1)}, bf16[160,640]{1,0:T(8,128)(2,1)S(1)}, u32[]{:S(2)}, u32[]{:S(2)}) %collective-permute-start.25) | collective-permute-done | bytes 204832 | tf_op jit(solution)/shard_map/ppermute | solution.py:230
  104.2 4.5 %all-to-all-start = ((bf16[16,80,120]{2,1,0:T(8,128)(2,1)}), bf16[16,80,120]{2,1,0:T(8,128)(2,1)}, u32[]{:S(2)}, u32[]{:S(2)}) async-start(bf16[16,80,120]{2,1,0:T(8,128)(2,1)} %shard_map.103), calls=%async_computation | async-start | bytes 655360 | tf_op jit(solution)/shard_map/all_to_all | solution.py:684
  111.9 7.9 %shard_map.102 = (f32[320,128]{1,0:T(8,128)}, f32[320,128]{1,0:T(8,128)}) custom-call(s32[4]{0:T(128)} %pad_add_fusion.where, bf16[160,1024]{1,0:T(8,128)(2,1)} %copy-done.2, bf16[160,1024]{1,0:T(8,128)(2,1)} %copy-done.31, bf16[160,1024]{1,0:T(8,128)(2,1)} %collective-permute-done.26.refs_2_, bf16[160,1024]{1,0:T(8,128)(2,1)} %copy-done.34, ...), custom_call_target="tpu_custom_call" | custom-call | tf_op jit(solution)/shard_map/pallas_call | solution.py:541
  124.2 3.9 %collective-permute-start.38 = (bf16[2,80,640]{2,1,0:T(8,128)(2,1)S(1)}, bf16[2,80,640]{2,1,0:T(8,128)(2,1)S(1)}, u32[]{:S(2)}, u32[]{:S(2)}) collective-permute-start(bf16[2,80,640]{2,1,0:T(8,128)(2,1)S(1)} %pad_maximum_fusion.6), channel_id=1, source_target_pairs={{0,16},{2,18},{4,20},{6,22},{8,24},{10,26},{12,28},{14,30},{17,1},... | collective-permute-start | bytes 614408 | tf_op jit(solution)/shard_map/ppermute | solution.py:561
  131.5 2.7 %collective-permute-start.36 = (bf16[320,128]{1,0:T(8,128)(2,1)S(1)}, bf16[320,128]{1,0:T(8,128)(2,1)S(1)}, u32[]{:S(2)}, u32[]{:S(2)}) collective-permute-start(bf16[320,128]{1,0:T(8,128)(2,1)S(1)} %add_convert_fusion), channel_id=1, source_target_pairs={{0,16},{2,18},{4,20},{6,22},{8,24},{10,26},{12,28},{14,30},{16,0},... | collective-permute-start | bytes 245768 | tf_op jit(solution)/shard_map/ppermute | solution.py:240
  140.3 4.8 %collective-permute-start.39 = (bf16[4,320,128]{2,1,0:T(8,128)(2,1)S(1)}, bf16[4,320,128]{2,1,0:T(8,128)(2,1)S(1)}, u32[]{:S(2)}, u32[]{:S(2)}) collective-permute-start(bf16[4,320,128]{2,1,0:T(8,128)(2,1)S(1)} %pad_maximum_fusion.4.refs_0_), channel_id=1, source_target_pairs={{0,1},{1,0},{2,3},{3,2},{4,5},{5,4},{6,7},{7,6},{8,9},{9,8},{10,11... | collective-permute-start | bytes 983048 | tf_op jit(solution)/shard_map/ppermute | solution.py:223
  155.8 2.8 %shard_map.104 = (bf16[1280,384]{1,0:T(8,128)(2,1)S(1)}, bf16[4,384,320]{2,1,0:T(8,128)(2,1)S(1)}, f32[4,320,128]{2,1,0:T(8,128)S(1)}) custom-call(s32[4]{0:T(128)S(1)} %copy-done.16, bf16[16,80,120]{2,1,0:T(8,128)(2,1)} %all-to-all-done.own, bf16[16,80,120]{2,1,0:T(8,128)(2,1)S(1)} %copy-done.13, f32[1,1280]{1,0:T(1,128)S(1)} %broadcast_in_dim.7.gain), custom_call_target="tpu_custom_call" | custom-call | tf_op jit(solution)/shard_map/pallas_call | solution.py:541
  158.7 4.1 %shard_map.106.refs_11_ = bf16[1280,384]{1,0:T(8,128)(2,1)S(1)} custom-call(s32[4]{0:T(128)S(1)} %copy-done.16, bf16[4,160,640]{2,1,0:T(8,128)(2,1)S(1)} %pad_maximum_fusion.own, bf16[4,160,640]{2,1,0:T(8,128)(2,1)S(1)} %collective-permute-done.32.own_y, bf16[4,160,640]{2,1,0:T(8,128)(2,1)S(1)} %collective-permute-done.33.own_x, ...), custom_call_target="tpu_custom_call" | custom-call | tf_op jit(solution)/shard_map/pallas_call | solution.py:541
  162.9 5.7 %collective-permute-done.41.refs_5_ = bf16[4,320,128]{2,1,0:T(8,128)(2,1)} collective-permute-done((bf16[4,320,128]{2,1,0:T(8,128)(2,1)S(1)}, bf16[4,320,128]{2,1,0:T(8,128)(2,1)}, u32[]{:S(2)}, u32[]{:S(2)}) %collective-permute-start.41) | collective-permute-done | bytes 327712 | tf_op jit(solution)/shard_map/ppermute | solution.py:246
  171.5 5.9 %shard_map.107 = (bf16[1280,128]{1,0:T(8,128)(2,1)S(1)}, bf16[1280,128]{1,0:T(8,128)(2,1)S(1)}, bf16[1280,128]{1,0:T(8,128)(2,1)S(1)}) custom-call(bf16[4,320,128]{2,1,0:T(8,128)(2,1)S(1)} %pad_maximum_fusion.4.refs_0_, bf16[4,320,128]{2,1,0:T(8,128)(2,1)S(1)} %collective-permute-done.39.refs_1_, bf16[4,320,128]{2,1,0:T(8,128)(2,1)S(1)} %collective-permute-done.46.refs_2_, ...), custom_call_target="tpu_custom_call" | custom-call | tf_op jit(solution)/shard_map/pallas_call | solution.py:541
  179.5 6.0 %shard_map.108 = bf16[16,16,800]{2,1,0:T(8,128)(2,1)} custom-call(s32[4]{0:T(128)S(1)} %copy-done.16, bf16[1280,128]{1,0:T(8,128)(2,1)S(1)} %get-tuple-element.128.query, bf16[1280,128]{1,0:T(8,128)(2,1)S(1)} %get-tuple-element.129.own_key, bf16[1280,128]{1,0:T(8,128)(2,1)S(1)} %get-tuple-element.130.own_value, ...), custom_call_target="tpu_custom_call" | custom-call | tf_op jit(solution)/shard_map/pallas_call | solution.py:541
  187.1 5.4 %all-to-all-start.1 = ((bf16[16,16,800]{2,1,0:T(8,128)(2,1)}), bf16[16,16,800]{2,1,0:T(8,128)(2,1)S(1)}, u32[]{:S(2)}, u32[]{:S(2)}) async-start(bf16[16,16,800]{2,1,0:T(8,128)(2,1)} %shard_map.108), calls=%async_computation.1 | async-start | bytes 917504 | tf_op jit(solution)/shard_map/all_to_all | solution.py:790
  200.8 6.1 %all-to-all-done.1.heads = bf16[16,16,800]{2,1,0:T(8,128)(2,1)S(1)} async-done(((bf16[16,16,800]{2,1,0:T(8,128)(2,1)}), bf16[16,16,800]{2,1,0:T(8,128)(2,1)S(1)}, u32[]{:S(2)}, u32[]{:S(2)}) %all-to-all-start.1) | async-done | bytes 409632 | tf_op jit(solution)/shard_map/all_to_all | solution.py:790
  (228 shorter events, 87.4 us)
Async XLA Ops:
  0.0 17.4 %collective-permute-start.2 = (bf16[4,80,640]{2,1,0:T(8,128)(2,1)}, bf16[4,80,640]{2,1,0:T(8,128)(2,1)S(1)}, u32[]{:S(2)}, u32[]{:S(2)}) collective-permute-start(bf16[4,80,640]{2,1,0:T(8,128)(2,1)} %bitcast.63), channel_id=1, source_target_pairs={{0,8},{2,10},{4,12},{6,14},{8,24},{10,26},{12,28},{14,30},{24,16},... | collective-permute-start | bytes 1228808 | tf_op jit(solution)/shard_map/ppermute | solution.py:230
  32.1 18.1 %collective-permute-start.10 = (bf16[2,80,640]{2,1,0:T(8,128)(2,1)S(1)}, bf16[2,80,640]{2,1,0:T(8,128)(2,1)S(1)}, u32[]{:S(2)}, u32[]{:S(2)}) collective-permute-start(bf16[2,80,640]{2,1,0:T(8,128)(2,1)S(1)} %broadcast_select_fusion.2), channel_id=1, source_target_pairs={{0,8},{2,10},{4,12},{6,14},{8,0},{10,2},{12,4},{14,6},{16,24},{18,... | collective-permute-start | bytes 614408 | tf_op jit(solution)/shard_map/ppermute | solution.py:565
  50.3 18.4 %collective-permute-start.16 = (bf16[2,2,80,640]{3,2,1,0:T(8,128)(2,1)S(1)}, bf16[2,2,80,640]{3,2,1,0:T(8,128)(2,1)S(1)}, u32[]{:S(2)}, u32[]{:S(2)}) collective-permute-start(bf16[2,2,80,640]{3,2,1,0:T(8,128)(2,1)S(1)} %pad_maximum_fusion.1.refs_9_), channel_id=1, source_target_pairs={{0,4},{2,6},{4,0},{6,2},{8,12},{10,14},{12,8},{14,10},{16,20},{18,... | collective-permute-start | bytes 1228808 | tf_op jit(solution)/shard_map/ppermute | solution.py:215
  51.8 16.8 %collective-permute-start.17 = (bf16[2,2,80,640]{3,2,1,0:T(8,128)(2,1)S(1)}, bf16[2,2,80,640]{3,2,1,0:T(8,128)(2,1)}, u32[]{:S(2)}, u32[]{:S(2)}) collective-permute-start(bf16[2,2,80,640]{3,2,1,0:T(8,128)(2,1)S(1)} %pad_maximum_fusion.1.refs_9_), channel_id=1, source_target_pairs={{0,2},{2,0},{4,6},{6,4},{8,10},{10,8},{12,14},{14,12},{16,18},{18,... | collective-permute-start | bytes 1228808 | tf_op jit(solution)/shard_map/ppermute | solution.py:219
  53.0 15.7 %collective-permute-start.11 = (bf16[320,512]{1,0:T(8,128)(2,1)S(1)}, bf16[320,512]{1,0:T(8,128)(2,1)S(1)}, u32[]{:S(2)}, u32[]{:S(2)}) collective-permute-start(bf16[320,512]{1,0:T(8,128)(2,1)S(1)} %collective-permute-done.8.third), channel_id=1, source_target_pairs={{0,8},{2,10},{4,12},{6,14},{8,24},{10,26},{12,28},{14,30},{24,16},... | collective-permute-start | bytes 983048 | tf_op jit(solution)/shard_map/ppermute | solution.py:230
  54.6 14.1 %collective-permute-start.18 = (bf16[160,640]{1,0:T(8,128)(2,1)S(1)}, bf16[160,640]{1,0:T(8,128)(2,1)}, u32[]{:S(2)}, u32[]{:S(2)}) collective-permute-start(bf16[160,640]{1,0:T(8,128)(2,1)S(1)} %copy-done.23), channel_id=1, source_target_pairs={{0,8},{2,10},{4,12},{6,14},{8,24},{10,26},{12,28},{14,30},{24,16},... | collective-permute-start | bytes 614408 | tf_op jit(solution)/shard_map/ppermute | solution.py:230
  68.7 13.3 %collective-permute-start.19 = (bf16[4,80,640]{2,1,0:T(8,128)(2,1)S(1)}, bf16[4,80,640]{2,1,0:T(8,128)(2,1)S(1)}, u32[]{:S(2)}, u32[]{:S(2)}) collective-permute-start(bf16[4,80,640]{2,1,0:T(8,128)(2,1)S(1)} %collective-permute-done.2.refs_14_), channel_id=1, source_target_pairs={{0,8},{2,10},{4,12},{6,14},{8,24},{10,26},{12,28},{14,30},{24,16},... | collective-permute-start | bytes 1228808 | tf_op jit(solution)/shard_map/ppermute | solution.py:230
  70.0 16.9 %collective-permute-start.24 = (bf16[160,640]{1,0:T(8,128)(2,1)}, bf16[160,640]{1,0:T(8,128)(2,1)S(1)}, u32[]{:S(2)}, u32[]{:S(2)}) collective-permute-start(bf16[160,640]{1,0:T(8,128)(2,1)} %collective-permute-done.18), channel_id=1, source_target_pairs={{0,8},{2,10},{4,12},{6,14},{8,24},{10,26},{12,28},{14,30},{24,16},... | collective-permute-start | bytes 614408 | tf_op jit(solution)/shard_map/ppermute | solution.py:230
  82.0 16.1 %collective-permute-start.23 = (bf16[4,80,640]{2,1,0:T(8,128)(2,1)S(1)}, bf16[4,80,640]{2,1,0:T(8,128)(2,1)S(1)}, u32[]{:S(2)}, u32[]{:S(2)}) collective-permute-start(bf16[4,80,640]{2,1,0:T(8,128)(2,1)S(1)} %collective-permute-done.19.refs_15_), channel_id=1, source_target_pairs={{0,8},{2,10},{4,12},{6,14},{8,24},{10,26},{12,28},{14,30},{24,16},... | collective-permute-start | bytes 1228808 | tf_op jit(solution)/shard_map/ppermute | solution.py:230
  83.4 14.8 %collective-permute-start.20 = (bf16[160,1024]{1,0:T(8,128)(2,1)S(1)}, bf16[160,1024]{1,0:T(8,128)(2,1)S(1)}, u32[]{:S(2)}, u32[]{:S(2)}) collective-permute-start(bf16[160,1024]{1,0:T(8,128)(2,1)S(1)} %shard_map.101.refs_0_), channel_id=1, source_target_pairs={{0,1},{1,0},{2,3},{3,2},{4,5},{5,4},{6,7},{7,6},{8,9},{9,8},{10,11... | collective-permute-start | bytes 983048 | tf_op jit(solution)/shard_map/ppermute | solution.py:223
  84.1 14.1 %collective-permute-start.21 = (bf16[160,1024]{1,0:T(8,128)(2,1)S(1)}, bf16[160,1024]{1,0:T(8,128)(2,1)S(1)}, u32[]{:S(2)}, u32[]{:S(2)}) collective-permute-start(bf16[160,1024]{1,0:T(8,128)(2,1)S(1)} %shard_map.101.refs_0_), channel_id=1, source_target_pairs={{0,4},{2,6},{4,0},{6,2},{8,12},{10,14},{12,8},{14,10},{16,20},{18,... | collective-permute-start | bytes 983048 | tf_op jit(solution)/shard_map/ppermute | solution.py:215
  84.6 13.5 %collective-permute-start.22 = (bf16[160,1024]{1,0:T(8,128)(2,1)S(1)}, bf16[160,1024]{1,0:T(8,128)(2,1)S(1)}, u32[]{:S(2)}, u32[]{:S(2)}) collective-permute-start(bf16[160,1024]{1,0:T(8,128)(2,1)S(1)} %shard_map.101.refs_0_), channel_id=1, source_target_pairs={{0,5},{1,4},{2,7},{3,6},{4,1},{5,0},{6,3},{7,2},{8,13},{9,12},{10,... | collective-permute-start | bytes 983048 | tf_op jit(solution)/shard_map/ppermute | solution.py:246
  100.2 23.5 %collective-permute-start.32 = (bf16[4,160,640]{2,1,0:T(8,128)(2,1)S(1)}, bf16[4,160,640]{2,1,0:T(8,128)(2,1)S(1)}, u32[]{:S(2)}, u32[]{:S(2)}) collective-permute-start(bf16[4,160,640]{2,1,0:T(8,128)(2,1)S(1)} %pad_maximum_fusion.own), channel_id=1, source_target_pairs={{0,1},{1,0},{2,3},{3,2},{4,5},{5,4},{6,7},{7,6},{8,9},{9,8},{10,11... | collective-permute-start | bytes 2457608 | tf_op jit(solution)/shard_map/ppermute | solution.py:223
  102.1 21.6 %collective-permute-start.33 = (bf16[4,160,640]{2,1,0:T(8,128)(2,1)S(1)}, bf16[4,160,640]{2,1,0:T(8,128)(2,1)S(1)}, u32[]{:S(2)}, u32[]{:S(2)}) collective-permute-start(bf16[4,160,640]{2,1,0:T(8,128)(2,1)S(1)} %pad_maximum_fusion.own), channel_id=1, source_target_pairs={{0,4},{2,6},{4,0},{6,2},{8,12},{10,14},{12,8},{14,10},{16,20},{18,... | collective-permute-start | bytes 2457608 | tf_op jit(solution)/shard_map/ppermute | solution.py:215
  104.2 19.6 %all-to-all-start = ((bf16[16,80,120]{2,1,0:T(8,128)(2,1)}), bf16[16,80,120]{2,1,0:T(8,128)(2,1)}, u32[]{:S(2)}, u32[]{:S(2)}) async-start(bf16[16,80,120]{2,1,0:T(8,128)(2,1)} %shard_map.103), calls=%async_computation | async-start | bytes 655360 | tf_op jit(solution)/shard_map/all_to_all | solution.py:684
  124.2 14.0 %collective-permute-start.38 = (bf16[2,80,640]{2,1,0:T(8,128)(2,1)S(1)}, bf16[2,80,640]{2,1,0:T(8,128)(2,1)S(1)}, u32[]{:S(2)}, u32[]{:S(2)}) collective-permute-start(bf16[2,80,640]{2,1,0:T(8,128)(2,1)S(1)} %pad_maximum_fusion.6), channel_id=1, source_target_pairs={{0,16},{2,18},{4,20},{6,22},{8,24},{10,26},{12,28},{14,30},{17,1},... | collective-permute-start | bytes 614408 | tf_op jit(solution)/shard_map/ppermute | solution.py:561
  138.4 20.2 %collective-permute-start.43 = (bf16[2,160,640]{2,1,0:T(8,128)(2,1)}, bf16[2,160,640]{2,1,0:T(8,128)(2,1)}, u32[]{:S(2)}, u32[]{:S(2)}) collective-permute-start(bf16[2,160,640]{2,1,0:T(8,128)(2,1)} %slice.7), channel_id=1, source_target_pairs={{0,4},{2,6},{4,0},{6,2},{8,12},{10,14},{12,8},{14,10},{16,20},{18,... | collective-permute-start | bytes 1228808 | tf_op jit(solution)/shard_map/ppermute | solution.py:215
  140.3 22.5 %collective-permute-start.39 = (bf16[4,320,128]{2,1,0:T(8,128)(2,1)S(1)}, bf16[4,320,128]{2,1,0:T(8,128)(2,1)S(1)}, u32[]{:S(2)}, u32[]{:S(2)}) collective-permute-start(bf16[4,320,128]{2,1,0:T(8,128)(2,1)S(1)} %pad_maximum_fusion.4.refs_0_), channel_id=1, source_target_pairs={{0,1},{1,0},{2,3},{3,2},{4,5},{5,4},{6,7},{7,6},{8,9},{9,8},{10,11... | collective-permute-start | bytes 983048 | tf_op jit(solution)/shard_map/ppermute | solution.py:223
  145.2 17.7 %collective-permute-start.40 = (bf16[4,320,128]{2,1,0:T(8,128)(2,1)S(1)}, bf16[4,320,128]{2,1,0:T(8,128)(2,1)S(1)}, u32[]{:S(2)}, u32[]{:S(2)}) collective-permute-start(bf16[4,320,128]{2,1,0:T(8,128)(2,1)S(1)} %pad_maximum_fusion.4.refs_0_), channel_id=1, source_target_pairs={{0,4},{2,6},{4,0},{6,2},{8,12},{10,14},{12,8},{14,10},{16,20},{18,... | collective-permute-start | bytes 983048 | tf_op jit(solution)/shard_map/ppermute | solution.py:215
  148.3 20.3 %collective-permute-start.41 = (bf16[4,320,128]{2,1,0:T(8,128)(2,1)S(1)}, bf16[4,320,128]{2,1,0:T(8,128)(2,1)}, u32[]{:S(2)}, u32[]{:S(2)}) collective-permute-start(bf16[4,320,128]{2,1,0:T(8,128)(2,1)S(1)} %pad_maximum_fusion.4.refs_0_), channel_id=1, source_target_pairs={{0,5},{1,4},{2,7},{3,6},{4,1},{5,0},{6,3},{7,2},{8,13},{9,12},{10,... | collective-permute-start | bytes 983048 | tf_op jit(solution)/shard_map/ppermute | solution.py:246
  149.2 13.7 %collective-permute-start.45 = (bf16[2,80,640]{2,1,0:T(8,128)(2,1)}, bf16[2,80,640]{2,1,0:T(8,128)(2,1)}, u32[]{:S(2)}, u32[]{:S(2)}) collective-permute-start(bf16[2,80,640]{2,1,0:T(8,128)(2,1)} %broadcast_select_fusion.1), channel_id=1, source_target_pairs={{0,8},{2,10},{4,12},{6,14},{8,0},{10,2},{12,4},{14,6},{16,24},{18,... | collective-permute-start | bytes 614408 | tf_op jit(solution)/shard_map/ppermute | solution.py:565
  170.1 15.5 %collective-permute-start.52 = (bf16[2,2,80,640]{3,2,1,0:T(8,128)(2,1)S(1)}, bf16[2,2,80,640]{3,2,1,0:T(8,128)(2,1)S(1)}, u32[]{:S(2)}, u32[]{:S(2)}) collective-permute-start(bf16[2,2,80,640]{3,2,1,0:T(8,128)(2,1)S(1)} %pad_maximum_fusion.2.own), channel_id=1, source_target_pairs={{0,4},{2,6},{4,0},{6,2},{8,12},{10,14},{12,8},{14,10},{16,20},{18,... | collective-permute-start | bytes 1228808 | tf_op jit(solution)/shard_map/ppermute | solution.py:215
  171.2 15.1 %collective-permute-start.53 = (bf16[2,2,80,640]{3,2,1,0:T(8,128)(2,1)S(1)}, bf16[2,2,80,640]{3,2,1,0:T(8,128)(2,1)S(1)}, u32[]{:S(2)}, u32[]{:S(2)}) collective-permute-start(bf16[2,2,80,640]{3,2,1,0:T(8,128)(2,1)S(1)} %pad_maximum_fusion.2.own), channel_id=1, source_target_pairs={{0,2},{2,0},{4,6},{6,4},{8,10},{10,8},{12,14},{14,12},{16,18},{18,... | collective-permute-start | bytes 1228808 | tf_op jit(solution)/shard_map/ppermute | solution.py:219
  187.1 19.8 %all-to-all-start.1 = ((bf16[16,16,800]{2,1,0:T(8,128)(2,1)}), bf16[16,16,800]{2,1,0:T(8,128)(2,1)S(1)}, u32[]{:S(2)}, u32[]{:S(2)}) async-start(bf16[16,16,800]{2,1,0:T(8,128)(2,1)} %shard_map.108), calls=%async_computation.1 | async-start | bytes 917504 | tf_op jit(solution)/shard_map/all_to_all | solution.py:790
  (72 other events, 834.0 us)

commit v3 on v2

--- a/solution.py
+++ b/solution.py
@@ -664,23 +664,24 @@
     attended, merge_third = fence(attended, merge_third)
     merge_fourth = next_z(merge_third)
     text_third = next_z(text_second)
-    att_y, att_x, att_xy, merge_fourth, text_fourth, dec_qkv, turned = fence(
+    pieces = run(
+        split_kernel,
+        jax.ShapeDtypeStruct((16, dec_qkv.shape[0], dec_qkv.shape[1] // 16), BF16),
+        [],
+        dec_qkv,
+    )
+    turned = dec_out.T
+    att_y, att_x, att_xy, merge_fourth, text_fourth, pieces, dec_came = fence(
         over_y(attended),
         over_x(attended),
         over_xy(attended),
         merge_fourth,
         next_z(text_third),
-        dec_qkv,
-        dec_out.T,
+        pieces,
+        send_out_y(turned),
     )
     head_parts = [attended, att_y, over_c(attended), over_c(att_y), att_x, att_xy]
     head_parts += [over_c(att_x), over_c(att_xy)]
-    pieces = run(
-        split_kernel,
-        jax.ShapeDtypeStruct((16, dec_qkv.shape[0], dec_qkv.shape[1] // 16), BF16),
-        [],
-        dec_qkv,
-    )
     pieces = lax.all_to_all(pieces, "wide", 0, 0, tiled=True)
     merge_rows = [merge_first, merge_second, merge_third, merge_fourth]
     part = jax.ShapeDtypeStruct((320, 128), F32)
@@ -700,8 +701,8 @@
         grant=MOST,
     )
     stacked = jnp.stack([text_embeds, text_second, text_third, text_fourth])
-    kept, sent, pieces, dec_came, text_y, text_x = fence(
-        kept, sent, pieces, send_out_y(turned), over_y(stacked), over_x(stacked)
+    kept, sent, pieces, text_y, text_x = fence(
+        kept, sent, pieces, over_y(stacked), over_x(stacked)
     )
     came = over_y(sent)
     text_weight, token_weight, token_gain = run(

time: 210 us -> 209 us (level)
    ppermute x9, waiting for transfers between devices: 14.6 us -> 12.1 us  [next_z(): return lax.ppermute(value, 'wide', RING_Z)]
  transfers between devices with their start and end apart: 57 -> 57, of which waited for: 18 -> 20; matrix products, arithmetic and copies ran while one was open for 8% -> 8% of each run, Pallas kernels for 20% -> 20%
where the time goes in v3:
time: 209 us; the launch traced here: 208 us
  starting transfers between devices  81.4 us (39%)
  waiting for transfers between devices  57.1 us (27%)
  Pallas kernels  44.6 us (21%)
  local copies, waits for them, and re-layouts  17.5 us (8%)
  other arithmetic  6.96 us (3%)
    pallas_call x11, Pallas kernels, run(): pl.pallas_call(kernel, out_shape=shapes, in_specs=specs, out_specs=pl.Blo...  44.6 us
    ppermute x9, starting transfers between devices, next_z(): return lax.ppermute(value, 'wide', RING_Z)  21.4 us
    ppermute x9, waiting for transfers between devices, next_z(): return lax.ppermute(value, 'wide', RING_Z)  12.1 us
    ppermute x6, starting transfers between devices, over_y(): return lax.ppermute(value, 'narrow', CROSS_Y)  10.5 us
    unnamed x82, local copies, waits for them, and re-layouts  9.02 us
    ppermute x2, starting transfers between devices, send_out_near(): return lax.ppermute(held, 'wide', OUT_NEAR)  8.2 us
    ppermute x2, waiting for transfers between devices, send_out_near(): return lax.ppermute(held, 'wide', OUT_NEAR)  7.79 us
    ppermute x2, waiting for transfers between devices, send_out_y(): return lax.ppermute(turned, ('wide', 'narrow'), OUT_Y)  7.18 us
  transfers between devices with their start and end apart: 57, of which 20 were waited for; matrix products, arithmetic and copies ran while one was open for 8% of the time, Pallas kernels for 20%

profile of v3, /device:TPU:0, one launch (start us, length us, event | category | flops | bytes accessed | tf_op | source)
XLA Modules:
  0.0 208.3 jit_solution(18377269887989553001)
XLA Ops:
  0.0 3.0 %collective-permute-start.2 = (bf16[4,80,640]{2,1,0:T(8,128)(2,1)}, bf16[4,80,640]{2,1,0:T(8,128)(2,1)S(1)}, u32[]{:S(2)}, u32[]{:S(2)}) collective-permute-start(bf16[4,80,640]{2,1,0:T(8,128)(2,1)} %bitcast.64), channel_id=1, source_target_pairs={{0,8},{2,10},{4,12},{6,14},{8,24},{10,26},{12,28},{14,30},{24,16},... | collective-permute-start | bytes 1228808 | tf_op jit(solution)/shard_map/ppermute | solution.py:230
  9.3 7.2 %collective-permute-done.3 = bf16[80,640]{1,0:T(8,128)(2,1)S(1)} collective-permute-done((bf16[80,640]{1,0:T(8,128)(2,1)}, bf16[80,640]{1,0:T(8,128)(2,1)S(1)}, u32[]{:S(2)}, u32[]{:S(2)}) %collective-permute-start.3) | collective-permute-done | bytes 102432 | tf_op jit(solution)/shard_map/ppermute | solution.py:557
  25.6 4.6 %collective-permute-done.6.refs_4_ = bf16[256,640]{1,0:T(8,128)(2,1)} collective-permute-done((bf16[256,640]{1,0:T(8,128)(2,1)}, bf16[256,640]{1,0:T(8,128)(2,1)}, u32[]{:S(2)}, u32[]{:S(2)}) %collective-permute-start.6) | collective-permute-done | bytes 327712 | tf_op jit(solution)/shard_map/ppermute | solution.py:215
  32.1 5.8 %collective-permute-start.10 = (bf16[2,80,640]{2,1,0:T(8,128)(2,1)S(1)}, bf16[2,80,640]{2,1,0:T(8,128)(2,1)S(1)}, u32[]{:S(2)}, u32[]{:S(2)}) collective-permute-start(bf16[2,80,640]{2,1,0:T(8,128)(2,1)S(1)} %broadcast_select_fusion.2), channel_id=1, source_target_pairs={{0,8},{2,10},{4,12},{6,14},{8,0},{10,2},{12,4},{14,6},{16,24},{18,... | collective-permute-start | bytes 614408 | tf_op jit(solution)/shard_map/ppermute | solution.py:565
  42.4 7.8 %collective-permute-done.10 = bf16[2,80,640]{2,1,0:T(8,128)(2,1)S(1)} collective-permute-done((bf16[2,80,640]{2,1,0:T(8,128)(2,1)S(1)}, bf16[2,80,640]{2,1,0:T(8,128)(2,1)S(1)}, u32[]{:S(2)}, u32[]{:S(2)}) %collective-permute-start.10) | collective-permute-done | bytes 204832 | tf_op jit(solution)/shard_map/ppermute | solution.py:565
  54.6 3.6 %collective-permute-start.18 = (bf16[160,640]{1,0:T(8,128)(2,1)S(1)}, bf16[160,640]{1,0:T(8,128)(2,1)S(1)}, u32[]{:S(2)}, u32[]{:S(2)}) collective-permute-start(bf16[160,640]{1,0:T(8,128)(2,1)S(1)} %copy-done.25), channel_id=1, source_target_pairs={{0,8},{2,10},{4,12},{6,14},{8,24},{10,26},{12,28},{14,30},{24,16},... | collective-permute-start | bytes 614408 | tf_op jit(solution)/shard_map/ppermute | solution.py:230
  59.5 6.2 %shard_map.100 = (bf16[1024,1280]{1,0:T(8,128)(2,1)}, bf16[640,1024]{1,0:T(8,128)(2,1)}) custom-call(s32[4]{0:T(128)} %pad_add_fusion.where, bf16[256,640]{1,0:T(8,128)(2,1)} %bitcast.6.refs_0_, bf16[256,640]{1,0:T(8,128)(2,1)} %collective-permute-done.1.refs_1_, bf16[256,640]{1,0:T(8,128)(2,1)} %copy-done.36, ...), custom_call_target="tpu_custom_call" | custom-call | tf_op jit(solution)/shard_map/pallas_call | solution.py:541
  65.7 2.8 %collective-permute-done.18 = bf16[160,640]{1,0:T(8,128)(2,1)S(1)} collective-permute-done((bf16[160,640]{1,0:T(8,128)(2,1)S(1)}, bf16[160,640]{1,0:T(8,128)(2,1)S(1)}, u32[]{:S(2)}, u32[]{:S(2)}) %collective-permute-start.18) | collective-permute-done | bytes 204832 | tf_op jit(solution)/shard_map/ppermute | solution.py:230
  71.2 3.4 %collective-permute-start.24 = (bf16[160,640]{1,0:T(8,128)(2,1)S(1)}, bf16[160,640]{1,0:T(8,128)(2,1)S(1)}, u32[]{:S(2)}, u32[]{:S(2)}) collective-permute-start(bf16[160,640]{1,0:T(8,128)(2,1)S(1)} %collective-permute-done.18), channel_id=1, source_target_pairs={{0,8},{2,10},{4,12},{6,14},{8,24},{10,26},{12,28},{14,30},{24,16},... | collective-permute-start | bytes 614408 | tf_op jit(solution)/shard_map/ppermute | solution.py:230
  76.4 5.0 %shard_map.101.refs_0_ = bf16[160,1024]{1,0:T(8,128)(2,1)S(1)} custom-call(s32[4]{0:T(128)S(1)} %copy-done.15, bf16[1024,1280]{1,0:T(8,128)(2,1)S(1)} %copy-done.1, bf16[320,512]{1,0:T(8,128)(2,1)S(1)} %bitcast.51, bf16[320,512]{1,0:T(8,128)(2,1)S(1)} %collective-permute-done.5.second, bf16[320,512]{1,0:T(8,128)(2,1)S(1)} %collective-permute-done.8.third, ...), custom_call_target="tpu_custom_call" | custom-call | tf_op jit(solution)/shard_map/pallas_call | solution.py:541
  86.8 3.4 %collective-permute-start.25 = (bf16[160,640]{1,0:T(8,128)(2,1)S(1)}, bf16[160,640]{1,0:T(8,128)(2,1)S(1)}, u32[]{:S(2)}, u32[]{:S(2)}) collective-permute-start(bf16[160,640]{1,0:T(8,128)(2,1)S(1)} %collective-permute-done.24), channel_id=1, source_target_pairs={{0,8},{2,10},{4,12},{6,14},{8,24},{10,26},{12,28},{14,30},{24,16},... | collective-permute-start | bytes 614408 | tf_op jit(solution)/shard_map/ppermute | solution.py:230
  91.1 6.9 %collective-permute-done.25 = bf16[160,640]{1,0:T(8,128)(2,1)S(1)} collective-permute-done((bf16[160,640]{1,0:T(8,128)(2,1)S(1)}, bf16[160,640]{1,0:T(8,128)(2,1)S(1)}, u32[]{:S(2)}, u32[]{:S(2)}) %collective-permute-start.25) | collective-permute-done | bytes 204832 | tf_op jit(solution)/shard_map/ppermute | solution.py:230
  102.8 4.9 %all-to-all-start = ((bf16[16,80,120]{2,1,0:T(8,128)(2,1)}), bf16[16,80,120]{2,1,0:T(8,128)(2,1)}, u32[]{:S(2)}, u32[]{:S(2)}) async-start(bf16[16,80,120]{2,1,0:T(8,128)(2,1)} %shard_map.102), calls=%async_computation | async-start | bytes 655360 | tf_op jit(solution)/shard_map/all_to_all | solution.py:685
  110.7 8.0 %shard_map.103 = (f32[320,128]{1,0:T(8,128)}, f32[320,128]{1,0:T(8,128)}) custom-call(s32[4]{0:T(128)} %pad_add_fusion.where, bf16[160,1024]{1,0:T(8,128)(2,1)} %copy-done.2, bf16[160,1024]{1,0:T(8,128)(2,1)} %copy-done.32, bf16[160,1024]{1,0:T(8,128)(2,1)} %collective-permute-done.27.refs_2_, bf16[160,1024]{1,0:T(8,128)(2,1)} %collective-permute-done.28.refs_3_, ...), custom_call_target="tpu_custom_call" | custom-call | tf_op jit(solution)/shard_map/pallas_call | solution.py:541
  118.7 3.7 %all-to-all-done.own = bf16[16,80,120]{2,1,0:T(8,128)(2,1)} async-done(((bf16[16,80,120]{2,1,0:T(8,128)(2,1)}), bf16[16,80,120]{2,1,0:T(8,128)(2,1)}, u32[]{:S(2)}, u32[]{:S(2)}) %all-to-all-start) | async-done | bytes 307232 | tf_op jit(solution)/shard_map/all_to_all | solution.py:685
  123.1 4.1 %collective-permute-start.38 = (bf16[2,80,640]{2,1,0:T(8,128)(2,1)S(1)}, bf16[2,80,640]{2,1,0:T(8,128)(2,1)S(1)}, u32[]{:S(2)}, u32[]{:S(2)}) collective-permute-start(bf16[2,80,640]{2,1,0:T(8,128)(2,1)S(1)} %pad_maximum_fusion.6), channel_id=1, source_target_pairs={{0,16},{2,18},{4,20},{6,22},{8,24},{10,26},{12,28},{14,30},{17,1},... | collective-permute-start | bytes 614408 | tf_op jit(solution)/shard_map/ppermute | solution.py:561
  139.1 5.0 %collective-permute-start.39 = (bf16[4,320,128]{2,1,0:T(8,128)(2,1)S(1)}, bf16[4,320,128]{2,1,0:T(8,128)(2,1)S(1)}, u32[]{:S(2)}, u32[]{:S(2)}) collective-permute-start(bf16[4,320,128]{2,1,0:T(8,128)(2,1)S(1)} %pad_maximum_fusion.4.refs_0_), channel_id=1, source_target_pairs={{0,1},{1,0},{2,3},{3,2},{4,5},{5,4},{6,7},{7,6},{8,9},{9,8},{10,11... | collective-permute-start | bytes 983048 | tf_op jit(solution)/shard_map/ppermute | solution.py:223
  154.9 2.8 %shard_map.104 = (bf16[1280,384]{1,0:T(8,128)(2,1)S(1)}, bf16[4,384,320]{2,1,0:T(8,128)(2,1)S(1)}, f32[4,320,128]{2,1,0:T(8,128)S(1)}) custom-call(s32[4]{0:T(128)S(1)} %copy-done.16, bf16[16,80,120]{2,1,0:T(8,128)(2,1)} %all-to-all-done.own, bf16[16,80,120]{2,1,0:T(8,128)(2,1)S(1)} %copy-done.13, f32[1,1280]{1,0:T(1,128)S(1)} %broadcast_in_dim.7.gain), custom_call_target="tpu_custom_call" | custom-call | tf_op jit(solution)/shard_map/pallas_call | solution.py:541
  157.8 4.1 %shard_map.106.refs_11_ = bf16[1280,384]{1,0:T(8,128)(2,1)S(1)} custom-call(s32[4]{0:T(128)S(1)} %copy-done.16, bf16[4,160,640]{2,1,0:T(8,128)(2,1)S(1)} %pad_maximum_fusion.own, bf16[4,160,640]{2,1,0:T(8,128)(2,1)S(1)} %collective-permute-done.32.own_y, bf16[4,160,640]{2,1,0:T(8,128)(2,1)S(1)} %collective-permute-done.33.own_x, ...), custom_call_target="tpu_custom_call" | custom-call | tf_op jit(solution)/shard_map/pallas_call | solution.py:541
  162.0 5.4 %collective-permute-done.41.refs_5_ = bf16[4,320,128]{2,1,0:T(8,128)(2,1)} collective-permute-done((bf16[4,320,128]{2,1,0:T(8,128)(2,1)S(1)}, bf16[4,320,128]{2,1,0:T(8,128)(2,1)}, u32[]{:S(2)}, u32[]{:S(2)}) %collective-permute-start.41) | collective-permute-done | bytes 327712 | tf_op jit(solution)/shard_map/ppermute | solution.py:246
  170.2 5.9 %shard_map.107 = (bf16[1280,128]{1,0:T(8,128)(2,1)S(1)}, bf16[1280,128]{1,0:T(8,128)(2,1)S(1)}, bf16[1280,128]{1,0:T(8,128)(2,1)S(1)}) custom-call(bf16[4,320,128]{2,1,0:T(8,128)(2,1)S(1)} %pad_maximum_fusion.4.refs_0_, bf16[4,320,128]{2,1,0:T(8,128)(2,1)S(1)} %collective-permute-done.39.refs_1_, bf16[4,320,128]{2,1,0:T(8,128)(2,1)S(1)} %collective-permute-done.46.refs_2_, ...), custom_call_target="tpu_custom_call" | custom-call | tf_op jit(solution)/shard_map/pallas_call | solution.py:541
  178.3 6.0 %shard_map.108 = bf16[16,16,800]{2,1,0:T(8,128)(2,1)} custom-call(s32[4]{0:T(128)S(1)} %copy-done.16, bf16[1280,128]{1,0:T(8,128)(2,1)S(1)} %get-tuple-element.126.query, bf16[1280,128]{1,0:T(8,128)(2,1)S(1)} %get-tuple-element.127.own_key, bf16[1280,128]{1,0:T(8,128)(2,1)S(1)} %get-tuple-element.128.own_value, ...), custom_call_target="tpu_custom_call" | custom-call | tf_op jit(solution)/shard_map/pallas_call | solution.py:541
  185.8 5.8 %all-to-all-start.1 = ((bf16[16,16,800]{2,1,0:T(8,128)(2,1)}), bf16[16,16,800]{2,1,0:T(8,128)(2,1)S(1)}, u32[]{:S(2)}, u32[]{:S(2)}) async-start(bf16[16,16,800]{2,1,0:T(8,128)(2,1)} %shard_map.108), calls=%async_computation.1 | async-start | bytes 917504 | tf_op jit(solution)/shard_map/all_to_all | solution.py:791
  199.9 6.1 %all-to-all-done.1.heads = bf16[16,16,800]{2,1,0:T(8,128)(2,1)S(1)} async-done(((bf16[16,16,800]{2,1,0:T(8,128)(2,1)}), bf16[16,16,800]{2,1,0:T(8,128)(2,1)S(1)}, u32[]{:S(2)}, u32[]{:S(2)}) %all-to-all-start.1) | async-done | bytes 409632 | tf_op jit(solution)/shard_map/all_to_all | solution.py:791
  (228 shorter events, 86.0 us)
Async XLA Ops:
  0.0 17.4 %collective-permute-start.2 = (bf16[4,80,640]{2,1,0:T(8,128)(2,1)}, bf16[4,80,640]{2,1,0:T(8,128)(2,1)S(1)}, u32[]{:S(2)}, u32[]{:S(2)}) collective-permute-start(bf16[4,80,640]{2,1,0:T(8,128)(2,1)} %bitcast.64), channel_id=1, source_target_pairs={{0,8},{2,10},{4,12},{6,14},{8,24},{10,26},{12,28},{14,30},{24,16},... | collective-permute-start | bytes 1228808 | tf_op jit(solution)/shard_map/ppermute | solution.py:230
  32.1 18.1 %collective-permute-start.10 = (bf16[2,80,640]{2,1,0:T(8,128)(2,1)S(1)}, bf16[2,80,640]{2,1,0:T(8,128)(2,1)S(1)}, u32[]{:S(2)}, u32[]{:S(2)}) collective-permute-start(bf16[2,80,640]{2,1,0:T(8,128)(2,1)S(1)} %broadcast_select_fusion.2), channel_id=1, source_target_pairs={{0,8},{2,10},{4,12},{6,14},{8,0},{10,2},{12,4},{14,6},{16,24},{18,... | collective-permute-start | bytes 614408 | tf_op jit(solution)/shard_map/ppermute | solution.py:565
  50.3 18.3 %collective-permute-start.16 = (bf16[2,2,80,640]{3,2,1,0:T(8,128)(2,1)S(1)}, bf16[2,2,80,640]{3,2,1,0:T(8,128)(2,1)}, u32[]{:S(2)}, u32[]{:S(2)}) collective-permute-start(bf16[2,2,80,640]{3,2,1,0:T(8,128)(2,1)S(1)} %pad_maximum_fusion.1.refs_9_), channel_id=1, source_target_pairs={{0,4},{2,6},{4,0},{6,2},{8,12},{10,14},{12,8},{14,10},{16,20},{18,... | collective-permute-start | bytes 1228808 | tf_op jit(solution)/shard_map/ppermute | solution.py:215
  51.8 16.7 %collective-permute-start.17 = (bf16[2,2,80,640]{3,2,1,0:T(8,128)(2,1)S(1)}, bf16[2,2,80,640]{3,2,1,0:T(8,128)(2,1)}, u32[]{:S(2)}, u32[]{:S(2)}) collective-permute-start(bf16[2,2,80,640]{3,2,1,0:T(8,128)(2,1)S(1)} %pad_maximum_fusion.1.refs_9_), channel_id=1, source_target_pairs={{0,2},{2,0},{4,6},{6,4},{8,10},{10,8},{12,14},{14,12},{16,18},{18,... | collective-permute-start | bytes 1228808 | tf_op jit(solution)/shard_map/ppermute | solution.py:219
  53.0 15.5 %collective-permute-start.11 = (bf16[320,512]{1,0:T(8,128)(2,1)S(1)}, bf16[320,512]{1,0:T(8,128)(2,1)S(1)}, u32[]{:S(2)}, u32[]{:S(2)}) collective-permute-start(bf16[320,512]{1,0:T(8,128)(2,1)S(1)} %collective-permute-done.8.third), channel_id=1, source_target_pairs={{0,8},{2,10},{4,12},{6,14},{8,24},{10,26},{12,28},{14,30},{24,16},... | collective-permute-start | bytes 983048 | tf_op jit(solution)/shard_map/ppermute | solution.py:230
  54.6 14.0 %collective-permute-start.18 = (bf16[160,640]{1,0:T(8,128)(2,1)S(1)}, bf16[160,640]{1,0:T(8,128)(2,1)S(1)}, u32[]{:S(2)}, u32[]{:S(2)}) collective-permute-start(bf16[160,640]{1,0:T(8,128)(2,1)S(1)} %copy-done.25), channel_id=1, source_target_pairs={{0,8},{2,10},{4,12},{6,14},{8,24},{10,26},{12,28},{14,30},{24,16},... | collective-permute-start | bytes 614408 | tf_op jit(solution)/shard_map/ppermute | solution.py:230
  70.0 14.8 %collective-permute-start.26 = (bf16[80,640]{1,0:T(8,128)(2,1)S(1)}, bf16[80,640]{1,0:T(8,128)(2,1)S(1)}, u32[]{:S(2)}, u32[]{:S(2)}) collective-permute-start(bf16[80,640]{1,0:T(8,128)(2,1)S(1)} %bitcast.55), channel_id=1, source_target_pairs={{1,0},{3,2},{5,4},{7,6},{9,8},{11,10},{13,12},{15,14},{16,17},{18,... | collective-permute-start | bytes 307208 | tf_op jit(solution)/shard_map/ppermute | solution.py:557
  71.2 15.5 %collective-permute-start.24 = (bf16[160,640]{1,0:T(8,128)(2,1)S(1)}, bf16[160,640]{1,0:T(8,128)(2,1)S(1)}, u32[]{:S(2)}, u32[]{:S(2)}) collective-permute-start(bf16[160,640]{1,0:T(8,128)(2,1)S(1)} %collective-permute-done.18), channel_id=1, source_target_pairs={{0,8},{2,10},{4,12},{6,14},{8,24},{10,26},{12,28},{14,30},{24,16},... | collective-permute-start | bytes 614408 | tf_op jit(solution)/shard_map/ppermute | solution.py:230
  81.9 17.1 %collective-permute-start.23 = (bf16[4,80,640]{2,1,0:T(8,128)(2,1)S(1)}, bf16[4,80,640]{2,1,0:T(8,128)(2,1)S(1)}, u32[]{:S(2)}, u32[]{:S(2)}) collective-permute-start(bf16[4,80,640]{2,1,0:T(8,128)(2,1)S(1)} %collective-permute-done.19.refs_15_), channel_id=1, source_target_pairs={{0,8},{2,10},{4,12},{6,14},{8,24},{10,26},{12,28},{14,30},{24,16},... | collective-permute-start | bytes 1228808 | tf_op jit(solution)/shard_map/ppermute | solution.py:230
  83.3 14.8 %collective-permute-start.20 = (bf16[160,1024]{1,0:T(8,128)(2,1)S(1)}, bf16[160,1024]{1,0:T(8,128)(2,1)S(1)}, u32[]{:S(2)}, u32[]{:S(2)}) collective-permute-start(bf16[160,1024]{1,0:T(8,128)(2,1)S(1)} %shard_map.101.refs_0_), channel_id=1, source_target_pairs={{0,1},{1,0},{2,3},{3,2},{4,5},{5,4},{6,7},{7,6},{8,9},{9,8},{10,11... | collective-permute-start | bytes 983048 | tf_op jit(solution)/shard_map/ppermute | solution.py:223
  84.3 13.8 %collective-permute-start.21 = (bf16[160,1024]{1,0:T(8,128)(2,1)S(1)}, bf16[160,1024]{1,0:T(8,128)(2,1)S(1)}, u32[]{:S(2)}, u32[]{:S(2)}) collective-permute-start(bf16[160,1024]{1,0:T(8,128)(2,1)S(1)} %shard_map.101.refs_0_), channel_id=1, source_target_pairs={{0,4},{2,6},{4,0},{6,2},{8,12},{10,14},{12,8},{14,10},{16,20},{18,... | collective-permute-start | bytes 983048 | tf_op jit(solution)/shard_map/ppermute | solution.py:215
  84.8 14.2 %collective-permute-start.22 = (bf16[160,1024]{1,0:T(8,128)(2,1)S(1)}, bf16[160,1024]{1,0:T(8,128)(2,1)S(1)}, u32[]{:S(2)}, u32[]{:S(2)}) collective-permute-start(bf16[160,1024]{1,0:T(8,128)(2,1)S(1)} %shard_map.101.refs_0_), channel_id=1, source_target_pairs={{0,5},{1,4},{2,7},{3,6},{4,1},{5,0},{6,3},{7,2},{8,13},{9,12},{10,... | collective-permute-start | bytes 983048 | tf_op jit(solution)/shard_map/ppermute | solution.py:246
  100.0 22.4 %collective-permute-start.32 = (bf16[4,160,640]{2,1,0:T(8,128)(2,1)S(1)}, bf16[4,160,640]{2,1,0:T(8,128)(2,1)S(1)}, u32[]{:S(2)}, u32[]{:S(2)}) collective-permute-start(bf16[4,160,640]{2,1,0:T(8,128)(2,1)S(1)} %pad_maximum_fusion.own), channel_id=1, source_target_pairs={{0,1},{1,0},{2,3},{3,2},{4,5},{5,4},{6,7},{7,6},{8,9},{9,8},{10,11... | collective-permute-start | bytes 2457608 | tf_op jit(solution)/shard_map/ppermute | solution.py:223
  101.7 20.6 %collective-permute-start.33 = (bf16[4,160,640]{2,1,0:T(8,128)(2,1)S(1)}, bf16[4,160,640]{2,1,0:T(8,128)(2,1)S(1)}, u32[]{:S(2)}, u32[]{:S(2)}) collective-permute-start(bf16[4,160,640]{2,1,0:T(8,128)(2,1)S(1)} %pad_maximum_fusion.own), channel_id=1, source_target_pairs={{0,4},{2,6},{4,0},{6,2},{8,12},{10,14},{12,8},{14,10},{16,20},{18,... | collective-permute-start | bytes 2457608 | tf_op jit(solution)/shard_map/ppermute | solution.py:215
  102.8 19.6 %all-to-all-start = ((bf16[16,80,120]{2,1,0:T(8,128)(2,1)}), bf16[16,80,120]{2,1,0:T(8,128)(2,1)}, u32[]{:S(2)}, u32[]{:S(2)}) async-start(bf16[16,80,120]{2,1,0:T(8,128)(2,1)} %shard_map.102), calls=%async_computation | async-start | bytes 655360 | tf_op jit(solution)/shard_map/all_to_all | solution.py:685
  123.1 14.2 %collective-permute-start.38 = (bf16[2,80,640]{2,1,0:T(8,128)(2,1)S(1)}, bf16[2,80,640]{2,1,0:T(8,128)(2,1)S(1)}, u32[]{:S(2)}, u32[]{:S(2)}) collective-permute-start(bf16[2,80,640]{2,1,0:T(8,128)(2,1)S(1)} %pad_maximum_fusion.6), channel_id=1, source_target_pairs={{0,16},{2,18},{4,20},{6,22},{8,24},{10,26},{12,28},{14,30},{17,1},... | collective-permute-start | bytes 614408 | tf_op jit(solution)/shard_map/ppermute | solution.py:561
  137.3 20.3 %collective-permute-start.43 = (bf16[2,160,640]{2,1,0:T(8,128)(2,1)}, bf16[2,160,640]{2,1,0:T(8,128)(2,1)}, u32[]{:S(2)}, u32[]{:S(2)}) collective-permute-start(bf16[2,160,640]{2,1,0:T(8,128)(2,1)} %slice.7), channel_id=1, source_target_pairs={{0,4},{2,6},{4,0},{6,2},{8,12},{10,14},{12,8},{14,10},{16,20},{18,... | collective-permute-start | bytes 1228808 | tf_op jit(solution)/shard_map/ppermute | solution.py:215
  139.1 22.9 %collective-permute-start.39 = (bf16[4,320,128]{2,1,0:T(8,128)(2,1)S(1)}, bf16[4,320,128]{2,1,0:T(8,128)(2,1)S(1)}, u32[]{:S(2)}, u32[]{:S(2)}) collective-permute-start(bf16[4,320,128]{2,1,0:T(8,128)(2,1)S(1)} %pad_maximum_fusion.4.refs_0_), channel_id=1, source_target_pairs={{0,1},{1,0},{2,3},{3,2},{4,5},{5,4},{6,7},{7,6},{8,9},{9,8},{10,11... | collective-permute-start | bytes 983048 | tf_op jit(solution)/shard_map/ppermute | solution.py:223
  144.0 17.9 %collective-permute-start.40 = (bf16[4,320,128]{2,1,0:T(8,128)(2,1)S(1)}, bf16[4,320,128]{2,1,0:T(8,128)(2,1)S(1)}, u32[]{:S(2)}, u32[]{:S(2)}) collective-permute-start(bf16[4,320,128]{2,1,0:T(8,128)(2,1)S(1)} %pad_maximum_fusion.4.refs_0_), channel_id=1, source_target_pairs={{0,4},{2,6},{4,0},{6,2},{8,12},{10,14},{12,8},{14,10},{16,20},{18,... | collective-permute-start | bytes 983048 | tf_op jit(solution)/shard_map/ppermute | solution.py:215
  146.9 20.5 %collective-permute-start.41 = (bf16[4,320,128]{2,1,0:T(8,128)(2,1)S(1)}, bf16[4,320,128]{2,1,0:T(8,128)(2,1)}, u32[]{:S(2)}, u32[]{:S(2)}) collective-permute-start(bf16[4,320,128]{2,1,0:T(8,128)(2,1)S(1)} %pad_maximum_fusion.4.refs_0_), channel_id=1, source_target_pairs={{0,5},{1,4},{2,7},{3,6},{4,1},{5,0},{6,3},{7,2},{8,13},{9,12},{10,... | collective-permute-start | bytes 983048 | tf_op jit(solution)/shard_map/ppermute | solution.py:246
  148.1 13.9 %collective-permute-start.45 = (bf16[2,80,640]{2,1,0:T(8,128)(2,1)}, bf16[2,80,640]{2,1,0:T(8,128)(2,1)}, u32[]{:S(2)}, u32[]{:S(2)}) collective-permute-start(bf16[2,80,640]{2,1,0:T(8,128)(2,1)} %broadcast_select_fusion.1), channel_id=1, source_target_pairs={{0,8},{2,10},{4,12},{6,14},{8,0},{10,2},{12,4},{14,6},{16,24},{18,... | collective-permute-start | bytes 614408 | tf_op jit(solution)/shard_map/ppermute | solution.py:565
  169.0 15.3 %collective-permute-start.52 = (bf16[2,2,80,640]{3,2,1,0:T(8,128)(2,1)S(1)}, bf16[2,2,80,640]{3,2,1,0:T(8,128)(2,1)S(1)}, u32[]{:S(2)}, u32[]{:S(2)}) collective-permute-start(bf16[2,2,80,640]{3,2,1,0:T(8,128)(2,1)S(1)} %pad_maximum_fusion.2.own), channel_id=1, source_target_pairs={{0,4},{2,6},{4,0},{6,2},{8,12},{10,14},{12,8},{14,10},{16,20},{18,... | collective-permute-start | bytes 1228808 | tf_op jit(solution)/shard_map/ppermute | solution.py:215
  169.3 15.8 %collective-permute-start.53 = (bf16[2,2,80,640]{3,2,1,0:T(8,128)(2,1)S(1)}, bf16[2,2,80,640]{3,2,1,0:T(8,128)(2,1)S(1)}, u32[]{:S(2)}, u32[]{:S(2)}) collective-permute-start(bf16[2,2,80,640]{3,2,1,0:T(8,128)(2,1)S(1)} %pad_maximum_fusion.2.own), channel_id=1, source_target_pairs={{0,2},{2,0},{4,6},{6,4},{8,10},{10,8},{12,14},{14,12},{16,18},{18,... | collective-permute-start | bytes 1228808 | tf_op jit(solution)/shard_map/ppermute | solution.py:219
  185.8 20.2 %all-to-all-start.1 = ((bf16[16,16,800]{2,1,0:T(8,128)(2,1)}), bf16[16,16,800]{2,1,0:T(8,128)(2,1)S(1)}, u32[]{:S(2)}, u32[]{:S(2)}) async-start(bf16[16,16,800]{2,1,0:T(8,128)(2,1)} %shard_map.108), calls=%async_computation.1 | async-start | bytes 917504 | tf_op jit(solution)/shard_map/all_to_all | solution.py:791
  (72 other events, 868.8 us)

commit v4 on v3

--- a/solution.py
+++ b/solution.py
@@ -612,8 +612,12 @@
     own_cols, sent_cols = halves(sliced, x)
     merge_first = merge_weight.transpose(0, 2, 1)
     patch, sent_cols = fence(patches[0], sent_cols)
-    came_cols, patch_y, merge_second, out_held = fence(
-        over_x(sent_cols), over_y(patch), next_z(merge_first), out_over_y(vit_out.T)
+    came_cols, patch_y, merge_second, out_held, text_second = fence(
+        over_x(sent_cols),
+        over_y(patch),
+        next_z(merge_first),
+        out_over_y(vit_out.T),
+        next_z(text_embeds),
     )
     own_cols, sent_cols = halves(jnp.stack([own_cols, came_cols], axis=-3), c)
     patch, sent_cols = fence(patch, sent_cols)
@@ -622,8 +626,8 @@
         next_z(sliced), over_x(patch), out_over_far(out_held, z, y)
     )
     patch_xy = over_xy(patch)
-    third, patch_xy, out_held, text_first = fence(
-        next_z(second), patch_xy, out_over_near(out_held), text_embeds
+    third, patch_xy, out_held, text_second = fence(
+        next_z(second), patch_xy, out_over_near(out_held), text_second
     )
     patch_parts = [patch, patch_y, over_c(patch), over_c(patch_y), patch_x, patch_xy]
     patch_parts += [over_c(patch_x), over_c(patch_xy)]
@@ -645,7 +649,7 @@
         normed,
         over_x(out_held),
         over_c(out_held),
-        next_z(text_first),
+        text_second,
         merge_second,
         live,
     )

time: 209 us -> 208 us (level)
  starting transfers between devices: 81.4 us -> 77.8 us
    ppermute x9, starting transfers between devices: 21.4 us -> 25.4 us  [next_z(): return lax.ppermute(value, 'wide', RING_Z)]
    ppermute x2, starting transfers between devices: 8.2 us -> 5.47 us  [send_out_near(): return lax.ppermute(held, 'wide', OUT_NEAR)]
    ppermute x2, waiting for transfers between devices: 7.18 us -> 4.6 us  [send_out_y(): return lax.ppermute(turned, ('wide', 'narrow'), OUT_Y)]
    ppermute x3, starting transfers between devices: 5.07 us -> 2.67 us  [over_xy(): return lax.ppermute(value, ('wide', 'narrow'), both)]
    unnamed x82 -> x90, local copies, waits for them, and re-layouts: 9.02 us -> 10.6 us
  transfers between devices with their start and end apart: 57 -> 57, of which waited for: 20 -> 22; matrix products, arithmetic and copies ran while one was open for 8% -> 8% of each run, Pallas kernels for 20% -> 20%
where the time goes in v4:
time: 208 us; the launch traced here: 207 us
  starting transfers between devices  77.8 us (37%)
  waiting for transfers between devices  58 us (28%)
  Pallas kernels  44.7 us (21%)
  local copies, waits for them, and re-layouts  19 us (9%)
  other arithmetic  6.94 us (3%)
    pallas_call x11, Pallas kernels, run(): pl.pallas_call(kernel, out_shape=shapes, in_specs=specs, out_specs=pl.Blo...  44.7 us
    ppermute x9, starting transfers between devices, next_z(): return lax.ppermute(value, 'wide', RING_Z)  25.4 us
    ppermute x9, waiting for transfers between devices, next_z(): return lax.ppermute(value, 'wide', RING_Z)  12.2 us
    unnamed x90, local copies, waits for them, and re-layouts  10.6 us
    ppermute x6, starting transfers between devices, over_y(): return lax.ppermute(value, 'narrow', CROSS_Y)  10.4 us
    ppermute x2, waiting for transfers between devices, send_out_near(): return lax.ppermute(held, 'wide', OUT_NEAR)  7.08 us
    ppermute x2, starting transfers between devices, send_out_far(): return lax.ppermute(both, ('wide', 'narrow'), OUT_FAR)  6.98 us
    ppermute x3, waiting for transfers between devices, over_xy(): return lax.ppermute(value, ('wide', 'narrow'), both)  6.72 us
  transfers between devices with their start and end apart: 57, of which 22 were waited for; matrix products, arithmetic and copies ran while one was open for 8% of the time, Pallas kernels for 20%

profile of v4, /device:TPU:0, one launch (start us, length us, event | category | flops | bytes accessed | tf_op | source)
XLA Modules:
  0.0 207.1 jit_solution(12254082672820124285)
XLA Ops:
  0.0 3.0 %collective-permute-start.2 = (bf16[4,80,640]{2,1,0:T(8,128)(2,1)}, bf16[4,80,640]{2,1,0:T(8,128)(2,1)S(1)}, u32[]{:S(2)}, u32[]{:S(2)}) collective-permute-start(bf16[4,80,640]{2,1,0:T(8,128)(2,1)} %bitcast.64), channel_id=1, source_target_pairs={{0,8},{2,10},{4,12},{6,14},{8,24},{10,26},{12,28},{14,30},{24,16},... | collective-permute-start | bytes 1228808 | tf_op jit(solution)/shard_map/ppermute | solution.py:230
  11.9 4.6 %collective-permute-done.3 = bf16[80,640]{1,0:T(8,128)(2,1)S(1)} collective-permute-done((bf16[80,640]{1,0:T(8,128)(2,1)}, bf16[80,640]{1,0:T(8,128)(2,1)S(1)}, u32[]{:S(2)}, u32[]{:S(2)}) %collective-permute-start.3) | collective-permute-done | bytes 102432 | tf_op jit(solution)/shard_map/ppermute | solution.py:557
  18.3 3.8 %collective-permute-start.8 = (bf16[2,80,640]{2,1,0:T(8,128)(2,1)S(1)}, bf16[2,80,640]{2,1,0:T(8,128)(2,1)S(1)}, u32[]{:S(2)}, u32[]{:S(2)}) collective-permute-start(bf16[2,80,640]{2,1,0:T(8,128)(2,1)S(1)} %pad_maximum_fusion.5), channel_id=1, source_target_pairs={{0,16},{2,18},{4,20},{6,22},{8,24},{10,26},{12,28},{14,30},{17,1},... | collective-permute-start | bytes 614408 | tf_op jit(solution)/shard_map/ppermute | solution.py:561
  27.5 5.4 %collective-permute-done.7.refs_4_ = bf16[256,640]{1,0:T(8,128)(2,1)S(1)} collective-permute-done((bf16[256,640]{1,0:T(8,128)(2,1)}, bf16[256,640]{1,0:T(8,128)(2,1)S(1)}, u32[]{:S(2)}, u32[]{:S(2)}) %collective-permute-start.7) | collective-permute-done | bytes 327712 | tf_op jit(solution)/shard_map/ppermute | solution.py:215
  34.0 5.8 %collective-permute-start.9 = (bf16[320,512]{1,0:T(8,128)(2,1)S(1)}, bf16[320,512]{1,0:T(8,128)(2,1)S(1)}, u32[]{:S(2)}, u32[]{:S(2)}) collective-permute-start(bf16[320,512]{1,0:T(8,128)(2,1)S(1)} %collective-permute-done.6.second), channel_id=1, source_target_pairs={{0,8},{2,10},{4,12},{6,14},{8,24},{10,26},{12,28},{14,30},{24,16},... | collective-permute-start | bytes 983048 | tf_op jit(solution)/shard_map/ppermute | solution.py:230
  39.8 3.4 %collective-permute-start.11 = (bf16[2,80,640]{2,1,0:T(8,128)(2,1)S(1)}, bf16[2,80,640]{2,1,0:T(8,128)(2,1)S(1)}, u32[]{:S(2)}, u32[]{:S(2)}) collective-permute-start(bf16[2,80,640]{2,1,0:T(8,128)(2,1)S(1)} %broadcast_select_fusion.2), channel_id=1, source_target_pairs={{0,8},{2,10},{4,12},{6,14},{8,0},{10,2},{12,4},{14,6},{16,24},{18,... | collective-permute-start | bytes 614408 | tf_op jit(solution)/shard_map/ppermute | solution.py:565
  44.3 7.1 %collective-permute-done.11 = bf16[2,80,640]{2,1,0:T(8,128)(2,1)S(1)} collective-permute-done((bf16[2,80,640]{2,1,0:T(8,128)(2,1)S(1)}, bf16[2,80,640]{2,1,0:T(8,128)(2,1)S(1)}, u32[]{:S(2)}, u32[]{:S(2)}) %collective-permute-start.11) | collective-permute-done | bytes 204832 | tf_op jit(solution)/shard_map/ppermute | solution.py:565
  58.2 6.3 %shard_map.100 = (bf16[1024,1280]{1,0:T(8,128)(2,1)}, bf16[640,1024]{1,0:T(8,128)(2,1)}) custom-call(s32[4]{0:T(128)} %pad_add_fusion.where, bf16[256,640]{1,0:T(8,128)(2,1)} %bitcast.6.refs_0_, bf16[256,640]{1,0:T(8,128)(2,1)} %collective-permute-done.1.refs_1_, bf16[256,640]{1,0:T(8,128)(2,1)} %copy-done.38, ...), custom_call_target="tpu_custom_call" | custom-call | tf_op jit(solution)/shard_map/pallas_call | solution.py:541
  64.5 2.8 %collective-permute-done.12.fourth = bf16[320,512]{1,0:T(8,128)(2,1)S(1)} collective-permute-done((bf16[320,512]{1,0:T(8,128)(2,1)S(1)}, bf16[320,512]{1,0:T(8,128)(2,1)S(1)}, u32[]{:S(2)}, u32[]{:S(2)}) %collective-permute-start.12) | collective-permute-done | bytes 327712 | tf_op jit(solution)/shard_map/ppermute | solution.py:230
  69.8 3.4 %collective-permute-start.24 = (bf16[160,640]{1,0:T(8,128)(2,1)S(1)}, bf16[160,640]{1,0:T(8,128)(2,1)S(1)}, u32[]{:S(2)}, u32[]{:S(2)}) collective-permute-start(bf16[160,640]{1,0:T(8,128)(2,1)S(1)} %copy-done.40), channel_id=1, source_target_pairs={{0,8},{2,10},{4,12},{6,14},{8,24},{10,26},{12,28},{14,30},{24,16},... | collective-permute-start | bytes 614408 | tf_op jit(solution)/shard_map/ppermute | solution.py:230
  75.0 5.0 %shard_map.101.refs_0_ = bf16[160,1024]{1,0:T(8,128)(2,1)S(1)} custom-call(s32[4]{0:T(128)S(1)} %copy-done.15, bf16[1024,1280]{1,0:T(8,128)(2,1)S(1)} %copy-done.1, bf16[320,512]{1,0:T(8,128)(2,1)S(1)} %bitcast.51, bf16[320,512]{1,0:T(8,128)(2,1)S(1)} %collective-permute-done.6.second, bf16[320,512]{1,0:T(8,128)(2,1)S(1)} %collective-permute-done.9.third, ...), custom_call_target="tpu_custom_call" | custom-call | tf_op jit(solution)/shard_map/pallas_call | solution.py:541
  85.3 3.4 %collective-permute-start.25 = (bf16[160,640]{1,0:T(8,128)(2,1)S(1)}, bf16[160,640]{1,0:T(8,128)(2,1)S(1)}, u32[]{:S(2)}, u32[]{:S(2)}) collective-permute-start(bf16[160,640]{1,0:T(8,128)(2,1)S(1)} %collective-permute-done.24), channel_id=1, source_target_pairs={{0,8},{2,10},{4,12},{6,14},{8,24},{10,26},{12,28},{14,30},{24,16},... | collective-permute-start | bytes 614408 | tf_op jit(solution)/shard_map/ppermute | solution.py:230
  89.6 7.5 %collective-permute-done.25 = bf16[160,640]{1,0:T(8,128)(2,1)S(1)} collective-permute-done((bf16[160,640]{1,0:T(8,128)(2,1)S(1)}, bf16[160,640]{1,0:T(8,128)(2,1)S(1)}, u32[]{:S(2)}, u32[]{:S(2)}) %collective-permute-start.25) | collective-permute-done | bytes 204832 | tf_op jit(solution)/shard_map/ppermute | solution.py:230
  101.6 4.9 %all-to-all-start = ((bf16[16,80,120]{2,1,0:T(8,128)(2,1)}), bf16[16,80,120]{2,1,0:T(8,128)(2,1)}, u32[]{:S(2)}, u32[]{:S(2)}) async-start(bf16[16,80,120]{2,1,0:T(8,128)(2,1)} %shard_map.102), calls=%async_computation | async-start | bytes 655360 | tf_op jit(solution)/shard_map/all_to_all | solution.py:689
  109.5 8.0 %shard_map.103 = (f32[320,128]{1,0:T(8,128)}, f32[320,128]{1,0:T(8,128)}) custom-call(s32[4]{0:T(128)} %pad_add_fusion.where, bf16[160,1024]{1,0:T(8,128)(2,1)} %copy-done.2, bf16[160,1024]{1,0:T(8,128)(2,1)} %copy-done.33, bf16[160,1024]{1,0:T(8,128)(2,1)} %collective-permute-done.27.refs_2_, bf16[160,1024]{1,0:T(8,128)(2,1)} %collective-permute-done.28.refs_3_, ...), custom_call_target="tpu_custom_call" | custom-call | tf_op jit(solution)/shard_map/pallas_call | solution.py:541
  117.5 4.9 %all-to-all-done.own = bf16[16,80,120]{2,1,0:T(8,128)(2,1)} async-done(((bf16[16,80,120]{2,1,0:T(8,128)(2,1)}), bf16[16,80,120]{2,1,0:T(8,128)(2,1)}, u32[]{:S(2)}, u32[]{:S(2)}) %all-to-all-start) | async-done | bytes 307232 | tf_op jit(solution)/shard_map/all_to_all | solution.py:689
  122.9 3.2 %collective-permute-start.38 = (bf16[2,80,640]{2,1,0:T(8,128)(2,1)S(1)}, bf16[2,80,640]{2,1,0:T(8,128)(2,1)S(1)}, u32[]{:S(2)}, u32[]{:S(2)}) collective-permute-start(bf16[2,80,640]{2,1,0:T(8,128)(2,1)S(1)} %pad_maximum_fusion.6), channel_id=1, source_target_pairs={{0,16},{2,18},{4,20},{6,22},{8,24},{10,26},{12,28},{14,30},{17,1},... | collective-permute-start | bytes 614408 | tf_op jit(solution)/shard_map/ppermute | solution.py:561
  138.8 4.5 %collective-permute-start.39 = (bf16[4,320,128]{2,1,0:T(8,128)(2,1)S(1)}, bf16[4,320,128]{2,1,0:T(8,128)(2,1)S(1)}, u32[]{:S(2)}, u32[]{:S(2)}) collective-permute-start(bf16[4,320,128]{2,1,0:T(8,128)(2,1)S(1)} %pad_maximum_fusion.4.refs_0_), channel_id=1, source_target_pairs={{0,1},{1,0},{2,3},{3,2},{4,5},{5,4},{6,7},{7,6},{8,9},{9,8},{10,11... | collective-permute-start | bytes 983048 | tf_op jit(solution)/shard_map/ppermute | solution.py:223
  156.8 4.1 %shard_map.106.refs_11_ = bf16[1280,384]{1,0:T(8,128)(2,1)S(1)} custom-call(s32[4]{0:T(128)S(1)} %copy-done.16, bf16[4,160,640]{2,1,0:T(8,128)(2,1)S(1)} %pad_maximum_fusion.own, bf16[4,160,640]{2,1,0:T(8,128)(2,1)S(1)} %collective-permute-done.32.own_y, bf16[4,160,640]{2,1,0:T(8,128)(2,1)S(1)} %collective-permute-done.33.own_x, ...), custom_call_target="tpu_custom_call" | custom-call | tf_op jit(solution)/shard_map/pallas_call | solution.py:541
  160.9 6.1 %collective-permute-done.41.refs_5_ = bf16[4,320,128]{2,1,0:T(8,128)(2,1)} collective-permute-done((bf16[4,320,128]{2,1,0:T(8,128)(2,1)S(1)}, bf16[4,320,128]{2,1,0:T(8,128)(2,1)}, u32[]{:S(2)}, u32[]{:S(2)}) %collective-permute-start.41) | collective-permute-done | bytes 327712 | tf_op jit(solution)/shard_map/ppermute | solution.py:246
  169.8 5.9 %shard_map.107 = (bf16[1280,128]{1,0:T(8,128)(2,1)S(1)}, bf16[1280,128]{1,0:T(8,128)(2,1)S(1)}, bf16[1280,128]{1,0:T(8,128)(2,1)S(1)}) custom-call(bf16[4,320,128]{2,1,0:T(8,128)(2,1)S(1)} %pad_maximum_fusion.4.refs_0_, bf16[4,320,128]{2,1,0:T(8,128)(2,1)S(1)} %collective-permute-done.39.refs_1_, bf16[4,320,128]{2,1,0:T(8,128)(2,1)S(1)} %collective-permute-done.46.refs_2_, ...), custom_call_target="tpu_custom_call" | custom-call | tf_op jit(solution)/shard_map/pallas_call | solution.py:541
  177.9 6.0 %shard_map.108 = bf16[16,16,800]{2,1,0:T(8,128)(2,1)} custom-call(s32[4]{0:T(128)S(1)} %copy-done.16, bf16[1280,128]{1,0:T(8,128)(2,1)S(1)} %get-tuple-element.128.query, bf16[1280,128]{1,0:T(8,128)(2,1)S(1)} %get-tuple-element.129.own_key, bf16[1280,128]{1,0:T(8,128)(2,1)S(1)} %get-tuple-element.130.own_value, ...), custom_call_target="tpu_custom_call" | custom-call | tf_op jit(solution)/shard_map/pallas_call | solution.py:541
  185.5 5.0 %all-to-all-start.1 = ((bf16[16,16,800]{2,1,0:T(8,128)(2,1)}), bf16[16,16,800]{2,1,0:T(8,128)(2,1)S(1)}, u32[]{:S(2)}, u32[]{:S(2)}) async-start(bf16[16,16,800]{2,1,0:T(8,128)(2,1)} %shard_map.108), calls=%async_computation.1 | async-start | bytes 917504 | tf_op jit(solution)/shard_map/all_to_all | solution.py:795
  198.7 6.1 %all-to-all-done.1.heads = bf16[16,16,800]{2,1,0:T(8,128)(2,1)S(1)} async-done(((bf16[16,16,800]{2,1,0:T(8,128)(2,1)}), bf16[16,16,800]{2,1,0:T(8,128)(2,1)S(1)}, u32[]{:S(2)}, u32[]{:S(2)}) %all-to-all-start.1) | async-done | bytes 409632 | tf_op jit(solution)/shard_map/all_to_all | solution.py:795
  (236 shorter events, 86.2 us)
Async XLA Ops:
  0.0 18.1 %collective-permute-start.2 = (bf16[4,80,640]{2,1,0:T(8,128)(2,1)}, bf16[4,80,640]{2,1,0:T(8,128)(2,1)S(1)}, u32[]{:S(2)}, u32[]{:S(2)}) collective-permute-start(bf16[4,80,640]{2,1,0:T(8,128)(2,1)} %bitcast.64), channel_id=1, source_target_pairs={{0,8},{2,10},{4,12},{6,14},{8,24},{10,26},{12,28},{14,30},{24,16},... | collective-permute-start | bytes 1228808 | tf_op jit(solution)/shard_map/ppermute | solution.py:230
  4.8 13.3 %collective-permute-start.1 = (bf16[256,640]{1,0:T(8,128)(2,1)}, bf16[256,640]{1,0:T(8,128)(2,1)}, u32[]{:S(2)}, u32[]{:S(2)}) collective-permute-start(bf16[256,640]{1,0:T(8,128)(2,1)} %bitcast.6.refs_0_), channel_id=1, source_target_pairs={{0,1},{1,0},{2,3},{3,2},{4,5},{5,4},{6,7},{7,6},{8,9},{9,8},{10,11... | collective-permute-start | bytes 983048 | tf_op jit(solution)/shard_map/ppermute | solution.py:223
  26.2 25.2 %collective-permute-start.10 = (bf16[256,640]{1,0:T(8,128)(2,1)}, bf16[256,640]{1,0:T(8,128)(2,1)S(1)}, u32[]{:S(2)}, u32[]{:S(2)}) collective-permute-start(bf16[256,640]{1,0:T(8,128)(2,1)} %bitcast.6.refs_0_), channel_id=1, source_target_pairs={{0,5},{1,4},{2,7},{3,6},{4,1},{5,0},{6,3},{7,2},{8,13},{9,12},{10,... | collective-permute-start | bytes 983048 | tf_op jit(solution)/shard_map/ppermute | solution.py:246
  34.0 18.2 %collective-permute-start.9 = (bf16[320,512]{1,0:T(8,128)(2,1)S(1)}, bf16[320,512]{1,0:T(8,128)(2,1)S(1)}, u32[]{:S(2)}, u32[]{:S(2)}) collective-permute-start(bf16[320,512]{1,0:T(8,128)(2,1)S(1)} %collective-permute-done.6.second), channel_id=1, source_target_pairs={{0,8},{2,10},{4,12},{6,14},{8,24},{10,26},{12,28},{14,30},{24,16},... | collective-permute-start | bytes 983048 | tf_op jit(solution)/shard_map/ppermute | solution.py:230
  52.2 15.2 %collective-permute-start.17 = (bf16[2,2,80,640]{3,2,1,0:T(8,128)(2,1)S(1)}, bf16[2,2,80,640]{3,2,1,0:T(8,128)(2,1)S(1)}, u32[]{:S(2)}, u32[]{:S(2)}) collective-permute-start(bf16[2,2,80,640]{3,2,1,0:T(8,128)(2,1)S(1)} %pad_maximum_fusion.1.refs_9_), channel_id=1, source_target_pairs={{0,4},{2,6},{4,0},{6,2},{8,12},{10,14},{12,8},{14,10},{16,20},{18,... | collective-permute-start | bytes 1228808 | tf_op jit(solution)/shard_map/ppermute | solution.py:215
  53.7 13.7 %collective-permute-start.18 = (bf16[2,2,80,640]{3,2,1,0:T(8,128)(2,1)S(1)}, bf16[2,2,80,640]{3,2,1,0:T(8,128)(2,1)}, u32[]{:S(2)}, u32[]{:S(2)}) collective-permute-start(bf16[2,2,80,640]{3,2,1,0:T(8,128)(2,1)S(1)} %pad_maximum_fusion.1.refs_9_), channel_id=1, source_target_pairs={{0,2},{2,0},{4,6},{6,4},{8,10},{10,8},{12,14},{14,12},{16,18},{18,... | collective-permute-start | bytes 1228808 | tf_op jit(solution)/shard_map/ppermute | solution.py:219
  67.4 13.3 %collective-permute-start.19 = (bf16[4,80,640]{2,1,0:T(8,128)(2,1)S(1)}, bf16[4,80,640]{2,1,0:T(8,128)(2,1)S(1)}, u32[]{:S(2)}, u32[]{:S(2)}) collective-permute-start(bf16[4,80,640]{2,1,0:T(8,128)(2,1)S(1)} %collective-permute-done.2.refs_14_), channel_id=1, source_target_pairs={{0,8},{2,10},{4,12},{6,14},{8,24},{10,26},{12,28},{14,30},{24,16},... | collective-permute-start | bytes 1228808 | tf_op jit(solution)/shard_map/ppermute | solution.py:230
  68.5 15.2 %collective-permute-start.26 = (bf16[80,640]{1,0:T(8,128)(2,1)S(1)}, bf16[80,640]{1,0:T(8,128)(2,1)S(1)}, u32[]{:S(2)}, u32[]{:S(2)}) collective-permute-start(bf16[80,640]{1,0:T(8,128)(2,1)S(1)} %bitcast.55), channel_id=1, source_target_pairs={{1,0},{3,2},{5,4},{7,6},{9,8},{11,10},{13,12},{15,14},{16,17},{18,... | collective-permute-start | bytes 307208 | tf_op jit(solution)/shard_map/ppermute | solution.py:557
  69.8 15.5 %collective-permute-start.24 = (bf16[160,640]{1,0:T(8,128)(2,1)S(1)}, bf16[160,640]{1,0:T(8,128)(2,1)S(1)}, u32[]{:S(2)}, u32[]{:S(2)}) collective-permute-start(bf16[160,640]{1,0:T(8,128)(2,1)S(1)} %copy-done.40), channel_id=1, source_target_pairs={{0,8},{2,10},{4,12},{6,14},{8,24},{10,26},{12,28},{14,30},{24,16},... | collective-permute-start | bytes 614408 | tf_op jit(solution)/shard_map/ppermute | solution.py:230
  80.7 17.0 %collective-permute-start.23 = (bf16[4,80,640]{2,1,0:T(8,128)(2,1)S(1)}, bf16[4,80,640]{2,1,0:T(8,128)(2,1)S(1)}, u32[]{:S(2)}, u32[]{:S(2)}) collective-permute-start(bf16[4,80,640]{2,1,0:T(8,128)(2,1)S(1)} %collective-permute-done.19.refs_15_), channel_id=1, source_target_pairs={{0,8},{2,10},{4,12},{6,14},{8,24},{10,26},{12,28},{14,30},{24,16},... | collective-permute-start | bytes 1228808 | tf_op jit(solution)/shard_map/ppermute | solution.py:230
  81.8 15.4 %collective-permute-start.20 = (bf16[160,1024]{1,0:T(8,128)(2,1)S(1)}, bf16[160,1024]{1,0:T(8,128)(2,1)S(1)}, u32[]{:S(2)}, u32[]{:S(2)}) collective-permute-start(bf16[160,1024]{1,0:T(8,128)(2,1)S(1)} %shard_map.101.refs_0_), channel_id=1, source_target_pairs={{0,1},{1,0},{2,3},{3,2},{4,5},{5,4},{6,7},{7,6},{8,9},{9,8},{10,11... | collective-permute-start | bytes 983048 | tf_op jit(solution)/shard_map/ppermute | solution.py:223
  83.2 13.9 %collective-permute-start.21 = (bf16[160,1024]{1,0:T(8,128)(2,1)S(1)}, bf16[160,1024]{1,0:T(8,128)(2,1)S(1)}, u32[]{:S(2)}, u32[]{:S(2)}) collective-permute-start(bf16[160,1024]{1,0:T(8,128)(2,1)S(1)} %shard_map.101.refs_0_), channel_id=1, source_target_pairs={{0,4},{2,6},{4,0},{6,2},{8,12},{10,14},{12,8},{14,10},{16,20},{18,... | collective-permute-start | bytes 983048 | tf_op jit(solution)/shard_map/ppermute | solution.py:215
  83.7 14.0 %collective-permute-start.22 = (bf16[160,1024]{1,0:T(8,128)(2,1)S(1)}, bf16[160,1024]{1,0:T(8,128)(2,1)S(1)}, u32[]{:S(2)}, u32[]{:S(2)}) collective-permute-start(bf16[160,1024]{1,0:T(8,128)(2,1)S(1)} %shard_map.101.refs_0_), channel_id=1, source_target_pairs={{0,5},{1,4},{2,7},{3,6},{4,1},{5,0},{6,3},{7,2},{8,13},{9,12},{10,... | collective-permute-start | bytes 983048 | tf_op jit(solution)/shard_map/ppermute | solution.py:246
  98.8 23.6 %collective-permute-start.32 = (bf16[4,160,640]{2,1,0:T(8,128)(2,1)S(1)}, bf16[4,160,640]{2,1,0:T(8,128)(2,1)S(1)}, u32[]{:S(2)}, u32[]{:S(2)}) collective-permute-start(bf16[4,160,640]{2,1,0:T(8,128)(2,1)S(1)} %pad_maximum_fusion.own), channel_id=1, source_target_pairs={{0,1},{1,0},{2,3},{3,2},{4,5},{5,4},{6,7},{7,6},{8,9},{9,8},{10,11... | collective-permute-start | bytes 2457608 | tf_op jit(solution)/shard_map/ppermute | solution.py:223
  100.5 21.9 %collective-permute-start.33 = (bf16[4,160,640]{2,1,0:T(8,128)(2,1)S(1)}, bf16[4,160,640]{2,1,0:T(8,128)(2,1)S(1)}, u32[]{:S(2)}, u32[]{:S(2)}) collective-permute-start(bf16[4,160,640]{2,1,0:T(8,128)(2,1)S(1)} %pad_maximum_fusion.own), channel_id=1, source_target_pairs={{0,4},{2,6},{4,0},{6,2},{8,12},{10,14},{12,8},{14,10},{16,20},{18,... | collective-permute-start | bytes 2457608 | tf_op jit(solution)/shard_map/ppermute | solution.py:215
  101.6 20.8 %all-to-all-start = ((bf16[16,80,120]{2,1,0:T(8,128)(2,1)}), bf16[16,80,120]{2,1,0:T(8,128)(2,1)}, u32[]{:S(2)}, u32[]{:S(2)}) async-start(bf16[16,80,120]{2,1,0:T(8,128)(2,1)} %shard_map.102), calls=%async_computation | async-start | bytes 655360 | tf_op jit(solution)/shard_map/all_to_all | solution.py:689
  137.0 19.6 %collective-permute-start.43 = (bf16[2,160,640]{2,1,0:T(8,128)(2,1)}, bf16[2,160,640]{2,1,0:T(8,128)(2,1)}, u32[]{:S(2)}, u32[]{:S(2)}) collective-permute-start(bf16[2,160,640]{2,1,0:T(8,128)(2,1)} %slice.7), channel_id=1, source_target_pairs={{0,4},{2,6},{4,0},{6,2},{8,12},{10,14},{12,8},{14,10},{16,20},{18,... | collective-permute-start | bytes 1228808 | tf_op jit(solution)/shard_map/ppermute | solution.py:215
  138.8 22.1 %collective-permute-start.39 = (bf16[4,320,128]{2,1,0:T(8,128)(2,1)S(1)}, bf16[4,320,128]{2,1,0:T(8,128)(2,1)S(1)}, u32[]{:S(2)}, u32[]{:S(2)}) collective-permute-start(bf16[4,320,128]{2,1,0:T(8,128)(2,1)S(1)} %pad_maximum_fusion.4.refs_0_), channel_id=1, source_target_pairs={{0,1},{1,0},{2,3},{3,2},{4,5},{5,4},{6,7},{7,6},{8,9},{9,8},{10,11... | collective-permute-start | bytes 983048 | tf_op jit(solution)/shard_map/ppermute | solution.py:223
  143.3 17.6 %collective-permute-start.40 = (bf16[4,320,128]{2,1,0:T(8,128)(2,1)S(1)}, bf16[4,320,128]{2,1,0:T(8,128)(2,1)S(1)}, u32[]{:S(2)}, u32[]{:S(2)}) collective-permute-start(bf16[4,320,128]{2,1,0:T(8,128)(2,1)S(1)} %pad_maximum_fusion.4.refs_0_), channel_id=1, source_target_pairs={{0,4},{2,6},{4,0},{6,2},{8,12},{10,14},{12,8},{14,10},{16,20},{18,... | collective-permute-start | bytes 983048 | tf_op jit(solution)/shard_map/ppermute | solution.py:215
  146.2 20.9 %collective-permute-start.41 = (bf16[4,320,128]{2,1,0:T(8,128)(2,1)S(1)}, bf16[4,320,128]{2,1,0:T(8,128)(2,1)}, u32[]{:S(2)}, u32[]{:S(2)}) collective-permute-start(bf16[4,320,128]{2,1,0:T(8,128)(2,1)S(1)} %pad_maximum_fusion.4.refs_0_), channel_id=1, source_target_pairs={{0,5},{1,4},{2,7},{3,6},{4,1},{5,0},{6,3},{7,2},{8,13},{9,12},{10,... | collective-permute-start | bytes 983048 | tf_op jit(solution)/shard_map/ppermute | solution.py:246
  147.3 13.6 %collective-permute-start.45 = (bf16[2,80,640]{2,1,0:T(8,128)(2,1)}, bf16[2,80,640]{2,1,0:T(8,128)(2,1)}, u32[]{:S(2)}, u32[]{:S(2)}) collective-permute-start(bf16[2,80,640]{2,1,0:T(8,128)(2,1)} %broadcast_select_fusion.1), channel_id=1, source_target_pairs={{0,8},{2,10},{4,12},{6,14},{8,0},{10,2},{12,4},{14,6},{16,24},{18,... | collective-permute-start | bytes 614408 | tf_op jit(solution)/shard_map/ppermute | solution.py:565
  168.6 15.3 %collective-permute-start.52 = (bf16[2,2,80,640]{3,2,1,0:T(8,128)(2,1)S(1)}, bf16[2,2,80,640]{3,2,1,0:T(8,128)(2,1)S(1)}, u32[]{:S(2)}, u32[]{:S(2)}) collective-permute-start(bf16[2,2,80,640]{3,2,1,0:T(8,128)(2,1)S(1)} %pad_maximum_fusion.2.own), channel_id=1, source_target_pairs={{0,4},{2,6},{4,0},{6,2},{8,12},{10,14},{12,8},{14,10},{16,20},{18,... | collective-permute-start | bytes 1228808 | tf_op jit(solution)/shard_map/ppermute | solution.py:215
  169.0 15.8 %collective-permute-start.53 = (bf16[2,2,80,640]{3,2,1,0:T(8,128)(2,1)S(1)}, bf16[2,2,80,640]{3,2,1,0:T(8,128)(2,1)S(1)}, u32[]{:S(2)}, u32[]{:S(2)}) collective-permute-start(bf16[2,2,80,640]{3,2,1,0:T(8,128)(2,1)S(1)} %pad_maximum_fusion.2.own), channel_id=1, source_target_pairs={{0,2},{2,0},{4,6},{6,4},{8,10},{10,8},{12,14},{14,12},{16,18},{18,... | collective-permute-start | bytes 1228808 | tf_op jit(solution)/shard_map/ppermute | solution.py:219
  185.5 19.3 %all-to-all-start.1 = ((bf16[16,16,800]{2,1,0:T(8,128)(2,1)}), bf16[16,16,800]{2,1,0:T(8,128)(2,1)S(1)}, u32[]{:S(2)}, u32[]{:S(2)}) async-start(bf16[16,16,800]{2,1,0:T(8,128)(2,1)} %shard_map.108), calls=%async_computation.1 | async-start | bytes 917504 | tf_op jit(solution)/shard_map/all_to_all | solution.py:795
  (76 other events, 886.1 us)
